TPU v7x, 512 devices: a whole 4x8x8 slice. The times are simulated.
512 devices in a mesh: gx: 16 (over z_lo, x), gy: 32 (over z_hi, y, core).
Axes of the slice: x: 4, y: 8, z: 8 (z_hi: 2, z_lo: 4; z = z_hi * 4 + z_lo), core: 2. Of those that a mesh axis runs over, the one named last changes fastest.
Arguments:
- momentum_distribution: float32 [19, 8, 64, 4096], P(None, None, 'gx', 'gy'), may hold values from 0.02 to 0.05
- energy_distribution: float32 [7, 8, 64, 4096], P(None, None, 'gx', 'gy'), may hold values from 0.05 to 0.2
- metal_warmness: float32 [8, 32, 4096], P(None, 'gx', 'gy'), may hold values from 0.5 to 1.5
- metal_indicator: int32 [8, 32, 4096], P(None, 'gx', 'gy'), may hold values 0 or 1
- interface_holder: int32 [16, 4096, 1], P('gx', 'gy'), may hold values from 0 to 31; in each aligned block of 128 rows (0 to 127, 128 to 255, ..., all dimensions but the last counted through in order) at most 8 rows name the same one
- brick_tallies: int32 [16, 32], P('gx', 'gy'), may hold values from 96 to 128, as said below
- boundary_brick_index: int32 [16, 4096], P('gx', 'gy'), may hold values from 0 to 511, as said below
- metal_face_index: int32 [16, 4096], P('gx', 'gy'), may hold values from 0 to 255
Outputs:
- flow_out: float32 [19, 8, 64, 4096], P(None, None, 'gx', 'gy')
- heat_out: float32 [7, 8, 64, 4096], P(None, None, 'gx', 'gy')
- solid_out: float32 [8, 32, 4096], P(None, 'gx', 'gy')
Inputs may be any that keep to these rules, and one draw needn't show every extreme that they name: `interface_holder`: within the 128 rows of one brick, live or not, at most 8 name one owner; some brick reaches 8. `brick_tallies`: some brick has all 128 rows live. `boundary_brick_index`: the 128 entries of one brick are distinct.
All inputs are finite; a program needn't handle non-finite values. No bound on the sum of `metal_indicator` on one device may be relied on, other than what follows from the above.
Results may differ from a plain program's by a relative error of at most 0.0001.
Values sent between devices are 32-bit elements; how exact they have to be, the bound alone decides.
A program may use at most 64 MiB of HBM per device.

v0:
```python
import jax
import jax.numpy as jnp
from jax import lax
from jax.sharding import PartitionSpec as P

STEPS = 3


VELOCITY = [
    (0, 0, 0),
    (1, 0, 0),
    (-1, 0, 0),
    (0, 1, 0),
    (0, -1, 0),
    (0, 0, 1),
    (0, 0, -1),
    (1, 1, 0),
    (-1, -1, 0),
    (1, -1, 0),
    (-1, 1, 0),
    (1, 0, 1),
    (-1, 0, -1),
    (1, 0, -1),
    (-1, 0, 1),
    (0, 1, 1),
    (0, -1, -1),
    (0, 1, -1),
    (0, -1, 1),
]
WEIGHT_FLOW = [1.0 / 3.0] + [1.0 / 18.0] * 6 + [1.0 / 36.0] * 12
WARMTH_LATTICE_W = [0.25] + [0.125] * 6
ALL_VEL = VELOCITY + VELOCITY[:7]
relax_flow = 0.8
relax_heat = 0.7
solid_dt = 0.04
film_coef = 1.0


def extended_2(block, sides, width, periodic):
    for axis, dim in sides:
        count = lax.axis_size(axis)
        forward = [(i, i + 1) for i in range(count - 1)]
        if periodic:
            forward.append((count - 1, 0))
        backward = [(target, source) for source, target in forward]
        low = lax.ppermute(
            lax.slice_in_dim(block, block.shape[dim] - width, None, axis=dim), axis, forward
        )
        high = lax.ppermute(lax.slice_in_dim(block, 0, width, axis=dim), axis, backward)
        block = jnp.concatenate([low, block, high], axis=dim)
    return block


def opposite_of(main_launcher):
    local = main_launcher if main_launcher < 19 else main_launcher - 19
    vector = VELOCITY[local]
    target = VELOCITY.index((-vector[0], -vector[1], -vector[2]))
    return target if main_launcher < 19 else target + 19


def directed(states, axis):
    total = jnp.zeros_like(states[0])
    for main_launcher in range(states.shape[0]):
        if VELOCITY[main_launcher][axis] == 1:
            total = total + states[main_launcher]
        elif VELOCITY[main_launcher][axis] == -1:
            total = total - states[main_launcher]
    return total


def bgk_scattering(momentum_distribution, energy_distribution):
    density = jnp.sum(momentum_distribution, 0)
    velo_x = directed(momentum_distribution, 0) / density
    velo_y = directed(momentum_distribution, 1) / density
    velo_z = directed(momentum_distribution, 2) / density
    speed_sq = velo_x * velo_x + velo_y * velo_y + velo_z * velo_z
    momentum_after_bump = []
    for main_launcher in range(19):
        vector = VELOCITY[main_launcher]
        lattice_heading = vector[0] * velo_x + vector[1] * velo_y + vector[2] * velo_z
        maxwellian_balance = (
            WEIGHT_FLOW[main_launcher]
            * density
            * (
                1.0
                + 3.0 * lattice_heading
                + 4.5 * lattice_heading * lattice_heading
                - 1.5 * speed_sq
            )
        )
        momentum_after_bump.append(
            momentum_distribution[main_launcher]
            - (momentum_distribution[main_launcher] - maxwellian_balance) / relax_flow
        )
    site_warmness = jnp.sum(energy_distribution, 0)
    energy_after_bump = []
    for main_launcher in range(7):
        vector = VELOCITY[main_launcher]
        lattice_heading = vector[0] * velo_x + vector[1] * velo_y + vector[2] * velo_z
        maxwellian_balance = (
            WARMTH_LATTICE_W[main_launcher] * site_warmness * (1.0 + 4.0 * lattice_heading)
        )
        energy_after_bump.append(
            energy_distribution[main_launcher]
            - (energy_distribution[main_launcher] - maxwellian_balance) / relax_heat
        )
    return (jnp.stack(momentum_after_bump), jnp.stack(energy_after_bump), site_warmness)


def propagate_bounce(displaced_field, piled_arrays, interface_warmness, coated_mask_value):
    strata_count = piled_arrays.shape[1]
    result = []
    for main_launcher in range(26):
        lift = ALL_VEL[main_launcher][2]
        if lift == 0:
            result.append(displaced_field[main_launcher])
        elif lift == 1:
            lowest_plane = piled_arrays[opposite_of(main_launcher), 0]
            if main_launcher == 24:
                lowest_plane = jnp.where(
                    coated_mask_value > 0.5, 0.25 * interface_warmness - lowest_plane, lowest_plane
                )
            result.append(
                jnp.concatenate(
                    [lowest_plane[None], displaced_field[main_launcher][: strata_count - 1]], 0
                )
            )
        else:
            upper = piled_arrays[opposite_of(main_launcher), strata_count - 1]
            result.append(jnp.concatenate([displaced_field[main_launcher][1:], upper[None]], 0))
    joined = jnp.stack(result)
    return (joined[:19], joined[19:])


def spread_warmth(field_pad, cond_pad):
    size_z = field_pad.shape[0] - 2
    size_x = field_pad.shape[1] - 2
    size_y = field_pad.shape[2] - 2
    centre_field = field_pad[1 : 1 + size_z, 1 : 1 + size_x, 1 : 1 + size_y]
    centre_cond = cond_pad[1 : 1 + size_z, 1 : 1 + size_x, 1 : 1 + size_y]
    total = jnp.zeros_like(centre_field)
    for shift_vec in [(1, 0, 0), (-1, 0, 0), (0, 1, 0), (0, -1, 0), (0, 0, 1), (0, 0, -1)]:
        near_field = field_pad[
            1 + shift_vec[0] : 1 + shift_vec[0] + size_z,
            1 + shift_vec[1] : 1 + shift_vec[1] + size_x,
            1 + shift_vec[2] : 1 + shift_vec[2] + size_y,
        ]
        near_cond = cond_pad[
            1 + shift_vec[0] : 1 + shift_vec[0] + size_z,
            1 + shift_vec[1] : 1 + shift_vec[1] + size_x,
            1 + shift_vec[2] : 1 + shift_vec[2] + size_y,
        ]
        face = 2.0 * centre_cond * near_cond / (centre_cond + near_cond)
        total = total + face * (near_field - centre_field)
    return total


def march_forward(field, increment_amount, forcing_term):
    strata_count = field.shape[0]
    placed = jnp.concatenate(
        [jnp.zeros((strata_count - 1,) + forcing_term.shape, field.dtype), forcing_term[None]], 0
    )
    return field + solid_dt * (increment_amount + placed)


def extend_joint(piled_arrays):
    return extended_2(piled_arrays, (("gx", 2), ("gy", 3)), 1, True)


def bridge_fluid_metal(
    metal_warmness,
    nominal_diffusivity,
    site_warmness,
    interface_mapping,
    contact_surface,
    cell_groups,
):
    strata_count = metal_warmness.shape[0]
    outgoing_links = jnp.dot(
        interface_mapping, site_warmness[0].reshape(-1), precision=lax.Precision.HIGHEST
    ).reshape(cell_groups, -1)
    arrived = lax.all_to_all(outgoing_links, "gy", split_axis=0, concat_axis=0, tiled=True).reshape(
        -1
    )
    current_boundary = metal_warmness[strata_count - 1].reshape(-1)
    gain = film_coef * (
        arrived - jnp.dot(contact_surface, current_boundary, precision=lax.Precision.HIGHEST)
    )
    forcing_term = jnp.dot(gain, contact_surface, precision=lax.Precision.HIGHEST).reshape(
        metal_warmness.shape[1], metal_warmness.shape[2]
    )
    fourier_diffusion_step = nominal_diffusivity * (1.0 + 0.5 * metal_warmness)
    margin_extended = extended_2(
        jnp.stack([metal_warmness, fourier_diffusion_step]), (("gx", 2), ("gy", 3)), 1, False
    )
    margin_extended = jnp.pad(margin_extended, ((0, 0), (1, 1), (0, 0), (0, 0)))
    refreshed_state = march_forward(
        metal_warmness, spread_warmth(margin_extended[0], margin_extended[1]), forcing_term
    )
    reply = jnp.dot(
        contact_surface,
        refreshed_state[strata_count - 1].reshape(-1),
        precision=lax.Precision.HIGHEST,
    ).reshape(cell_groups, -1)
    bounced_back = lax.all_to_all(reply, "gy", split_axis=0, concat_axis=0, tiled=True).reshape(-1)
    interface_warmness = jnp.dot(
        bounced_back, interface_mapping, precision=lax.Precision.HIGHEST
    ).reshape(site_warmness.shape[1], site_warmness.shape[2])
    return (refreshed_state, interface_warmness)


def on_device(
    momentum_distribution,
    energy_distribution,
    metal_warmness,
    metal_indicator,
    interface_holder,
    brick_tallies,
    boundary_brick_index,
    metal_face_index,
):
    width_x = momentum_distribution.shape[2]
    width_y = momentum_distribution.shape[3]
    boundary_sites = metal_warmness.shape[1] * metal_warmness.shape[2]
    row_total = boundary_brick_index.shape[1]
    cell_groups = lax.axis_size("gy")
    capacity = max(2, 2 * row_total // cell_groups)
    owners = interface_holder[0, :, 0]
    active_flag = jnp.arange(row_total, dtype=jnp.int32) < brick_tallies[0, 0]
    hit_owner = (owners[:, None] == jnp.arange(cell_groups, dtype=jnp.int32)[None, :]).astype(
        jnp.int32
    )
    earlier = jnp.cumsum(hit_owner, 0) - hit_owner
    ranking = jnp.sum(earlier * hit_owner, 1)
    placed = owners * capacity + ranking
    chooser = (
        placed[:, None] == jnp.arange(cell_groups * capacity, dtype=jnp.int32)[None, :]
    ) & active_flag[:, None]
    wall_hit = (
        boundary_brick_index[0][:, None] == jnp.arange(width_x * width_y, dtype=jnp.int32)[None, :]
    ).astype(jnp.float32)
    interface_mapping = jnp.dot(
        chooser.astype(jnp.float32).T, wall_hit, precision=lax.Precision.HIGHEST
    )
    coated_mask_value = jnp.sum(interface_mapping, 0).reshape(width_x, width_y)
    slot_sent = jnp.sum(chooser.astype(jnp.int32) * (metal_face_index[0] + 1)[:, None], 0) - 1
    slot_recv = lax.all_to_all(
        slot_sent.reshape(cell_groups, capacity), "gy", split_axis=0, concat_axis=0, tiled=True
    ).reshape(-1)
    contact_surface = (
        slot_recv[:, None] == jnp.arange(boundary_sites, dtype=jnp.int32)[None, :]
    ).astype(jnp.float32)
    nominal_diffusivity = 0.2 + 0.8 * metal_indicator.astype(jnp.float32)
    for _ in range(STEPS):
        momentum_after_bump, energy_after_bump, site_warmness = bgk_scattering(
            momentum_distribution, energy_distribution
        )
        piled_arrays = jnp.concatenate([momentum_after_bump, energy_after_bump], 0)
        metal_warmness, interface_warmness = bridge_fluid_metal(
            metal_warmness,
            nominal_diffusivity,
            site_warmness,
            interface_mapping,
            contact_surface,
            cell_groups,
        )
        extended = extend_joint(piled_arrays)
        displaced_field = jnp.stack(
            [
                extended[
                    main_launcher,
                    :,
                    1 - ALL_VEL[main_launcher][0] : 1 - ALL_VEL[main_launcher][0] + width_x,
                    1 - ALL_VEL[main_launcher][1] : 1 - ALL_VEL[main_launcher][1] + width_y,
                ]
                for main_launcher in range(26)
            ]
        )
        momentum_distribution, energy_distribution = propagate_bounce(
            displaced_field, piled_arrays, interface_warmness, coated_mask_value
        )
    return (momentum_distribution, energy_distribution, metal_warmness)


def solution(mesh):
    placed = (
        P(None, None, "gx", "gy"),
        P(None, None, "gx", "gy"),
        P(None, "gx", "gy"),
        P(None, "gx", "gy"),
        P("gx", "gy", None),
        P("gx", "gy"),
        P("gx", "gy"),
        P("gx", "gy"),
    )
    return jax.shard_map(
        on_device,
        mesh=mesh,
        in_specs=placed,
        out_specs=(P(None, None, "gx", "gy"), P(None, None, "gx", "gy"), P(None, "gx", "gy")),
        check_vma=False,
    )
```

profile of v0, /device:TPU:63, one launch (start us, length us, event | category | flops | bytes accessed | tf_op | source)
XLA Modules:
  0.0 333.3 jit_solution(11597441714428964530)
XLA Ops:
  11.3 15.8 %all-to-all-start = ((s32[32,1,8]{2,1,0:T(1,128)}), s32[32,1,8]{2,1,0:T(1,128)S(1)}, u32[]{:S(2)}, u32[]{:S(2)}) async-start(s32[32,1,8]{2,1,0:T(1,128)} %bitcast.50), calls=%async_computation | async-start | bytes 32768 | tf_op jit(solution)/shard_map/all_to_all | solution.py:247
  30.3 5.1 %collective-permute-start = (f32[26,8,1,128]{3,2,1,0:T(1,128)S(1)}, f32[26,8,1,128]{3,2,1,0:T(1,128)S(1)}, u32[]{:S(2)}, u32[]{:S(2)}) collective-permute-start(f32[26,8,1,128]{3,2,1,0:T(1,128)S(1)} %get-tuple-element.258), channel_id=1, source_target_pairs={{0,32},{32,64},{64,96},{96,128},{128,160},{160,192},{192,224},{224... | collective-permute-start | bytes 319496 | tf_op jit(solution)/shard_map/ppermute | solution.py:46
  39.1 4.2 %convolution_bitcast_fusion.3 = f32[32,1,8]{2,1,0:T(1,128)} fusion(f32[512,1,1]{0,1,2:T(1,128)S(1)} %bitcast.960, f32[256,512]{1,0:T(8,128)S(1)} %get-tuple-element.347), kind=kOutput, calls=%fused_computation.3 | convolution fusion | flops 1572864 | bytes 527360 | tf_op jit(solution)/shard_map/dot_general | solution.py:179
  47.5 12.5 %all-to-all-start.1 = ((f32[32,1,8]{2,1,0:T(1,128)}), f32[32,1,8]{2,1,0:T(1,128)S(1)}, u32[]{:S(2)}, u32[]{:S(2)}) async-start(f32[32,1,8]{2,1,0:T(1,128)} %convolution_bitcast_fusion.3), calls=%async_computation.1 | async-start | bytes 32768 | tf_op jit(solution)/shard_map/all_to_all | solution.py:182
  62.3 7.2 %all-to-all-done.1 = f32[32,1,8]{2,1,0:T(1,128)S(1)} async-done(((f32[32,1,8]{2,1,0:T(1,128)}), f32[32,1,8]{2,1,0:T(1,128)S(1)}, u32[]{:S(2)}, u32[]{:S(2)}) %all-to-all-start.1) | async-done | bytes 1056 | tf_op jit(solution)/shard_map/all_to_all | solution.py:182
  70.9 4.9 %collective-permute-start.6 = (f32[2,8,4,1]{3,1,2,0:T(8,128)S(1)}, f32[2,8,4,1]{3,1,2,0:T(8,128)S(1)}, u32[]{:S(2)}, u32[]{:S(2)}) collective-permute-start(f32[2,8,4,1]{3,1,2,0:T(8,128)S(1)} %get-tuple-element.279), channel_id=1, source_target_pairs={{0,1},{1,2},{2,3},{3,4},{4,5},{5,6},{6,7},{7,8},{8,9},{9,10},{10,1... | collective-permute-start | bytes 776 | tf_op jit(solution)/shard_map/ppermute | solution.py:46
  77.9 9.4 %collective-permute-done.7 = f32[2,8,4,1]{3,1,2,0:T(8,128)S(1)} collective-permute-done((f32[2,8,4,1]{3,1,2,0:T(8,128)S(1)}, f32[2,8,4,1]{3,1,2,0:T(8,128)S(1)}, u32[]{:S(2)}, u32[]{:S(2)}) %collective-permute-start.7) | collective-permute-done | bytes 288 | tf_op jit(solution)/shard_map/ppermute | solution.py:49
  89.3 4.4 %all-to-all-start.2 = ((f32[32,1,8]{2,1,0:T(1,128)}), f32[32,1,8]{2,1,0:T(1,128)S(1)}, u32[]{:S(2)}, u32[]{:S(2)}) async-start(f32[32,1,8]{2,1,0:T(1,128)} %bitcast.70), calls=%async_computation.2 | async-start | bytes 32768 | tf_op jit(solution)/shard_map/all_to_all | solution.py:205
  93.8 5.4 %collective-permute-start.12 = (f32[2,8,1,128]{3,1,2,0:T(8,128)S(1)}, f32[2,8,1,128]{3,1,2,0:T(8,128)S(1)}, u32[]{:S(2)}, u32[]{:S(2)}) collective-permute-start(f32[2,8,1,128]{3,1,2,0:T(8,128)S(1)} %get-tuple-element.291), channel_id=1, source_target_pairs={{0,32},{32,64},{64,96},{96,128},{128,160},{160,192},{192,224},{224... | collective-permute-start | bytes 24584 | tf_op jit(solution)/shard_map/ppermute | solution.py:46
  105.8 8.7 %collective-permute-start.14 = (f32[2,8,4,1]{3,1,2,0:T(8,128)S(1)}, f32[2,8,4,1]{3,1,2,0:T(8,128)S(1)}, u32[]{:S(2)}, u32[]{:S(2)}) collective-permute-start(f32[2,8,4,1]{3,1,2,0:T(8,128)S(1)} %get-tuple-element.275), channel_id=1, source_target_pairs={{0,1},{1,2},{2,3},{3,4},{4,5},{5,6},{6,7},{7,8},{8,9},{9,10},{10,1... | collective-permute-start | bytes 776 | tf_op jit(solution)/shard_map/ppermute | solution.py:46
  116.5 9.6 %collective-permute-done.15 = f32[2,8,4,1]{3,1,2,0:T(8,128)S(1)} collective-permute-done((f32[2,8,4,1]{3,1,2,0:T(8,128)S(1)}, f32[2,8,4,1]{3,1,2,0:T(8,128)S(1)}, u32[]{:S(2)}, u32[]{:S(2)}) %collective-permute-start.15) | collective-permute-done | bytes 288 | tf_op jit(solution)/shard_map/ppermute | solution.py:49
  131.0 9.7 %collective-permute-start.2 = (f32[26,8,6,1]{0,1,3,2:T(8,128)}, f32[26,8,6,1]{0,1,3,2:T(8,128)S(1)}, u32[]{:S(2)}, u32[]{:S(2)}) collective-permute-start(f32[26,8,6,1]{0,1,3,2:T(8,128)} %copy.252), channel_id=1, source_target_pairs={{0,1},{1,2},{2,3},{3,4},{4,5},{5,6},{6,7},{7,8},{8,9},{9,10},{10,1... | collective-permute-start | bytes 14984 | tf_op jit(solution)/shard_map/ppermute | solution.py:46
  144.3 4.2 %convolution_bitcast_fusion.2 = f32[32,1,8]{2,1,0:T(1,128)} fusion(f32[512,1,1]{0,1,2:T(1,128)S(1)} %bitcast.1022, f32[256,512]{1,0:T(8,128)S(1)} %get-tuple-element.347), kind=kOutput, calls=%fused_computation.2 | convolution fusion | flops 1572864 | bytes 527360 | tf_op jit(solution)/shard_map/dot_general | solution.py:179
  148.5 10.7 %all-to-all-start.3 = ((f32[32,1,8]{2,1,0:T(1,128)}), f32[32,1,8]{2,1,0:T(1,128)}, u32[]{:S(2)}, u32[]{:S(2)}) async-start(f32[32,1,8]{2,1,0:T(1,128)} %convolution_bitcast_fusion.2), calls=%async_computation.3 | async-start | bytes 32768 | tf_op jit(solution)/shard_map/all_to_all | solution.py:182
  181.2 12.8 %all-to-all-start.4 = ((f32[32,1,8]{2,1,0:T(1,128)}), f32[32,1,8]{2,1,0:T(1,128)S(1)}, u32[]{:S(2)}, u32[]{:S(2)}) async-start(f32[32,1,8]{2,1,0:T(1,128)} %bitcast.143), calls=%async_computation.4 | async-start | bytes 32768 | tf_op jit(solution)/shard_map/all_to_all | solution.py:205
  204.7 8.3 %collective-permute-start.22 = (f32[2,8,4,1]{3,1,2,0:T(8,128)S(1)}, f32[2,8,4,1]{3,1,2,0:T(8,128)S(1)}, u32[]{:S(2)}, u32[]{:S(2)}) collective-permute-start(f32[2,8,4,1]{3,1,2,0:T(8,128)S(1)} %get-tuple-element.271), channel_id=1, source_target_pairs={{0,1},{1,2},{2,3},{3,4},{4,5},{5,6},{6,7},{7,8},{8,9},{9,10},{10,1... | collective-permute-start | bytes 776 | tf_op jit(solution)/shard_map/ppermute | solution.py:46
  216.2 8.4 %collective-permute-done.23 = f32[2,8,4,1]{3,1,2,0:T(8,128)S(1)} collective-permute-done((f32[2,8,4,1]{3,1,2,0:T(8,128)S(1)}, f32[2,8,4,1]{3,1,2,0:T(8,128)S(1)}, u32[]{:S(2)}, u32[]{:S(2)}) %collective-permute-start.23) | collective-permute-done | bytes 288 | tf_op jit(solution)/shard_map/ppermute | solution.py:49
  228.9 9.7 %collective-permute-start.10 = (f32[26,8,6,1]{0,1,3,2:T(8,128)S(1)}, f32[26,8,6,1]{0,1,3,2:T(8,128)S(1)}, u32[]{:S(2)}, u32[]{:S(2)}) collective-permute-start(f32[26,8,6,1]{0,1,3,2:T(8,128)S(1)} %copy.264), channel_id=1, source_target_pairs={{0,1},{1,2},{2,3},{3,4},{4,5},{5,6},{6,7},{7,8},{8,9},{9,10},{10,1... | collective-permute-start | bytes 14984 | tf_op jit(solution)/shard_map/ppermute | solution.py:46
  246.2 10.6 %all-to-all-start.5 = ((f32[32,1,8]{2,1,0:T(1,128)}), f32[32,1,8]{2,1,0:T(1,128)}, u32[]{:S(2)}, u32[]{:S(2)}) async-start(f32[32,1,8]{2,1,0:T(1,128)} %convolution_bitcast_fusion.1), calls=%async_computation.5 | async-start | bytes 32768 | tf_op jit(solution)/shard_map/all_to_all | solution.py:182
  272.9 5.8 %collective-permute-start.16 = (f32[26,8,1,128]{3,2,1,0:T(1,128)S(1)}, f32[26,8,1,128]{3,2,1,0:T(1,128)S(1)}, u32[]{:S(2)}, u32[]{:S(2)}) collective-permute-start(f32[26,8,1,128]{3,2,1,0:T(1,128)S(1)} %get-tuple-element.253), channel_id=1, source_target_pairs={{0,32},{32,64},{64,96},{96,128},{128,160},{160,192},{192,224},{224... | collective-permute-start | bytes 319496 | tf_op jit(solution)/shard_map/ppermute | solution.py:46
  282.9 12.8 %all-to-all-start.6 = ((f32[32,1,8]{2,1,0:T(1,128)}), f32[32,1,8]{2,1,0:T(1,128)S(1)}, u32[]{:S(2)}, u32[]{:S(2)}) async-start(f32[32,1,8]{2,1,0:T(1,128)} %convolution_bitcast_fusion), calls=%async_computation.6 | async-start | bytes 32768 | tf_op jit(solution)/shard_map/all_to_all | solution.py:205
  296.3 8.9 %all-to-all-done.6 = f32[32,1,8]{2,1,0:T(1,128)S(1)} async-done(((f32[32,1,8]{2,1,0:T(1,128)}), f32[32,1,8]{2,1,0:T(1,128)S(1)}, u32[]{:S(2)}, u32[]{:S(2)}) %all-to-all-start.6) | async-done | bytes 1056 | tf_op jit(solution)/shard_map/all_to_all | solution.py:205
  309.8 5.0 %collective-permute-start.18 = (f32[26,8,6,1]{0,1,3,2:T(8,128)S(1)}, f32[26,8,6,1]{0,1,3,2:T(8,128)S(1)}, u32[]{:S(2)}, u32[]{:S(2)}) collective-permute-start(f32[26,8,6,1]{0,1,3,2:T(8,128)S(1)} %copy.277), channel_id=1, source_target_pairs={{0,1},{1,2},{2,3},{3,4},{4,5},{5,6},{6,7},{7,8},{8,9},{9,10},{10,1... | collective-permute-start | bytes 14984 | tf_op jit(solution)/shard_map/ppermute | solution.py:46
  317.0 9.2 %collective-permute-done.19 = f32[26,8,6,1]{0,1,3,2:T(8,128)S(1)} collective-permute-done((f32[26,8,6,1]{0,1,3,2:T(8,128)S(1)}, f32[26,8,6,1]{0,1,3,2:T(8,128)S(1)}, u32[]{:S(2)}, u32[]{:S(2)}) %collective-permute-start.19) | collective-permute-done | bytes 5024 | tf_op jit(solution)/shard_map/ppermute | solution.py:49
  (576 shorter events, 126.4 us)
Async XLA Ops:
  1.4 69.4 %collective-permute-start.4 = (f32[2,8,1,128]{3,1,2,0:T(8,128)S(1)}, f32[2,8,1,128]{3,1,2,0:T(8,128)S(1)}, u32[]{:S(2)}, u32[]{:S(2)}) collective-permute-start(f32[2,8,1,128]{3,1,2,0:T(8,128)S(1)} %get-tuple-element.318), channel_id=1, source_target_pairs={{0,32},{32,64},{64,96},{96,128},{128,160},{160,192},{192,224},{224... | collective-permute-start | bytes 24584 | tf_op jit(solution)/shard_map/ppermute | solution.py:46
  5.3 65.5 %collective-permute-start.5 = (f32[2,8,1,128]{3,1,2,0:T(8,128)S(1)}, f32[2,8,1,128]{3,1,2,0:T(8,128)S(1)}, u32[]{:S(2)}, u32[]{:S(2)}) collective-permute-start(f32[2,8,1,128]{3,1,2,0:T(8,128)S(1)} %get-tuple-element.319), channel_id=1, source_target_pairs={{32,0},{64,32},{96,64},{128,96},{160,128},{192,160},{224,192},{256... | collective-permute-start | bytes 24584 | tf_op jit(solution)/shard_map/ppermute | solution.py:49
  11.3 36.3 %all-to-all-start = ((s32[32,1,8]{2,1,0:T(1,128)}), s32[32,1,8]{2,1,0:T(1,128)S(1)}, u32[]{:S(2)}, u32[]{:S(2)}) async-start(s32[32,1,8]{2,1,0:T(1,128)} %bitcast.50), calls=%async_computation | async-start | bytes 32768 | tf_op jit(solution)/shard_map/all_to_all | solution.py:247
  30.3 96.6 %collective-permute-start = (f32[26,8,1,128]{3,2,1,0:T(1,128)S(1)}, f32[26,8,1,128]{3,2,1,0:T(1,128)S(1)}, u32[]{:S(2)}, u32[]{:S(2)}) collective-permute-start(f32[26,8,1,128]{3,2,1,0:T(1,128)S(1)} %get-tuple-element.258), channel_id=1, source_target_pairs={{0,32},{32,64},{64,96},{96,128},{128,160},{160,192},{192,224},{224... | collective-permute-start | bytes 319496 | tf_op jit(solution)/shard_map/ppermute | solution.py:46
  35.4 91.4 %collective-permute-start.1 = (f32[26,8,1,128]{3,2,1,0:T(1,128)S(1)}, f32[26,8,1,128]{3,2,1,0:T(1,128)S(1)}, u32[]{:S(2)}, u32[]{:S(2)}) collective-permute-start(f32[26,8,1,128]{3,2,1,0:T(1,128)S(1)} %get-tuple-element.259), channel_id=1, source_target_pairs={{32,0},{64,32},{96,64},{128,96},{160,128},{192,160},{224,192},{256... | collective-permute-start | bytes 319496 | tf_op jit(solution)/shard_map/ppermute | solution.py:49
  47.5 21.9 %all-to-all-start.1 = ((f32[32,1,8]{2,1,0:T(1,128)}), f32[32,1,8]{2,1,0:T(1,128)S(1)}, u32[]{:S(2)}, u32[]{:S(2)}) async-start(f32[32,1,8]{2,1,0:T(1,128)} %convolution_bitcast_fusion.3), calls=%async_computation.1 | async-start | bytes 32768 | tf_op jit(solution)/shard_map/all_to_all | solution.py:182
  75.8 11.6 %collective-permute-start.7 = (f32[2,8,4,1]{3,1,2,0:T(8,128)S(1)}, f32[2,8,4,1]{3,1,2,0:T(8,128)S(1)}, u32[]{:S(2)}, u32[]{:S(2)}) collective-permute-start(f32[2,8,4,1]{3,1,2,0:T(8,128)S(1)} %get-tuple-element.280), channel_id=1, source_target_pairs={{1,0},{2,1},{3,2},{4,3},{5,4},{6,5},{7,6},{8,7},{9,8},{10,9},{11,1... | collective-permute-start | bytes 776 | tf_op jit(solution)/shard_map/ppermute | solution.py:49
  89.3 13.9 %all-to-all-start.2 = ((f32[32,1,8]{2,1,0:T(1,128)}), f32[32,1,8]{2,1,0:T(1,128)S(1)}, u32[]{:S(2)}, u32[]{:S(2)}) async-start(f32[32,1,8]{2,1,0:T(1,128)} %bitcast.70), calls=%async_computation.2 | async-start | bytes 32768 | tf_op jit(solution)/shard_map/all_to_all | solution.py:205
  93.8 11.1 %collective-permute-start.12 = (f32[2,8,1,128]{3,1,2,0:T(8,128)S(1)}, f32[2,8,1,128]{3,1,2,0:T(8,128)S(1)}, u32[]{:S(2)}, u32[]{:S(2)}) collective-permute-start(f32[2,8,1,128]{3,1,2,0:T(8,128)S(1)} %get-tuple-element.291), channel_id=1, source_target_pairs={{0,32},{32,64},{64,96},{96,128},{128,160},{160,192},{192,224},{224... | collective-permute-start | bytes 24584 | tf_op jit(solution)/shard_map/ppermute | solution.py:46
  114.5 11.6 %collective-permute-start.15 = (f32[2,8,4,1]{3,1,2,0:T(8,128)S(1)}, f32[2,8,4,1]{3,1,2,0:T(8,128)S(1)}, u32[]{:S(2)}, u32[]{:S(2)}) collective-permute-start(f32[2,8,4,1]{3,1,2,0:T(8,128)S(1)} %get-tuple-element.276), channel_id=1, source_target_pairs={{1,0},{2,1},{3,2},{4,3},{5,4},{6,5},{7,6},{8,7},{9,8},{10,9},{11,1... | collective-permute-start | bytes 776 | tf_op jit(solution)/shard_map/ppermute | solution.py:49
  129.1 13.6 %collective-permute-start.3 = (f32[26,8,6,1]{0,1,3,2:T(8,128)S(1)}, f32[26,8,6,1]{0,1,3,2:T(8,128)S(1)}, u32[]{:S(2)}, u32[]{:S(2)}) collective-permute-start(f32[26,8,6,1]{0,1,3,2:T(8,128)S(1)} %copy.254), channel_id=1, source_target_pairs={{1,0},{2,1},{3,2},{4,3},{5,4},{6,5},{7,6},{8,7},{9,8},{10,9},{11,1... | collective-permute-start | bytes 14984 | tf_op jit(solution)/shard_map/ppermute | solution.py:49
  148.5 29.8 %all-to-all-start.3 = ((f32[32,1,8]{2,1,0:T(1,128)}), f32[32,1,8]{2,1,0:T(1,128)}, u32[]{:S(2)}, u32[]{:S(2)}) async-start(f32[32,1,8]{2,1,0:T(1,128)} %convolution_bitcast_fusion.2), calls=%async_computation.3 | async-start | bytes 32768 | tf_op jit(solution)/shard_map/all_to_all | solution.py:182
  172.3 53.1 %collective-permute-start.8 = (f32[26,8,1,128]{3,2,1,0:T(1,128)S(1)}, f32[26,8,1,128]{3,2,1,0:T(1,128)S(1)}, u32[]{:S(2)}, u32[]{:S(2)}) collective-permute-start(f32[26,8,1,128]{3,2,1,0:T(1,128)S(1)} %get-tuple-element.255), channel_id=1, source_target_pairs={{0,32},{32,64},{64,96},{96,128},{128,160},{160,192},{192,224},{224... | collective-permute-start | bytes 319496 | tf_op jit(solution)/shard_map/ppermute | solution.py:46
  174.2 51.2 %collective-permute-start.9 = (f32[26,8,1,128]{3,2,1,0:T(1,128)S(1)}, f32[26,8,1,128]{3,2,1,0:T(1,128)S(1)}, u32[]{:S(2)}, u32[]{:S(2)}) collective-permute-start(f32[26,8,1,128]{3,2,1,0:T(1,128)S(1)} %get-tuple-element.256), channel_id=1, source_target_pairs={{32,0},{64,32},{96,64},{128,96},{160,128},{192,160},{224,192},{256... | collective-permute-start | bytes 319496 | tf_op jit(solution)/shard_map/ppermute | solution.py:49
  181.2 22.2 %all-to-all-start.4 = ((f32[32,1,8]{2,1,0:T(1,128)}), f32[32,1,8]{2,1,0:T(1,128)S(1)}, u32[]{:S(2)}, u32[]{:S(2)}) async-start(f32[32,1,8]{2,1,0:T(1,128)} %bitcast.143), calls=%async_computation.4 | async-start | bytes 32768 | tf_op jit(solution)/shard_map/all_to_all | solution.py:205
  204.7 11.5 %collective-permute-start.22 = (f32[2,8,4,1]{3,1,2,0:T(8,128)S(1)}, f32[2,8,4,1]{3,1,2,0:T(8,128)S(1)}, u32[]{:S(2)}, u32[]{:S(2)}) collective-permute-start(f32[2,8,4,1]{3,1,2,0:T(8,128)S(1)} %get-tuple-element.271), channel_id=1, source_target_pairs={{0,1},{1,2},{2,3},{3,4},{4,5},{5,6},{6,7},{7,8},{8,9},{9,10},{10,1... | collective-permute-start | bytes 776 | tf_op jit(solution)/shard_map/ppermute | solution.py:46
  213.1 11.6 %collective-permute-start.23 = (f32[2,8,4,1]{3,1,2,0:T(8,128)S(1)}, f32[2,8,4,1]{3,1,2,0:T(8,128)S(1)}, u32[]{:S(2)}, u32[]{:S(2)}) collective-permute-start(f32[2,8,4,1]{3,1,2,0:T(8,128)S(1)} %get-tuple-element.272), channel_id=1, source_target_pairs={{1,0},{2,1},{3,2},{4,3},{5,4},{6,5},{7,6},{8,7},{9,8},{10,9},{11,1... | collective-permute-start | bytes 776 | tf_op jit(solution)/shard_map/ppermute | solution.py:49
  227.0 13.4 %collective-permute-start.11 = (f32[26,8,6,1]{0,1,3,2:T(8,128)S(1)}, f32[26,8,6,1]{0,1,3,2:T(8,128)S(1)}, u32[]{:S(2)}, u32[]{:S(2)}) collective-permute-start(f32[26,8,6,1]{0,1,3,2:T(8,128)S(1)} %copy.266), channel_id=1, source_target_pairs={{1,0},{2,1},{3,2},{4,3},{5,4},{6,5},{7,6},{8,7},{9,8},{10,9},{11,1... | collective-permute-start | bytes 14984 | tf_op jit(solution)/shard_map/ppermute | solution.py:49
  246.2 32.5 %all-to-all-start.5 = ((f32[32,1,8]{2,1,0:T(1,128)}), f32[32,1,8]{2,1,0:T(1,128)}, u32[]{:S(2)}, u32[]{:S(2)}) async-start(f32[32,1,8]{2,1,0:T(1,128)} %convolution_bitcast_fusion.1), calls=%async_computation.5 | async-start | bytes 32768 | tf_op jit(solution)/shard_map/all_to_all | solution.py:182
  270.9 36.0 %collective-permute-start.17 = (f32[26,8,1,128]{3,2,1,0:T(1,128)S(1)}, f32[26,8,1,128]{3,2,1,0:T(1,128)S(1)}, u32[]{:S(2)}, u32[]{:S(2)}) collective-permute-start(f32[26,8,1,128]{3,2,1,0:T(1,128)S(1)} %get-tuple-element.252), channel_id=1, source_target_pairs={{32,0},{64,32},{96,64},{128,96},{160,128},{192,160},{224,192},{256... | collective-permute-start | bytes 319496 | tf_op jit(solution)/shard_map/ppermute | solution.py:49
  272.9 34.1 %collective-permute-start.16 = (f32[26,8,1,128]{3,2,1,0:T(1,128)S(1)}, f32[26,8,1,128]{3,2,1,0:T(1,128)S(1)}, u32[]{:S(2)}, u32[]{:S(2)}) collective-permute-start(f32[26,8,1,128]{3,2,1,0:T(1,128)S(1)} %get-tuple-element.253), channel_id=1, source_target_pairs={{0,32},{32,64},{64,96},{96,128},{128,160},{160,192},{192,224},{224... | collective-permute-start | bytes 319496 | tf_op jit(solution)/shard_map/ppermute | solution.py:46
  282.9 22.3 %all-to-all-start.6 = ((f32[32,1,8]{2,1,0:T(1,128)}), f32[32,1,8]{2,1,0:T(1,128)S(1)}, u32[]{:S(2)}, u32[]{:S(2)}) async-start(f32[32,1,8]{2,1,0:T(1,128)} %convolution_bitcast_fusion), calls=%async_computation.6 | async-start | bytes 32768 | tf_op jit(solution)/shard_map/all_to_all | solution.py:205
  309.8 16.9 %collective-permute-start.18 = (f32[26,8,6,1]{0,1,3,2:T(8,128)S(1)}, f32[26,8,6,1]{0,1,3,2:T(8,128)S(1)}, u32[]{:S(2)}, u32[]{:S(2)}) collective-permute-start(f32[26,8,6,1]{0,1,3,2:T(8,128)S(1)} %copy.277), channel_id=1, source_target_pairs={{0,1},{1,2},{2,3},{3,4},{4,5},{5,6},{6,7},{7,8},{8,9},{9,10},{10,1... | collective-permute-start | bytes 14984 | tf_op jit(solution)/shard_map/ppermute | solution.py:46
  314.8 11.4 %collective-permute-start.19 = (f32[26,8,6,1]{0,1,3,2:T(8,128)S(1)}, f32[26,8,6,1]{0,1,3,2:T(8,128)S(1)}, u32[]{:S(2)}, u32[]{:S(2)}) collective-permute-start(f32[26,8,6,1]{0,1,3,2:T(8,128)S(1)} %copy.279), channel_id=1, source_target_pairs={{1,0},{2,1},{3,2},{4,3},{5,4},{6,5},{7,6},{8,7},{9,8},{10,9},{11,1... | collective-permute-start | bytes 14984 | tf_op jit(solution)/shard_map/ppermute | solution.py:49
  (142 other events, 587.7 us)
where the time goes:
time: 336 us; the launch traced here: 333 us
  starting transfers between devices  176 us (52%)
  waiting for transfers between devices  61.4 us (18%)
  local copies, waits for them, and re-layouts  53.3 us (16%)
  other arithmetic  21.8 us (6%)
  matrix products  17 us (5%)
  between operations  3.64 us (1%)
    ppermute x12, starting transfers between devices, extended_2(): lax.ppermute(lax.slice_in_dim(block, block.shape[dim] - width, None, axis...  72.1 us
    ppermute x12, waiting for transfers between devices, extended_2(): lax.ppermute(lax.slice_in_dim(block, 0, width, axis=dim), axis, backward)  37.5 us
    all_to_all x3, starting transfers between devices, bridge_fluid_metal(): lax.all_to_all(outgoing_links, 'gy', split_axis=0, concat_axis=0, tiled=T...  33.8 us
    all_to_all x3, starting transfers between devices, bridge_fluid_metal(): lax.all_to_all(reply, 'gy', split_axis=0, concat_axis=0, tiled=True)  30 us
    ppermute x12, starting transfers between devices, extended_2(): lax.ppermute(lax.slice_in_dim(block, 0, width, axis=dim), axis, backward)  24.5 us
    unnamed x288, local copies, waits for them, and re-layouts  20.6 us
    all_to_all x1, starting transfers between devices, on_device(): lax.all_to_all(slot_sent.reshape(cell_groups, capacity), 'gy', split_axis...  15.8 us
    all_to_all x3, waiting for transfers between devices, bridge_fluid_metal(): lax.all_to_all(reply, 'gy', split_axis=0, concat_axis=0, tiled=True)  14.7 us
  transfers between devices with their start and end apart: 31, of which 11 were waited for; matrix products, arithmetic and copies ran while one was open for 15% of the time, Pallas kernels for 0%

commit v1 on v0

v1 whole, which is shorter than its diff:
```python
import functools

import jax
import jax.numpy as jnp
from jax import lax
from jax.experimental import pallas as pl
from jax.experimental.pallas import tpu as pltpu
from jax.sharding import PartitionSpec as P

MESH = pl.DeviceIdType.MESH
F32 = jnp.float32
STEPS = 3
CAP = 8

VELOCITY = [
    (0, 0, 0),
    (1, 0, 0),
    (-1, 0, 0),
    (0, 1, 0),
    (0, -1, 0),
    (0, 0, 1),
    (0, 0, -1),
    (1, 1, 0),
    (-1, -1, 0),
    (1, -1, 0),
    (-1, 1, 0),
    (1, 0, 1),
    (-1, 0, -1),
    (1, 0, -1),
    (-1, 0, 1),
    (0, 1, 1),
    (0, -1, -1),
    (0, 1, -1),
    (0, -1, 1),
]
OPPOSITE = [VELOCITY.index((-a, -b, -c)) for a, b, c in VELOCITY]
ORDER = [1, 7, 9, 11, 13, 2, 8, 10, 12, 14, 0, 3, 4, 5, 6, 15, 16, 17, 18]
PLACE = {q: n for n, q in enumerate(ORDER)}
FLOW_UP = [3, 7, 10, 15, 17]
FLOW_DOWN = [4, 8, 9, 16, 18]
HEAT_UP = [3]
HEAT_DOWN = [4]
DT = 0.04
ROOM = 63 * 1024 * 1024


def lane_of(shape):
    return lax.broadcasted_iota(jnp.int32, shape, len(shape) - 1)


def sub_of(shape):
    return lax.broadcasted_iota(jnp.int32, shape, len(shape) - 2)


def turn(value, amount, axis):
    size = value.shape[axis]
    amount = amount % size
    return value if amount == 0 else pltpu.roll(value, amount, axis)


def collide_flow(state, post, velocity):
    total, moved = None, [None, None, None]
    for q in range(19):
        value = state[q]
        total = value if total is None else total + value
        for axis in range(3):
            if VELOCITY[q][axis] == 1:
                moved[axis] = value if moved[axis] is None else moved[axis] + value
            elif VELOCITY[q][axis] == -1:
                moved[axis] = -value if moved[axis] is None else moved[axis] - value
    inverse = 1.0 / total
    speed = [part * inverse for part in moved]
    for axis in range(3):
        velocity[axis] = speed[axis]
    base = 1.0 - 1.5 * (speed[0] * speed[0] + speed[1] * speed[1] + speed[2] * speed[2])
    post[1:5, PLACE[0]] = (1.25 / 3.0) * total * base - 0.25 * state[0]
    axial = (1.25 / 18.0) * total
    diagonal = (1.25 / 36.0) * total
    for q in range(1, 19):
        if OPPOSITE[q] < q:
            continue
        along = None
        for axis in range(3):
            c = VELOCITY[q][axis]
            if c:
                term = speed[axis] if c == 1 else -speed[axis]
                along = term if along is None else along + term
        even = base + 4.5 * along * along
        odd = 3.0 * along
        scale = axial if q < 7 else diagonal
        post[1:5, PLACE[q]] = scale * (even + odd) - 0.25 * state[q]
        post[1:5, PLACE[OPPOSITE[q]]] = scale * (even - odd) - 0.25 * state[OPPOSITE[q]]


def collide_heat(state, post, velocity):
    keep = 1.0 - 1.0 / 0.7
    warmth = state[0]
    for q in range(1, 7):
        warmth = warmth + state[q]
    post[1:5, 0] = keep * state[0] + (0.25 / 0.7) * warmth
    part = (0.125 / 0.7) * warmth
    for axis in range(3):
        tilt = part * (4.0 * velocity[axis])
        for q in (1 + 2 * axis, 2 + 2 * axis):
            sign = tilt if q == 1 + 2 * axis else -tilt
            post[1:5, q] = keep * state[q] + (part + sign)


def pack_edges(post, rows_up, rows_down, shift_up, shift_down):
    lane = lane_of((8, 128))
    up = down = jnp.zeros((8, 128), F32)
    for n, (a, b) in enumerate(zip(rows_up, rows_down)):
        for x in range(4):
            k = 4 * n + x
            up = jnp.where(lane == k, turn(post[x + 1 - shift_up[n], a], k + 1, 1), up)
            down = jnp.where(lane == k, turn(post[x + 1 - shift_down[n], b], k, 1), down)
    return up, down


def moved_flat(post, row, vector, n, tile):
    cx, cy = vector[0], vector[1]
    value = post[1 - cx : 5 - cx, row]
    if cy == 0:
        return value
    edge = jnp.stack([turn(tile, (128 if cy == 1 else 127) - (4 * n + x), 1) for x in range(4)])
    lane = lane_of((4, 8, 128))
    if cy == 1:
        return jnp.where(lane == 0, edge, turn(value, 1, 2))
    return jnp.where(lane == 127, edge, turn(value, 127, 2))


def lifted(value, cz, bounce):
    if cz == 0:
        return value
    layer = sub_of((4, 8, 128))
    if cz == 1:
        return jnp.where(layer == 0, bounce, turn(value, 1, 1))
    return jnp.where(layer == 7, bounce, turn(value, 7, 1))


def stream_flow(post, from_below, from_above, put):
    for q in range(19):
        vector = VELOCITY[q]
        n, tile = 0, None
        if vector[1] == 1:
            n, tile = FLOW_UP.index(q), from_below
        elif vector[1] == -1:
            n, tile = FLOW_DOWN.index(q), from_above
        value = moved_flat(post, PLACE[q], vector, n, tile)
        put(q, lifted(value, vector[2], post[1:5, PLACE[OPPOSITE[q]]]))


def stream_heat(post, from_below, from_above, covered, put):
    for q in range(7):
        vector = VELOCITY[q]
        value = moved_flat(post, q, vector, 0, from_below if vector[1] == 1 else from_above)
        bounce = post[1:5, OPPOSITE[q]]
        if q == 5:
            bounce = jnp.where(covered > 0.5, -bounce, bounce)
        put(q, lifted(value, vector[2], bounce))


def conduct_of(warmth, k):
    return k * (1.0 + 0.5 * warmth)


def fluxes(field, k, low_x, low_xk, high_x, high_xk, low_y, low_yk, high_y, high_yk, gates):
    gate_low_x, gate_high_x, gate_low_y, gate_high_y = gates
    lane, layer = lane_of((8, 128)), sub_of((8, 128))
    cond = [conduct_of(field[x], k[x]) for x in range(2)]
    result = []

    def face(a, ca, b, cb):
        return 2.0 * ca * cb / (ca + cb) * (b - a)

    inner = face(field[0], cond[0], field[1], cond[1])
    for x in range(2):
        here, c = field[x], cond[x]
        if x == 0:
            total = inner + gate_low_x * face(here, c, low_x, conduct_of(low_x, low_xk))
        else:
            total = gate_high_x * face(here, c, high_x, conduct_of(high_x, high_xk)) - inner
        below = jnp.where(lane == 0, turn(low_y[x], 1, 1), turn(here, 1, 1))
        below_k = jnp.where(lane == 0, turn(low_yk[x], 1, 1), turn(k[x], 1, 1))
        above = jnp.where(lane == 127, turn(high_y[x], 127, 1), turn(here, 127, 1))
        above_k = jnp.where(lane == 127, turn(high_yk[x], 127, 1), turn(k[x], 127, 1))
        total = total + jnp.where(lane == 0, gate_low_y, 1.0) * face(here, c, below, conduct_of(below, below_k))
        total = total + jnp.where(lane == 127, gate_high_y, 1.0) * face(here, c, above, conduct_of(above, above_k))
        down = face(here, c, turn(here, 1, 0), turn(c, 1, 0))
        up = face(here, c, turn(here, 7, 0), turn(c, 7, 0))
        total = total + jnp.where(layer == 0, 0.0, down) + jnp.where(layer == 7, 0.0, up)
        result.append(total)
    return result


def kernel(
    nx,
    ny,
    f_hbm,
    g_hbm,
    s_hbm,
    m_hbm,
    owner_hbm,
    tally_hbm,
    wall_hbm,
    face_hbm,
    f_out,
    g_out,
    s_out,
    f_in,
    g_in,
    s_in,
    m_in,
    owner_in,
    tally_in,
    wall_in,
    face_in,
    flow,
    heat,
    post_f,
    post_g,
    speeds,
    x_out,
    x_in,
    y_out,
    y_in,
    flow_out,
    flow_in,
    wall_mask,
    covered_ref,
    cell_ref,
    slot_key,
    early,
    got_early,
    late,
    got_late,
    mid,
    got_mid,
    third,
    got_third,
    answer_out,
    got_answer,
    i_sem,
    n_send,
    n_recv,
    g_send,
    g_recv,
):
    arrivals = []
    for n, (source, target) in enumerate(
        (
            (g_hbm, g_in),
            (f_hbm, f_in),
            (s_hbm, s_in),
            (m_hbm, m_in),
            (owner_hbm, owner_in),
            (tally_hbm, tally_in),
            (wall_hbm, wall_in),
            (face_hbm, face_in),
        )
    ):
        made = pltpu.make_async_copy(source, target, i_sem.at[n])
        made.start()
        arrivals.append(made)

    i, j = lax.axis_index("gx"), lax.axis_index("gy")
    right, left = lax.rem(i + 1, nx), lax.rem(i + nx - 1, nx)
    upper, lower = lax.rem(j + 1, ny), lax.rem(j + ny - 1, ny)
    barrier = pltpu.get_barrier_semaphore()
    for device in ((right, j), (left, j), (i, upper), (i, lower)):
        pl.semaphore_signal(barrier, inc=1, device_id=device, device_id_type=MESH)

    @pl.loop(1, ny)
    def _(o):
        pl.semaphore_signal(barrier, inc=1, device_id=(i, lax.rem(j + o, ny)), device_id_type=MESH)

    counter = [0]

    def copy(source, target, device):
        n = counter[0]
        counter[0] += 1
        made = pltpu.make_async_remote_copy(
            src_ref=source,
            dst_ref=target,
            send_sem=n_send.at[n],
            recv_sem=n_recv.at[n],
            device_id=device,
            device_id_type=MESH,
        )
        made.start()
        return made

    def settle(copies):
        for made in copies:
            made.wait()

    def send_flow_x(t):
        return [
            copy(post_f.at[t, 4, pl.ds(0, 5)], post_f.at[t, 0, pl.ds(0, 5)], (right, j)),
            copy(post_f.at[t, 1, pl.ds(5, 5)], post_f.at[t, 5, pl.ds(5, 5)], (left, j)),
        ]

    def send_flow_y(t):
        up, down = pack_edges(
            post_f.at[t],
            [PLACE[q] for q in FLOW_UP],
            [PLACE[q] for q in FLOW_DOWN],
            [VELOCITY[q][0] for q in FLOW_UP],
            [VELOCITY[q][0] for q in FLOW_DOWN],
        )
        flow_out[t, 0] = up
        flow_out[t, 1] = down
        return [
            copy(flow_out.at[t, 0], flow_in.at[t, 0], (i, upper)),
            copy(flow_out.at[t, 1], flow_in.at[t, 1], (i, lower)),
        ]

    def send_x(r, right_tiles, left_tiles):
        span = pl.ds(0, len(right_tiles))
        for n, (a, b) in enumerate(zip(right_tiles, left_tiles)):
            x_out[r, 0, n], x_out[r, 1, n] = a, b
        return [
            copy(x_out.at[r, 0, span], x_in.at[r, 0, span], (right, j)),
            copy(x_out.at[r, 1, span], x_in.at[r, 1, span], (left, j)),
        ]

    def send_y(r, up_tiles, down_tiles):
        span = pl.ds(0, len(up_tiles))
        for n, (a, b) in enumerate(zip(up_tiles, down_tiles)):
            y_out[r, 0, n], y_out[r, 1, n] = a, b
        return [
            copy(y_out.at[r, 0, span], y_in.at[r, 0, span], (i, upper)),
            copy(y_out.at[r, 1, span], y_in.at[r, 1, span], (i, lower)),
        ]

    def send_solid(r, field):
        return send_y(r, field, field) + send_x(r, [field[1]], [field[0]])

    def send_heat(t):
        post = post_g.at[t]
        up, down = pack_edges(post, [3], [4], [0], [0])
        return send_y(3 + t, [up], [down]) + send_x(3 + t, [post[4, 1]], [post[1, 2]])

    def to_all(source, target, pair, personal):
        @pl.loop(0, ny - 1)
        def _(s):
            pltpu.make_async_remote_copy(
                src_ref=source.at[s] if personal else source.at[0],
                dst_ref=target.at[ny - 2 - s],
                send_sem=g_send.at[pair],
                recv_sem=g_recv.at[pair],
                device_id=(i, lax.rem(j + 2 * ny - 1 - s, ny)),
                device_id_type=MESH,
            ).start()

        target[ny - 1] = source[ny - 1 if personal else 0]

    def from_all(target, pair):
        span = pl.ds(0, ny - 1)
        pltpu.make_async_copy(target.at[span], target.at[span], g_recv.at[pair]).wait()

    def all_sent(target, pair):
        span = pl.ds(0, ny - 1)
        pltpu.make_async_copy(target.at[span], target.at[span], g_send.at[pair]).wait()

    for n in (2, 3):
        arrivals[n].wait()
    solid_0 = [s_in[pl.ds(x, 8, stride=2), :] for x in range(2)]
    k = [0.2 + 0.8 * m_in[pl.ds(x, 8, stride=2), :].astype(F32) for x in range(2)]
    pl.semaphore_wait(barrier, ny - 1 + 4)
    solid_x_halo = send_x(0, [solid_0[1], k[1]], [solid_0[0], k[0]])
    solid_y_halo = send_y(0, solid_0 + k, solid_0 + k)

    square = (128, 128)
    lane, sub = lane_of(square), sub_of(square)
    lane_8, sub_8 = lane_of((8, 128)), sub_of((8, 128))
    lane_32, sub_32 = lane_of((32, 128)), sub_of((32, 128))
    diagonal = lane == sub

    def column(row):
        return jnp.sum(jnp.where(diagonal, jnp.broadcast_to(row, square), 0.0), axis=1, keepdims=True)

    def as_row(col):
        return jnp.sum(jnp.where(diagonal, jnp.broadcast_to(col, square), 0.0), axis=0, keepdims=True)

    for n in (4, 5, 6, 7):
        arrivals[n].wait()
    owner = owner_in[...]
    face_index = face_in[...]
    wall = wall_in[...]
    live = lane_of((1, 128)) < jnp.broadcast_to(tally_in[...], (1, 128))
    block = (j - owner - 1) & (ny - 1)
    cell_row = jnp.where(live, owner * 256 + face_index, -1).astype(F32)
    live_col = column(jnp.where(live, 1.0, 0.0))
    block_row = block.astype(F32)
    block_col = column(block_row)
    face_col = column(face_index.astype(F32))
    wall_y_col = column((wall & 127).astype(F32))
    wall_x_col = column((wall >> 7).astype(F32))
    rank_col = jnp.sum(
        jnp.where((jnp.broadcast_to(block_row, square) == block_col) & (lane < sub), 1.0, 0.0),
        axis=1,
        keepdims=True,
    )
    lane_f = lane.astype(F32)
    wall_hit = jnp.where(lane_f == wall_y_col, live_col, 0.0)
    for x in range(4):
        wall_mask[x] = jnp.where(wall_x_col == float(x), wall_hit, 0.0)
    slot_key[...] = jnp.where((lane & 7).astype(F32) == rank_col, jnp.broadcast_to(live_col, square), 0.0)
    to_owner = jnp.where(jnp.broadcast_to(block_row, (32, 128)) == sub_32.astype(F32), 1.0, 0.0)

    def at_wall(rows):
        total = wall_mask[0] * rows[0]
        for x in range(1, 4):
            total = total + wall_mask[x] * rows[x]
        return jnp.sum(total, axis=1, keepdims=True)

    def on_wall(col):
        return [jnp.sum(wall_mask[x] * col, axis=0, keepdims=True) for x in range(4)]

    def slots(first, second):
        fields = jnp.where(lane < 8, first, jnp.where(lane < 16, second, 0.0))
        return jnp.dot(
            to_owner, fields * slot_key[...], precision=lax.Precision.HIGHEST, preferred_element_type=F32
        )

    def fill(buffer, n, value):
        buffer[:, n, :] = jnp.broadcast_to(value, (32, 128))

    arrivals[0].wait()
    for q in range(7):
        for x in range(4):
            heat[q, x] = g_in[q, pl.ds(x, 8, stride=4), :]

    def wall_sums():
        total = heat[0, :, 0:1, :]
        for q in range(1, 7):
            total = total + heat[q, :, 0:1, :]
        return [total[x] for x in range(4)]

    t1_col = at_wall(wall_sums())
    fill(early, 0, cell_row)
    fill(early, 1, as_row(t1_col))
    early[:, 2, :] = slots(t1_col, face_col + 1.0)
    row_lane = lane_of((1, 128))
    k_top = [k[x][7:8] for x in range(2)]
    k_inner = jnp.where(row_lane == 1, turn(k_top[1], 1, 1), turn(k_top[1], 127, 1))
    fill(early, 3, jnp.where((row_lane == 0) | (row_lane == 127), k_top[0], k_inner))
    for x in range(2):
        fill(early, 4 + x, solid_0[x][7:8])
    to_all(early, got_early, 0, True)

    arrivals[1].wait()
    for q in range(19):
        for x in range(4):
            flow[q, x] = f_in[q, pl.ds(x, 8, stride=4), :]
    collide_flow(flow, post_f.at[0], speeds.at[0])
    collide_heat(heat, post_g.at[0], speeds.at[0])
    heat_halo = send_heat(0)
    flow_halo = send_flow_x(0)

    gates_x = (jnp.where(i == 0, 0.0, 1.0), jnp.where(i == nx - 1, 0.0, 1.0))
    gates_y = (jnp.where(j == 0, 0.0, 1.0), jnp.where(j == ny - 1, 0.0, 1.0))

    def conduct(field, r, inner=False):
        change = fluxes(
            field,
            k,
            x_in[r, 0, 0],
            x_in[0, 0, 1],
            x_in[r, 1, 0],
            x_in[0, 1, 1],
            field if inner else [y_in[r, 0, x] for x in range(2)],
            k if inner else [y_in[0, 0, 2 + x] for x in range(2)],
            field if inner else [y_in[r, 1, x] for x in range(2)],
            k if inner else [y_in[0, 1, 2 + x] for x in range(2)],
            gates_x + ((0.0, 0.0) if inner else gates_y),
        )
        return [field[x] + DT * change[x] for x in range(2)]

    def move_heat(t, put):
        post_g[t, 0, 1] = x_in[3 + t, 0, 0]
        post_g[t, 5, 2] = x_in[3 + t, 1, 0]
        stream_heat(post_g.at[t], y_in[3 + t, 0, 0], y_in[3 + t, 1, 0], covered_ref[...], put)

    def move_flow(t, put):
        stream_flow(post_f.at[t], flow_in[t, 0], flow_in[t, 1], put)

    def put_heat(q, value):
        heat[q] = value

    def put_flow(q, value):
        flow[q] = value

    settle(solid_x_halo)
    inner_1 = conduct(solid_0, 0, inner=True)
    for x in range(2):
        late[0, x : x + 1, :] = inner_1[x][7:8]
    to_all(late, got_late, 1, False)

    cell_ref[...] = jnp.broadcast_to(column(cell_row), square)
    for x in range(4):
        covered_ref[x] = jnp.broadcast_to(jnp.sum(wall_mask[x], axis=0, keepdims=True), (8, 128))
    face_hit = jnp.where(lane_f == column((face_index & 127).astype(F32)), 1.0, 0.0)
    lane_64 = lane_of((128, 64))
    face_x_col = column((face_index >> 7).astype(F32))
    pick = jnp.where(
        ((lane_64 & 31).astype(F32) == block_col) & ((lane_64 >> 5).astype(F32) == face_x_col), 1.0, 0.0
    )

    settle(heat_halo)
    move_heat(0, put_heat)
    third[:, 0, :] = slots(at_wall(wall_sums()), 0.0)
    to_all(third, got_third, 2, True)

    settle(flow_halo)
    flow_halo = send_flow_y(0)
    settle(solid_y_halo)
    p1 = conduct(solid_0, 0)

    from_all(got_early, 0)

    def slot_columns(value, field):
        return [
            jnp.broadcast_to(
                jnp.sum(jnp.where(lane_32 == 8 * field + c, value, 0.0), axis=1, keepdims=True), (32, 128)
            )
            for c in range(CAP)
        ]

    faces = slot_columns(got_early[:, 2, :], 1)

    def own_sums(fields):
        result = []
        for x in range(2):
            place = (lane_32 + (128 * x + 1)).astype(F32)
            totals = [jnp.zeros((32, 128), F32) for _ in fields]
            for c in range(CAP):
                hit = faces[c] == place
                for n, field in enumerate(fields):
                    totals[n] = totals[n] + jnp.where(hit, 1.0 if field is None else field[c], 0.0)
            result.append([jnp.sum(total, axis=0, keepdims=True) for total in totals])
        return result

    def on_top(value, row):
        return value + jnp.where(sub_8 == 7, jnp.broadcast_to(row, (8, 128)), 0.0)

    sums = own_sums([slot_columns(got_early[:, 2, :], 0), None])
    many = [sums[x][1] for x in range(2)]
    solid_1 = [on_top(p1[x], DT * (sums[x][0] - many[x] * solid_0[x][7:8])) for x in range(2)]
    solid_halo = send_solid(1, solid_1)

    def same_cell(ref, n, count):
        cells = cell_ref[...]

        def body(b, carry):
            hit = cells == got_early[b, 0:1, :]
            total = carry[0] + jnp.where(hit, ref[b, n : n + 1, :], 0.0)
            if count:
                return total, carry[1] + jnp.where(hit, 1.0, 0.0)
            return (total,)

        zero = jnp.zeros(square, F32)
        return lax.fori_loop(0, ny, body, (zero, zero) if count else (zero,))

    total_1, number = same_cell(got_early, 1, True)
    number_col = jnp.sum(number, axis=1, keepdims=True)
    edge_k = got_early[:, 3, :]
    crossing = []
    for x in range(2):
        here = got_early[:, 4 + x, :]
        here_k = edge_k if x == 0 else jnp.where(lane_32 == 0, turn(edge_k, 127, 1), turn(edge_k, 1, 1))
        beyond, beyond_k = (turn(turn(part, 1, 0), 127, 1) for part in (here, here_k))
        c, cb = conduct_of(here, here_k), conduct_of(beyond, beyond_k)
        up = 2.0 * c * cb / (c + cb) * (beyond - here)
        up = jnp.where((lane_32 == 127) & (sub_32 != j), up, 0.0)
        crossing.append(DT * (up - turn(turn(up, 31, 0), 1, 1)))
    settle(flow_halo)
    move_flow(0, put_flow)
    collide_flow(flow, post_f.at[1], speeds.at[1])
    flow_halo = send_flow_x(1)

    from_all(got_late, 1)
    surfaces = jnp.concatenate(
        [
            jnp.concatenate([got_late[:, x, :] + crossing[x] for x in range(2)], axis=0),
            jnp.concatenate([got_early[:, 4 + x, :] for x in range(2)], axis=0),
        ],
        axis=1,
    )
    picked = jnp.dot(pick, surfaces, precision=lax.Precision.HIGHEST, preferred_element_type=F32)
    w1_col = jnp.sum(
        face_hit * (picked[:, 0:128] - DT * number_col * picked[:, 128:256]) + DT * total_1,
        axis=1,
        keepdims=True,
    )

    def warm_wall(col):
        rows = on_wall(col)
        for x in range(4):
            heat[5, x] = heat[5, x] + jnp.where(sub_8 == 0, 0.25 * rows[x], 0.0)

    warm_wall(w1_col)
    collide_heat(heat, post_g.at[1], speeds.at[1])
    heat_halo = send_heat(1)

    from_all(got_third, 2)
    rest = own_sums([slot_columns(got_third[:, 0, :], 0)])
    settle(solid_halo)
    solid_2 = conduct(solid_1, 1)
    solid_2 = [
        on_top(solid_2[x], DT * (rest[x][0] - 0.75 * many[x] * solid_1[x][7:8])) for x in range(2)
    ]
    solid_halo = send_solid(2, solid_2)

    def at_slots(rows, field, total):
        for c in range(CAP):
            first = faces[c] == (lane_32 + 1).astype(F32)
            second = faces[c] == (lane_32 + 129).astype(F32)
            at_cell = jnp.where(first, rows[0][7:8], jnp.where(second, rows[1][7:8], 0.0))
            total = jnp.where(lane_32 == 8 * field + c, jnp.sum(at_cell, axis=1, keepdims=True), total)
        return total

    answer = at_slots(solid_2, 1, jnp.zeros((32, 128), F32))
    settle(heat_halo)
    move_heat(1, put_heat)
    a3_col = at_wall(wall_sums())
    fill(mid, 0, as_row(a3_col))
    mid[:, 1, :] = jnp.where(lane_32 < 8, slots(a3_col, 0.0), answer)
    to_all(mid, got_mid, 3, True)

    settle(flow_halo)
    flow_halo = send_flow_y(1)

    settle(solid_halo)
    p3 = conduct(solid_2, 2)
    p3 = [on_top(p3[x], (-0.75 * DT) * many[x] * solid_2[x][7:8]) for x in range(2)]
    answer_out[:, 0, :] = at_slots(p3, 0, jnp.zeros((32, 128), F32))
    to_all(answer_out, got_answer, 4, True)

    settle(flow_halo)
    move_flow(1, put_flow)
    collide_flow(flow, post_f.at[2], speeds.at[2])
    flow_halo = send_flow_x(2)

    pick_owner = jnp.where(lane_of((128, 32)).astype(F32) == block_col, 1.0, 0.0)

    def replies(value, field):
        found = jnp.dot(pick_owner, value, precision=lax.Precision.HIGHEST, preferred_element_type=F32)
        return jnp.where((lane - 8 * field).astype(F32) == rank_col, found, 0.0)

    from_all(got_mid, 3)
    w2_col = jnp.sum(replies(got_mid[:, 1, :], 1), axis=1, keepdims=True)
    warm_wall(w2_col)
    collide_heat(heat, post_g.at[2], speeds.at[2])
    heat_halo = send_heat(2)

    settle(flow_halo)
    flow_halo = send_flow_y(2)
    (total_3,) = same_cell(got_mid, 0, False)
    last = own_sums([slot_columns(got_mid[:, 1, :], 0)])
    for x in range(2):
        s_out[pl.ds(x, 8, stride=2), :] = on_top(p3[x], DT * last[x][0])

    from_all(got_answer, 4)
    w3_col = jnp.sum(replies(got_answer[:, 0, :], 0) + DT * total_3, axis=1, keepdims=True)
    w3_rows = on_wall(w3_col)

    settle(flow_halo)

    def write_flow(q, value):
        for x in range(4):
            f_out[q, pl.ds(x, 8, stride=4), :] = value[x]

    move_flow(2, write_flow)

    settle(heat_halo)

    def write_heat(q, value):
        for x in range(4):
            row = value[x]
            if q == 5:
                row = row + jnp.where(sub_8 == 0, 0.25 * w3_rows[x], 0.0)
            g_out[q, pl.ds(x, 8, stride=4), :] = row

    move_heat(2, write_heat)

    for n, target in enumerate((got_early, got_late, got_third, got_mid, got_answer)):
        all_sent(target, n)


def finish(*refs):
    sources, targets, sems = refs[0:3], refs[3:6], refs[6]
    copies = [pltpu.make_async_copy(a, b, sems.at[n]) for n, (a, b) in enumerate(zip(sources, targets))]
    for made in copies:
        made.start()
    for made in copies:
        made.wait()


def on_device(nx, ny, flow, heat, solid, metal, owner, tally, wall, face):
    vmem = functools.partial(pltpu.VMEM, dtype=F32)
    tile = (8, 128)
    copies = 3 * 4 + 6 * 4
    results = (
        jax.ShapeDtypeStruct((19, 32, 128), F32),
        jax.ShapeDtypeStruct((7, 32, 128), F32),
        jax.ShapeDtypeStruct((16, 128), F32),
    )
    out = pl.pallas_call(
        functools.partial(kernel, nx, ny),
        out_shape=tuple(pltpu.VMEM(result.shape, result.dtype) for result in results),
        in_specs=[pl.BlockSpec(memory_space=pltpu.HBM)] * 8,
        out_specs=[pl.BlockSpec(memory_space=pltpu.VMEM)] * 3,
        scratch_shapes=[
            vmem((19, 32, 128)),
            vmem((7, 32, 128)),
            vmem((16, 128)),
            pltpu.VMEM((16, 128), jnp.int32),
            pltpu.VMEM((1, 128), jnp.int32),
            pltpu.VMEM((1, 1), jnp.int32),
            pltpu.VMEM((1, 128), jnp.int32),
            pltpu.VMEM((1, 128), jnp.int32),
            vmem((19, 4) + tile),
            vmem((7, 4) + tile),
            vmem((STEPS, 6, 19) + tile),
            vmem((STEPS, 6, 7) + tile),
            vmem((STEPS, 3, 4) + tile),
            vmem((6, 2, 2) + tile),
            vmem((6, 2, 2) + tile),
            vmem((6, 2, 4) + tile),
            vmem((6, 2, 4) + tile),
            vmem((STEPS, 2) + tile),
            vmem((STEPS, 2) + tile),
            vmem((4, 128, 128)),
            vmem((4,) + tile),
            vmem((128, 128)),
            vmem((128, 128)),
            vmem((32, 6, 128)),
            vmem((32, 6, 128)),
            vmem((1, 2, 128)),
            vmem((32, 2, 128)),
            vmem((32, 2, 128)),
            vmem((32, 2, 128)),
            vmem((32, 1, 128)),
            vmem((32, 1, 128)),
            vmem((32, 1, 128)),
            vmem((32, 1, 128)),
            pltpu.SemaphoreType.DMA((8,)),
            pltpu.SemaphoreType.DMA((copies,)),
            pltpu.SemaphoreType.DMA((copies,)),
            pltpu.SemaphoreType.DMA((5,)),
            pltpu.SemaphoreType.DMA((5,)),
        ],
        compiler_params=pltpu.CompilerParams(
            collective_id=0, has_side_effects=True, vmem_limit_bytes=ROOM
        ),
        name="coupled_steps",
    )(
        flow.reshape(19, 32, 128),
        heat.reshape(7, 32, 128),
        solid.reshape(16, 128),
        metal.reshape(16, 128),
        owner.reshape(1, 128),
        tally,
        wall,
        face,
    )
    out = pl.pallas_call(
        finish,
        out_shape=results,
        in_specs=[pl.BlockSpec(memory_space=pltpu.VMEM)] * 3,
        out_specs=[pl.BlockSpec(memory_space=pltpu.HBM)] * 3,
        scratch_shapes=[pltpu.SemaphoreType.DMA((3,))],
        name="write_out",
    )(*out)
    return out[0].reshape(19, 8, 4, 128), out[1].reshape(7, 8, 4, 128), out[2].reshape(8, 2, 128)


def solution(mesh):
    placed = (
        P(None, None, "gx", "gy"),
        P(None, None, "gx", "gy"),
        P(None, "gx", "gy"),
        P(None, "gx", "gy"),
        P("gx", "gy", None),
        P("gx", "gy"),
        P("gx", "gy"),
        P("gx", "gy"),
    )
    return jax.shard_map(
        functools.partial(on_device, mesh.shape["gx"], mesh.shape["gy"]),
        mesh=mesh,
        in_specs=placed,
        out_specs=(P(None, None, "gx", "gy"), P(None, None, "gx", "gy"), P(None, "gx", "gy")),
        check_vma=False,
    )
```

time: 336 us -> 57.6 us (0.17)
  the two profiles are of different devices: /device:TPU:63 before, /device:TPU:1 now
where the time goes in v1:
time: 57.6 us; the launch traced here: 57.4 us
  Pallas kernels  54.2 us (94%)
  local copies, waits for them, and re-layouts  1.94 us (3%)
  between operations  1.3 us (2%)
    pallas_call x1, Pallas kernels, on_device(): pl.pallas_call(functools.partial(kernel, nx, ny), out_shape=tuple((pltpu....  52.4 us
    unnamed x6, local copies, waits for them, and re-layouts  1.94 us
    pallas_call x1, Pallas kernels, on_device(): pl.pallas_call(finish, out_shape=results, in_specs=[pl.BlockSpec(memory_s...  1.81 us

profile of v1, /device:TPU:1, one launch (start us, length us, event | category | flops | bytes accessed | tf_op | source)
XLA Modules:
  0.0 57.4 jit_solution(2188888993892664805)
XLA Ops:
  1.3 52.4 %coupled_steps.1 = (f32[19,32,128]{2,1,0:T(8,128)S(1)}, f32[7,32,128]{2,1,0:T(8,128)S(1)}, f32[16,128]{1,0:T(8,128)S(1)}) custom-call(f32[19,32,128]{2,1,0:T(8,128)} %bitcast.8, f32[7,32,128]{2,1,0:T(8,128)} %bitcast.9, f32[16,128]{1,0:T(8,128)} %bitcast.10, s32[16,128]{1,0:T(8,128)} %bitcast.11, s32[1,128]{1,0:T(1,128)} %bitcast.12, ...), custom_call_target="tpu_custom_call" | custom-call | tf_op jit(solution)/shard_map/coupled_steps/pallas_call | solution.py:710
  53.7 0.0 copy-start
  53.7 0.7 %copy-done = f32[19,32,128]{2,1,0:T(8,128)} copy-done((f32[19,32,128]{2,1,0:T(8,128)}, f32[19,32,128]{2,1,0:T(8,128)S(1)}, u32[]{:S(2)}) %copy-start) | copy-done | bytes 311320
  54.4 0.0 copy-start.1
  54.4 0.6 %copy-done.1 = f32[7,32,128]{2,1,0:T(8,128)} copy-done((f32[7,32,128]{2,1,0:T(8,128)}, f32[7,32,128]{2,1,0:T(8,128)S(1)}, u32[]{:S(2)}) %copy-start.1) | copy-done | bytes 114712
  55.0 0.0 copy-start.2
  55.0 0.6 %copy-done.2 = f32[16,128]{1,0:T(8,128)} copy-done((f32[16,128]{1,0:T(8,128)}, f32[16,128]{1,0:T(8,128)S(1)}, u32[]{:S(2)}) %copy-start.2) | copy-done | bytes 8216
  55.6 1.8 %write_out.1 = (f32[19,32,128]{2,1,0:T(8,128)}, f32[7,32,128]{2,1,0:T(8,128)}, f32[16,128]{1,0:T(8,128)}) custom-call(f32[19,32,128]{2,1,0:T(8,128)} %copy-done, f32[7,32,128]{2,1,0:T(8,128)} %copy-done.1, f32[16,128]{1,0:T(8,128)} %copy-done.2), custom_call_target="tpu_custom_call" | custom-call | tf_op jit(solution)/shard_map/write_out/pallas_call | solution.py:769
Async XLA Ops:
  53.7 0.7 %copy-start = (f32[19,32,128]{2,1,0:T(8,128)}, f32[19,32,128]{2,1,0:T(8,128)S(1)}, u32[]{:S(2)}) copy-start(f32[19,32,128]{2,1,0:T(8,128)S(1)} %get-tuple-element.9.refs_0_) | copy-start | bytes 933892
  54.4 0.6 %copy-start.1 = (f32[7,32,128]{2,1,0:T(8,128)}, f32[7,32,128]{2,1,0:T(8,128)S(1)}, u32[]{:S(2)}) copy-start(f32[7,32,128]{2,1,0:T(8,128)S(1)} %get-tuple-element.10.refs_1_) | copy-start | bytes 344068
  55.0 0.6 %copy-start.2 = (f32[16,128]{1,0:T(8,128)}, f32[16,128]{1,0:T(8,128)S(1)}, u32[]{:S(2)}) copy-start(f32[16,128]{1,0:T(8,128)S(1)} %get-tuple-element.11.refs_2_) | copy-start | bytes 24580

commit v2 on v1

v2 whole, which is shorter than its diff:
```python
import functools

import jax
import jax.numpy as jnp
from jax import lax
from jax.experimental import pallas as pl
from jax.experimental.pallas import tpu as pltpu
from jax.sharding import PartitionSpec as P

MESH = pl.DeviceIdType.MESH
F32 = jnp.float32
STEPS = 3
CAP = 8

VELOCITY = [
    (0, 0, 0),
    (1, 0, 0),
    (-1, 0, 0),
    (0, 1, 0),
    (0, -1, 0),
    (0, 0, 1),
    (0, 0, -1),
    (1, 1, 0),
    (-1, -1, 0),
    (1, -1, 0),
    (-1, 1, 0),
    (1, 0, 1),
    (-1, 0, -1),
    (1, 0, -1),
    (-1, 0, 1),
    (0, 1, 1),
    (0, -1, -1),
    (0, 1, -1),
    (0, -1, 1),
]
OPPOSITE = [VELOCITY.index((-a, -b, -c)) for a, b, c in VELOCITY]
ORDER = [1, 7, 9, 11, 13, 2, 8, 10, 12, 14, 0, 3, 4, 5, 6, 15, 16, 17, 18]
PLACE = {q: n for n, q in enumerate(ORDER)}
DT = 0.04
ROOM = 63 * 1024 * 1024


def lane_of(shape):
    return lax.broadcasted_iota(jnp.int32, shape, len(shape) - 1)


def sub_of(shape):
    return lax.broadcasted_iota(jnp.int32, shape, len(shape) - 2)


def turn(value, amount, axis):
    size = value.shape[axis]
    amount = amount % size
    return value if amount == 0 else pltpu.roll(value, amount, axis)


def collide_flow(state, post, velocity, span):
    total, moved = None, [None, None, None]
    for q in range(19):
        value = state[q, :, :, span]
        total = value if total is None else total + value
        for axis in range(3):
            if VELOCITY[q][axis] == 1:
                moved[axis] = value if moved[axis] is None else moved[axis] + value
            elif VELOCITY[q][axis] == -1:
                moved[axis] = -value if moved[axis] is None else moved[axis] - value
    inverse = 1.0 / total
    speed = [part * inverse for part in moved]
    for axis in range(3):
        velocity[axis, :, :, span] = speed[axis]
    base = 1.0 - 1.5 * (speed[0] * speed[0] + speed[1] * speed[1] + speed[2] * speed[2])
    post[1:5, PLACE[0], :, span] = (1.25 / 3.0) * total * base - 0.25 * state[0, :, :, span]
    axial = (1.25 / 18.0) * total
    diagonal = (1.25 / 36.0) * total
    for q in range(1, 19):
        p = OPPOSITE[q]
        if p < q:
            continue
        along = None
        for axis in range(3):
            c = VELOCITY[q][axis]
            if c:
                term = speed[axis] if c == 1 else -speed[axis]
                along = term if along is None else along + term
        even = base + 4.5 * along * along
        odd = 3.0 * along
        scale = axial if q < 7 else diagonal
        post[1:5, PLACE[q], :, span] = scale * (even + odd) - 0.25 * state[q, :, :, span]
        post[1:5, PLACE[p], :, span] = scale * (even - odd) - 0.25 * state[p, :, :, span]


def collide_heat(state, post, velocity, span):
    keep = 1.0 - 1.0 / 0.7
    warmth = state[0, :, :, span]
    for q in range(1, 7):
        warmth = warmth + state[q, :, :, span]
    post[1:5, 0, :, span] = keep * state[0, :, :, span] + (0.25 / 0.7) * warmth
    part = (0.125 / 0.7) * warmth
    for axis in range(3):
        tilt = part * (4.0 * velocity[axis, :, :, span])
        for q in (1 + 2 * axis, 2 + 2 * axis):
            sign = tilt if q == 1 + 2 * axis else -tilt
            post[1:5, q, :, span] = keep * state[q, :, :, span] + (part + sign)


def lifted(value, cz, bounce):
    if cz == 0:
        return value
    layer = sub_of(value.shape)
    if cz == 1:
        return jnp.where(layer == 0, bounce, turn(value, 1, 1))
    return jnp.where(layer == 7, bounce, turn(value, 7, 1))


def stream(post, places, covered, put):
    for q, place in enumerate(places):
        cx, cy, cz = VELOCITY[q]
        value = turn(post[1 - cx : 5 - cx, place], cy, 2)
        bounce = None
        if cz:
            bounce = post[1:5, places[OPPOSITE[q]]]
            if covered is not None and q == 5:
                bounce = jnp.where(covered > 0.5, -bounce, bounce)
        put(q, lifted(value, cz, bounce))


FLOW_PLACES = [PLACE[q] for q in range(19)]
HEAT_PLACES = list(range(7))


def conduct_of(warmth, k):
    return k * (1.0 + 0.5 * warmth)


def fluxes(field, k, low_x, low_xk, high_x, high_xk, gates):
    gate_low_x, gate_high_x, gate_low_y, gate_high_y = gates
    shape = field[0].shape
    lane, layer = lane_of(shape), sub_of(shape)
    cond = [conduct_of(field[x], k[x]) for x in range(2)]
    result = []

    def face(a, ca, b, cb):
        return 2.0 * ca * cb / (ca + cb) * (b - a)

    inner = face(field[0], cond[0], field[1], cond[1])
    for x in range(2):
        here, c = field[x], cond[x]
        if x == 0:
            total = inner + gate_low_x * face(here, c, low_x, conduct_of(low_x, low_xk))
        else:
            total = gate_high_x * face(here, c, high_x, conduct_of(high_x, high_xk)) - inner
        above = face(here, c, turn(here, -1, 1), turn(c, -1, 1))
        below = -turn(above, 1, 1)
        total = total + jnp.where(lane == 127, gate_high_y, 1.0) * above
        total = total + jnp.where(lane == 0, gate_low_y, 1.0) * below
        up = face(here, c, turn(here, 7, 0), turn(c, 7, 0))
        down = -turn(up, 1, 0)
        total = total + jnp.where(layer == 0, 0.0, down) + jnp.where(layer == 7, 0.0, up)
        result.append(total)
    return result


def kernel(
    nx,
    ny,
    f_hbm,
    g_hbm,
    s_hbm,
    m_hbm,
    owner_hbm,
    tally_hbm,
    wall_hbm,
    face_hbm,
    f_out,
    g_out,
    s_out,
    f_in,
    g_in,
    s_in,
    m_in,
    owner_in,
    tally_in,
    wall_in,
    face_in,
    flow,
    heat,
    post_f,
    post_g,
    speeds,
    solid_k,
    solid_low_x,
    solid_high_x,
    solid_low_y,
    solid_high_y,
    columns,
    columns_low,
    columns_high,
    quick,
    got_quick,
    wall_mask,
    covered_ref,
    cell_ref,
    slot_key,
    early,
    got_early,
    late,
    got_late,
    third,
    got_third,
    mid,
    got_mid,
    answer_out,
    got_answer,
    i_sem,
    n_send,
    n_recv,
    g_send,
    g_recv,
):
    arrivals = []
    for n, (source, target) in enumerate(
        (
            (g_hbm, g_in),
            (f_hbm, f_in),
            (s_hbm, s_in),
            (m_hbm, m_in),
            (owner_hbm, owner_in),
            (tally_hbm, tally_in),
            (wall_hbm, wall_in),
            (face_hbm, face_in),
        )
    ):
        made = pltpu.make_async_copy(source, target, i_sem.at[n])
        made.start()
        arrivals.append(made)

    i, j = lax.axis_index("gx"), lax.axis_index("gy")
    right, left = lax.rem(i + 1, nx), lax.rem(i + nx - 1, nx)
    upper, lower = lax.rem(j + 1, ny), lax.rem(j + ny - 1, ny)
    barrier = pltpu.get_barrier_semaphore()
    for device in ((right, j), (left, j)):
        pl.semaphore_signal(barrier, inc=1, device_id=device, device_id_type=MESH)

    @pl.loop(1, ny)
    def _(o):
        pl.semaphore_signal(barrier, inc=1, device_id=(i, lax.rem(j + o, ny)), device_id_type=MESH)

    sent = []

    def copy(source, target, device, goes=None, comes=None):
        n = len(sent)
        made = pltpu.make_async_remote_copy(
            src_ref=source,
            dst_ref=target,
            send_sem=n_send.at[n],
            recv_sem=n_recv.at[n],
            device_id=device,
            device_id_type=MESH,
        )
        if goes is None:
            made.start()
        else:
            pl.when(goes)(made.start)
        sent.append((made, goes))
        return made, comes

    def settle(copies):
        for made, comes in copies:
            if comes is None:
                made.wait_recv()
            else:
                pl.when(comes)(made.wait_recv)

    def to_right(source, target):
        return copy(source, target, (right, j), i < nx - 1, i > 0)

    def to_left(source, target):
        return copy(source, target, (left, j), i > 0, i < nx - 1)

    def send_flow(t):
        return [
            copy(post_f.at[t, 4, pl.ds(0, 5)], post_f.at[t, 0, pl.ds(0, 5)], (right, j)),
            copy(post_f.at[t, 1, pl.ds(5, 5)], post_f.at[t, 5, pl.ds(5, 5)], (left, j)),
        ]

    def send_heat(t):
        return [
            copy(post_g.at[t, 4, 1], post_g.at[t, 0, 1], (right, j)),
            copy(post_g.at[t, 1, 2], post_g.at[t, 5, 2], (left, j)),
        ]

    def send_solid(r, lanes):
        return [
            to_right(solid_k.at[2 * r + 1, :, lanes], solid_low_x.at[r, :, lanes]),
            to_left(solid_k.at[2 * r, :, lanes], solid_high_x.at[r, :, lanes]),
        ]

    def to_all(source, target, pair, personal):
        @pl.loop(0, ny - 1)
        def _(s):
            pltpu.make_async_remote_copy(
                src_ref=source.at[s] if personal else source.at[0],
                dst_ref=target.at[ny - 2 - s],
                send_sem=g_send.at[pair],
                recv_sem=g_recv.at[pair],
                device_id=(i, lax.rem(j + 2 * ny - 1 - s, ny)),
                device_id_type=MESH,
            ).start()

        target[ny - 1] = source[ny - 1 if personal else 0]

    def from_all(target, pair):
        span = pl.ds(0, ny - 1)
        pltpu.make_async_copy(target.at[span], target.at[span], g_recv.at[pair]).wait()

    def all_sent(target, pair):
        span = pl.ds(0, ny - 1)
        pltpu.make_async_copy(target.at[span], target.at[span], g_send.at[pair]).wait()

    here, beyond, whole = pl.ds(0, 128), pl.ds(128, 128), pl.ds(0, 256)

    for n in (2, 3):
        arrivals[n].wait()
    for x in range(2):
        solid_k[x, :, here] = s_in[pl.ds(x, 8, stride=2), :]
        solid_k[6 + x, :, here] = 0.2 + 0.8 * m_in[pl.ds(x, 8, stride=2), :].astype(F32)
    solid_0 = [solid_k[x, :, here] for x in range(2)]
    k_here = [solid_k[6 + x, :, here] for x in range(2)]
    pl.semaphore_wait(barrier, ny - 1 + 2)
    solid_x_halo = send_solid(0, here) + send_solid(3, here)

    square = (128, 128)
    lane, sub = lane_of(square), sub_of(square)
    lane_8, sub_8 = lane_of((8, 128)), sub_of((8, 128))
    lane_32, sub_32 = lane_of((32, 128)), sub_of((32, 128))
    row_lane = lane_of((1, 128))
    diagonal = lane == sub

    def column(row):
        return jnp.sum(jnp.where(diagonal, jnp.broadcast_to(row, square), 0.0), axis=1, keepdims=True)

    def as_row(col):
        return jnp.sum(jnp.where(diagonal, jnp.broadcast_to(col, square), 0.0), axis=0, keepdims=True)

    for n in (4, 5, 6, 7):
        arrivals[n].wait()
    owner = owner_in[...]
    face_index = face_in[...]
    wall = wall_in[...]
    live = lane_of((1, 128)) < jnp.broadcast_to(tally_in[...], (1, 128))
    block = (j - owner - 1) & (ny - 1)
    cell_row = jnp.where(live, owner * 256 + face_index, -1).astype(F32)
    cell_col = column(cell_row)
    live_col = column(jnp.where(live, 1.0, 0.0))
    block_row = block.astype(F32)
    block_col = column(block_row)
    face_col = column(face_index.astype(F32))
    wall_y_col = column((wall & 127).astype(F32))
    wall_x_col = column((wall >> 7).astype(F32))
    rank_col = jnp.sum(
        jnp.where((jnp.broadcast_to(block_row, square) == block_col) & (lane < sub), 1.0, 0.0),
        axis=1,
        keepdims=True,
    )
    lane_f = lane.astype(F32)
    wall_hit = jnp.where(lane_f == wall_y_col, live_col, 0.0)
    for x in range(4):
        wall_mask[x] = jnp.where(wall_x_col == float(x), wall_hit, 0.0)
    slot_key[...] = jnp.where((lane & 7).astype(F32) == rank_col, jnp.broadcast_to(live_col, square), 0.0)
    to_owner = jnp.where(jnp.broadcast_to(block_row, (32, 128)) == sub_32.astype(F32), 1.0, 0.0)

    def at_wall(rows):
        total = wall_mask[0] * rows[0]
        for x in range(1, 4):
            total = total + wall_mask[x] * rows[x]
        return jnp.sum(total, axis=1, keepdims=True)

    def on_wall(col):
        return [jnp.sum(wall_mask[x] * col, axis=0, keepdims=True) for x in range(4)]

    def slots(first, second):
        fields = jnp.where(lane < 8, first, jnp.where(lane < 16, second, 0.0))
        return jnp.dot(
            to_owner, fields * slot_key[...], precision=lax.Precision.HIGHEST, preferred_element_type=F32
        )

    def fill(buffer, n, value):
        buffer[:, n, :] = jnp.broadcast_to(value, (32, 128))

    arrivals[0].wait()
    for q in range(7):
        for x in range(4):
            heat[q, x, :, here] = g_in[q, pl.ds(x, 8, stride=4), :]

    def wall_sums():
        total = heat[0, :, 0:1, here]
        for q in range(1, 7):
            total = total + heat[q, :, 0:1, here]
        return [total[x] for x in range(4)]

    t1_col = at_wall(wall_sums())
    fill(early, 0, cell_row)
    fill(early, 1, as_row(t1_col))
    early[:, 2, :] = slots(t1_col, face_col + 1.0)
    k_top = [k_here[x][7:8] for x in range(2)]
    k_inner = jnp.where(row_lane == 1, turn(k_top[1], 1, 1), turn(k_top[1], 127, 1))
    fill(early, 3, jnp.where((row_lane == 0) | (row_lane == 127), k_top[0], k_inner))
    for x in range(2):
        fill(early, 4 + x, solid_0[x][7:8])
    to_all(early, got_early, 0, True)

    arrivals[1].wait()
    for q in range(19):
        for x in range(4):
            flow[q, x, :, here] = f_in[q, pl.ds(x, 8, stride=4), :]
    named = on_wall(cell_col + 1.0)
    named_8 = jnp.zeros((8, 128), F32)
    for x in range(4):
        named_8 = jnp.where((sub_8 & 3) == x, named[x], named_8)
    units = [(flow, q, x) for q in range(19) for x in range(4)] + [(heat, q, x) for q in range(7) for x in range(4)]
    for tile in range(5):
        packed = jnp.zeros((8, 128), F32)
        for n in range(21):
            place = 21 * tile + n
            value = named_8
            if place < len(units):
                ref, q, x = units[place]
                value = ref[q, x, :, here]
            packed = jnp.where((lane_8 >= 6 * n) & (lane_8 < 6 * n + 6), turn(value, 6 * n + 3, 1), packed)
        columns[tile] = packed
    column_halo = [copy(columns, columns_low, (i, upper)), copy(columns, columns_high, (i, lower))]
    both = [solid_k.at[pl.ds(0, 2), :, here], solid_k.at[pl.ds(6, 2), :, here]]
    solid_y_halo = [
        made
        for n, part in enumerate(both)
        for made in (copy(part, solid_low_y.at[n], (i, upper)), copy(part, solid_high_y.at[n], (i, lower)))
    ]

    collide_flow(flow, post_f.at[0], speeds.at[0], here)
    collide_heat(heat, post_g.at[0], speeds.at[0], here)
    up = down = jnp.zeros((1, 128), F32)
    for x in range(4):
        up = jnp.where(row_lane == x, turn(post_g[0, x + 1, 3, 0:1, here], x + 1, 1), up)
        down = jnp.where(row_lane == x, turn(post_g[0, x + 1, 4, 0:1, here], x, 1), down)
    quick[0], quick[1] = up, down
    quick[2], quick[3] = post_g[0, 4, 1, 0:1, here], post_g[0, 1, 2, 0:1, here]
    quick_halo = [
        copy(quick.at[0], got_quick.at[0], (i, upper)),
        copy(quick.at[1], got_quick.at[1], (i, lower)),
        copy(quick.at[2], got_quick.at[2], (right, j)),
        copy(quick.at[3], got_quick.at[3], (left, j)),
    ]

    gates_x = (jnp.where(i == 0, 0.0, 1.0), jnp.where(i == nx - 1, 0.0, 1.0))
    gates_y = (jnp.where(j == 0, 0.0, 1.0), jnp.where(j == ny - 1, 0.0, 1.0))

    def conduct(field, r, k, span, y_gates):
        change = fluxes(
            field,
            k,
            jnp.where(i > 0, solid_low_x[r, :, span], field[0]),
            jnp.where(i > 0, solid_low_x[3, :, span], k[0]),
            jnp.where(i < nx - 1, solid_high_x[r, :, span], field[1]),
            jnp.where(i < nx - 1, solid_high_x[3, :, span], k[1]),
            gates_x + y_gates,
        )
        return [field[x] + DT * change[x] for x in range(2)]

    settle(solid_x_halo)
    inner_1 = conduct(solid_0, 0, k_here, here, (0.0, 0.0))
    for x in range(2):
        late[0, x : x + 1, :] = inner_1[x][7:8]
    to_all(late, got_late, 1, False)

    for x in range(4):
        covered_ref[x, :, here] = jnp.broadcast_to(jnp.sum(wall_mask[x], axis=0, keepdims=True), (8, 128))
    settle(quick_halo)
    rest_rows = []
    for x in range(4):
        post = lambda q, at=x: post_g[0, at + 1, q, 0:1, here]
        total = post(0) + (post_g[0, x, 1, 0:1, here] if x else got_quick[2])
        total = total + (post_g[0, x + 2, 2, 0:1, here] if x < 3 else got_quick[3])
        total = total + jnp.where(row_lane == 0, turn(got_quick[0], 128 - x, 1), turn(post(3), 1, 1))
        total = total + jnp.where(row_lane == 127, turn(got_quick[1], 127 - x, 1), turn(post(4), 127, 1))
        wall_post = post(6)
        total = total + jnp.where(covered_ref[x, 0:1, here] > 0.5, -wall_post, wall_post)
        rest_rows.append(total + post_g[0, x + 1, 6, 1:2, here])
    a2_col = at_wall(rest_rows)
    third[:, 0, :] = slots(a2_col, 0.0)
    fill(third, 1, as_row(a2_col))
    to_all(third, got_third, 2, True)

    settle(solid_y_halo)
    for x in range(2):
        for n, at in ((0, 0), (1, 6)):
            solid_k[at + x, :, beyond] = jnp.where(lane_8 < 64, solid_high_y[n, x], solid_low_y[n, x])
    solid_x_halo = send_solid(0, beyond) + send_solid(3, beyond)
    settle(column_halo)
    named_beyond = None
    for tile in range(5):
        low, high = columns_low[tile], columns_high[tile]
        for n in range(21):
            place = 21 * tile + n
            value = jnp.where(lane_8 < 64, turn(high, 125 - 6 * n, 1), turn(low, 125 - 6 * n, 1))
            if place < len(units):
                ref, q, x = units[place]
                ref[q, x, :, beyond] = value
            else:
                named_beyond = value
    collide_flow(flow, post_f.at[0], speeds.at[0], beyond)
    collide_heat(heat, post_g.at[0], speeds.at[0], beyond)
    heat_halo = send_heat(0)
    flow_halo = send_flow(0)
    for x in range(4):
        covered_ref[x, :, beyond] = jnp.where(jnp.broadcast_to(named_beyond[x : x + 1], (8, 128)) > 0.5, 1.0, 0.0)
    halo_lanes = (126, 127, 0, 1)
    halo_cells = [
        jnp.sum(
            jnp.where(lane_8 == jnp.where(sub_8 < 4, halo_lanes[n], halo_lanes[n + 1]), named_beyond, 0.0),
            axis=1,
            keepdims=True,
        )
        - 1.0
        for n in (0, 2)
    ]
    rows_col = jnp.concatenate([cell_col] + halo_cells, axis=0)
    cell_ref[...] = jnp.broadcast_to(rows_col, (144, 128))
    rows_cell = cell_ref[...].astype(jnp.int32)
    lane_144 = lane_of((144, 128))
    face_hit = jnp.where(lane_144 == (rows_cell & 127), 1.0, 0.0)
    rows_place = ((j - (rows_cell >> 8) - 1) & 31) + 32 * ((rows_cell >> 7) & 1)
    pick = jnp.where(lane_144 == rows_place, 1.0, 0.0)[:, 0:64]

    def put_heat(q, value):
        heat[q] = value

    def put_flow(q, value):
        flow[q] = value

    settle(heat_halo)
    stream(post_g.at[0], HEAT_PLACES, covered_ref[...], put_heat)
    settle(flow_halo)
    stream(post_f.at[0], FLOW_PLACES, None, put_flow)
    collide_flow(flow, post_f.at[1], speeds.at[1], whole)
    flow_halo = send_flow(1)

    settle(solid_x_halo)
    k = [solid_k[6 + x] for x in range(2)]
    field_0 = [solid_k[x] for x in range(2)]
    p1 = conduct(field_0, 0, k, whole, gates_y)

    from_all(got_early, 0)

    def slot_columns(value, field):
        return [
            jnp.broadcast_to(
                jnp.sum(jnp.where(lane_32 == 8 * field + c, value, 0.0), axis=1, keepdims=True), (32, 128)
            )
            for c in range(CAP)
        ]

    faces = slot_columns(got_early[:, 2, :], 1)

    def own_sums(fields):
        result = []
        for x in range(2):
            place = (lane_32 + (128 * x + 1)).astype(F32)
            totals = [jnp.zeros((32, 128), F32) for _ in fields]
            for c in range(CAP):
                hit = faces[c] == place
                for n, field in enumerate(fields):
                    totals[n] = totals[n] + jnp.where(hit, 1.0 if field is None else field[c], 0.0)
            result.append([jnp.sum(total, axis=0, keepdims=True) for total in totals])
        return result

    def halo_sums(fields):
        cells = got_early[:, 0, :]
        result = []
        for x in range(2):
            rows = [jnp.zeros((1, 128), F32) for _ in fields]
            for at in halo_lanes:
                there = (j + (1 if at < 64 else -1)) * 256 + 128 * x + at
                hit = cells == jnp.full((32, 128), there, jnp.int32).astype(F32)
                for n, field in enumerate(fields):
                    total = jnp.sum(jnp.where(hit, 1.0 if field is None else field, 0.0), axis=0, keepdims=True)
                    total = jnp.sum(total, axis=1, keepdims=True)
                    rows[n] = jnp.where(row_lane == at, total, rows[n])
            result.append(rows)
        return result

    def joined(own, halo):
        return [
            [jnp.concatenate([a, b], axis=1) for a, b in zip(own[x], halo[x])] for x in range(2)
        ]

    top_256 = sub_of((8, 256)) == 7

    def on_top(value, row):
        return value + jnp.where(top_256, jnp.broadcast_to(row, (8, 256)), 0.0)

    sums = joined(
        own_sums([slot_columns(got_early[:, 2, :], 0), None]), halo_sums([got_early[:, 1, :], None])
    )
    many = [sums[x][1] for x in range(2)]
    solid_1 = [on_top(p1[x], DT * (sums[x][0] - many[x] * field_0[x][7:8])) for x in range(2)]
    for x in range(2):
        solid_k[2 + x] = solid_1[x]
    solid_halo = send_solid(1, whole)

    def same_cell(ref, n, count, many_rows):
        cells = cell_ref[0:many_rows]

        def body(b, carry):
            hit = cells == got_early[b, 0:1, :]
            total = carry[0] + jnp.where(hit, ref[b, n : n + 1, :], 0.0)
            if count:
                return total, carry[1] + jnp.where(hit, 1.0, 0.0)
            return (total,)

        zero = jnp.zeros((many_rows, 128), F32)
        return lax.fori_loop(0, ny, body, (zero, zero) if count else (zero,))

    total_1, number = same_cell(got_early, 1, True, 144)
    number_col = jnp.sum(number, axis=1, keepdims=True)
    edge_k = got_early[:, 3, :]
    crossing = []
    for x in range(2):
        inside = got_early[:, 4 + x, :]
        inside_k = edge_k if x == 0 else jnp.where(lane_32 == 0, turn(edge_k, 127, 1), turn(edge_k, 1, 1))
        outside, outside_k = (turn(turn(part, 1, 0), 127, 1) for part in (inside, inside_k))
        c, cb = conduct_of(inside, inside_k), conduct_of(outside, outside_k)
        rise = 2.0 * c * cb / (c + cb) * (outside - inside)
        rise = jnp.where((lane_32 == 127) & (sub_32 != j), rise, 0.0)
        crossing.append(DT * (rise - turn(turn(rise, 31, 0), 1, 1)))

    from_all(got_late, 1)
    surfaces = jnp.concatenate(
        [
            jnp.concatenate([got_late[:, x, :] + crossing[x] for x in range(2)], axis=0),
            jnp.concatenate([got_early[:, 4 + x, :] for x in range(2)], axis=0),
        ],
        axis=1,
    )
    picked = jnp.dot(pick, surfaces, precision=lax.Precision.HIGHEST, preferred_element_type=F32)
    w1_col = jnp.sum(
        face_hit * (picked[:, 0:128] - DT * number_col * picked[:, 128:256]) + DT * total_1,
        axis=1,
        keepdims=True,
    )

    def warm_wall(col):
        rows = on_wall(col[0:128])
        for x in range(4):
            outer = jnp.zeros((1, 128), F32)
            for n, at in enumerate(halo_lanes):
                outer = jnp.where(row_lane == at, col[128 + 4 * n + x : 129 + 4 * n + x], outer)
            outer = jnp.where(covered_ref[x, 0:1, beyond] > 0.5, outer, 0.0)
            heat[5, x, 0:1, here] = heat[5, x, 0:1, here] + 0.25 * rows[x]
            heat[5, x, 0:1, beyond] = heat[5, x, 0:1, beyond] + 0.25 * outer

    warm_wall(w1_col)
    collide_heat(heat, post_g.at[1], speeds.at[1], whole)
    heat_halo = send_heat(1)

    from_all(got_third, 2)
    rest = joined(own_sums([slot_columns(got_third[:, 0, :], 0)]), halo_sums([got_third[:, 1, :]]))
    settle(solid_halo)
    solid_2 = conduct(solid_1, 1, k, whole, gates_y)
    solid_2 = [
        on_top(solid_2[x], DT * (rest[x][0] - 0.75 * many[x] * solid_1[x][7:8])) for x in range(2)
    ]
    for x in range(2):
        solid_k[4 + x] = solid_2[x]
        fill(mid, 2 + x, solid_2[x][7:8, 0:128])
    solid_halo = send_solid(2, whole)

    settle(heat_halo)
    stream(post_g.at[1], HEAT_PLACES, covered_ref[...], put_heat)
    a3_col = at_wall(wall_sums())
    fill(mid, 0, as_row(a3_col))
    mid[:, 1, :] = slots(a3_col, 0.0)
    to_all(mid, got_mid, 3, True)

    settle(solid_halo)
    p3 = conduct(solid_2, 2, k, whole, gates_y)
    p3 = [on_top(p3[x], (-0.75 * DT) * many[x] * solid_2[x][7:8])[:, 0:128] for x in range(2)]
    answer = jnp.zeros((32, 128), F32)
    for c in range(CAP):
        first = faces[c] == (lane_32 + 1).astype(F32)
        second = faces[c] == (lane_32 + 129).astype(F32)
        at_cell = jnp.where(first, p3[0][7:8], jnp.where(second, p3[1][7:8], 0.0))
        answer = jnp.where(lane_32 == c, jnp.sum(at_cell, axis=1, keepdims=True), answer)
    answer_out[:, 0, :] = answer
    to_all(answer_out, got_answer, 4, True)

    settle(flow_halo)
    stream(post_f.at[1], FLOW_PLACES, None, put_flow)
    collide_flow(flow, post_f.at[2], speeds.at[2], whole)
    flow_halo = send_flow(2)

    from_all(got_mid, 3)
    surfaces = jnp.concatenate([got_mid[:, 2 + x, :] for x in range(2)], axis=0)
    picked = jnp.dot(pick, surfaces, precision=lax.Precision.HIGHEST, preferred_element_type=F32)
    w2_col = jnp.sum(face_hit * picked, axis=1, keepdims=True)
    warm_wall(w2_col)
    collide_heat(heat, post_g.at[2], speeds.at[2], whole)
    heat_halo = send_heat(2)

    (total_3,) = same_cell(got_mid, 0, False, 128)
    last = own_sums([slot_columns(got_mid[:, 1, :], 0)])
    for x in range(2):
        s_out[pl.ds(x, 8, stride=2), :] = p3[x] + jnp.where(sub_8 == 7, DT * last[x][0], 0.0)

    settle(flow_halo)

    def write_flow(q, value):
        for x in range(4):
            f_out[q, pl.ds(x, 8, stride=4), :] = value[x, :, 0:128]

    stream(post_f.at[2], FLOW_PLACES, None, write_flow)

    from_all(got_answer, 4)
    pick_owner = jnp.where(lane_of((128, 32)).astype(F32) == block_col, 1.0, 0.0)
    found = jnp.dot(pick_owner, got_answer[:, 0, :], precision=lax.Precision.HIGHEST, preferred_element_type=F32)
    w3_col = jnp.sum(jnp.where(lane_f == rank_col, found, 0.0) + DT * total_3, axis=1, keepdims=True)
    w3_rows = on_wall(w3_col)

    settle(heat_halo)

    def write_heat(q, value):
        for x in range(4):
            row = value[x, :, 0:128]
            if q == 5:
                row = row + jnp.where(sub_8 == 0, 0.25 * w3_rows[x], 0.0)
            g_out[q, pl.ds(x, 8, stride=4), :] = row

    stream(post_g.at[2], HEAT_PLACES, covered_ref[...], write_heat)

    for n, target in enumerate((got_early, got_late, got_third, got_mid, got_answer)):
        all_sent(target, n)
    for made, goes in sent:
        if goes is None:
            made.wait_send()
        else:
            pl.when(goes)(made.wait_send)


def finish(*refs):
    sources, targets, sems = refs[0:3], refs[3:6], refs[6]
    copies = [pltpu.make_async_copy(a, b, sems.at[n]) for n, (a, b) in enumerate(zip(sources, targets))]
    for made in copies:
        made.start()
    for made in copies:
        made.wait()


def on_device(nx, ny, flow, heat, solid, metal, owner, tally, wall, face):
    vmem = functools.partial(pltpu.VMEM, dtype=F32)
    tile, wide = (8, 128), (8, 256)
    copies = 40
    results = (
        jax.ShapeDtypeStruct((19, 32, 128), F32),
        jax.ShapeDtypeStruct((7, 32, 128), F32),
        jax.ShapeDtypeStruct((16, 128), F32),
    )
    out = pl.pallas_call(
        functools.partial(kernel, nx, ny),
        out_shape=tuple(pltpu.VMEM(result.shape, result.dtype) for result in results),
        in_specs=[pl.BlockSpec(memory_space=pltpu.HBM)] * 8,
        out_specs=[pl.BlockSpec(memory_space=pltpu.VMEM)] * 3,
        scratch_shapes=[
            vmem((19, 32, 128)),
            vmem((7, 32, 128)),
            vmem((16, 128)),
            pltpu.VMEM((16, 128), jnp.int32),
            pltpu.VMEM((1, 128), jnp.int32),
            pltpu.VMEM((1, 1), jnp.int32),
            pltpu.VMEM((1, 128), jnp.int32),
            pltpu.VMEM((1, 128), jnp.int32),
            vmem((19, 4) + wide),
            vmem((7, 4) + wide),
            vmem((STEPS, 6, 19) + wide),
            vmem((STEPS, 6, 7) + wide),
            vmem((STEPS, 3, 4) + wide),
            vmem((8,) + wide),
            vmem((4,) + wide),
            vmem((4,) + wide),
            vmem((2, 2) + tile),
            vmem((2, 2) + tile),
            vmem((5,) + tile),
            vmem((5,) + tile),
            vmem((5,) + tile),
            vmem((4, 1, 128)),
            vmem((4, 1, 128)),
            vmem((4, 128, 128)),
            vmem((4,) + wide),
            vmem((144, 128)),
            vmem((128, 128)),
            vmem((32, 6, 128)),
            vmem((32, 6, 128)),
            vmem((1, 2, 128)),
            vmem((32, 2, 128)),
            vmem((32, 2, 128)),
            vmem((32, 2, 128)),
            vmem((32, 4, 128)),
            vmem((32, 4, 128)),
            vmem((32, 1, 128)),
            vmem((32, 1, 128)),
            pltpu.SemaphoreType.DMA((8,)),
            pltpu.SemaphoreType.DMA((copies,)),
            pltpu.SemaphoreType.DMA((copies,)),
            pltpu.SemaphoreType.DMA((5,)),
            pltpu.SemaphoreType.DMA((5,)),
        ],
        compiler_params=pltpu.CompilerParams(
            collective_id=0, has_side_effects=True, vmem_limit_bytes=ROOM
        ),
        name="coupled_steps",
    )(
        flow.reshape(19, 32, 128),
        heat.reshape(7, 32, 128),
        solid.reshape(16, 128),
        metal.reshape(16, 128),
        owner.reshape(1, 128),
        tally,
        wall,
        face,
    )
    out = pl.pallas_call(
        finish,
        out_shape=results,
        in_specs=[pl.BlockSpec(memory_space=pltpu.VMEM)] * 3,
        out_specs=[pl.BlockSpec(memory_space=pltpu.HBM)] * 3,
        scratch_shapes=[pltpu.SemaphoreType.DMA((3,))],
        compiler_params=pltpu.CompilerParams(vmem_limit_bytes=1024 * 1024),
        name="write_out",
    )(*out)
    return out[0].reshape(19, 8, 4, 128), out[1].reshape(7, 8, 4, 128), out[2].reshape(8, 2, 128)


def solution(mesh):
    placed = (
        P(None, None, "gx", "gy"),
        P(None, None, "gx", "gy"),
        P(None, "gx", "gy"),
        P(None, "gx", "gy"),
        P("gx", "gy", None),
        P("gx", "gy"),
        P("gx", "gy"),
        P("gx", "gy"),
    )
    return jax.shard_map(
        functools.partial(on_device, mesh.shape["gx"], mesh.shape["gy"]),
        mesh=mesh,
        in_specs=placed,
        out_specs=(P(None, None, "gx", "gy"), P(None, None, "gx", "gy"), P(None, "gx", "gy")),
        check_vma=False,
    )
```

time: 57.6 us -> 53 us (0.920)
  Pallas kernels: 54.2 us -> 51.6 us
  local copies, waits for them, and re-layouts: 1.94 us -> 0 us
    unnamed x6 -> x0, local copies, waits for them, and re-layouts: 1.94 us -> none
    pallas_call x1, Pallas kernels: 52.4 us -> 50.8 us  [on_device(): pl.pallas_call(functools.partial(kernel, nx, ny), out_shape=tuple((pltpu....]
    pallas_call x1, Pallas kernels: 1.81 us -> 0.78 us  [on_device(): pl.pallas_call(finish, out_shape=results, in_specs=[pl.BlockSpec(memory_s...]
where the time goes in v2:
time: 53 us; the launch traced here: 52.8 us
  Pallas kernels  51.6 us (97%)
  between operations  1.29 us (2%)
    pallas_call x1, Pallas kernels, on_device(): pl.pallas_call(functools.partial(kernel, nx, ny), out_shape=tuple((pltpu....  50.8 us

profile of v2, /device:TPU:1, one launch (start us, length us, event | category | flops | bytes accessed | tf_op | source)
XLA Modules:
  0.0 52.8 jit_solution(15815940074015650490)
XLA Ops:
  1.3 50.8 %coupled_steps.1 = (f32[19,32,128]{2,1,0:T(8,128)S(1)}, f32[7,32,128]{2,1,0:T(8,128)S(1)}, f32[16,128]{1,0:T(8,128)S(1)}) custom-call(f32[19,32,128]{2,1,0:T(8,128)} %bitcast.8, f32[7,32,128]{2,1,0:T(8,128)} %bitcast.9, f32[16,128]{1,0:T(8,128)} %bitcast.10, s32[16,128]{1,0:T(8,128)} %bitcast.11, s32[1,128]{1,0:T(1,128)} %bitcast.12, ...), custom_call_target="tpu_custom_call" | custom-call | tf_op jit(solution)/shard_map/coupled_steps/pallas_call | solution.py:766
  52.1 0.8 %write_out.1 = (f32[19,32,128]{2,1,0:T(8,128)}, f32[7,32,128]{2,1,0:T(8,128)}, f32[16,128]{1,0:T(8,128)}) custom-call(f32[19,32,128]{2,1,0:T(8,128)S(1)} %get-tuple-element.9.refs_0_, f32[7,32,128]{2,1,0:T(8,128)S(1)} %get-tuple-element.10.refs_1_, f32[16,128]{1,0:T(8,128)S(1)} %get-tuple-element.11.refs_2_), custom_call_target="tpu_custom_call" | custom-call | tf_op jit(solution)/shard_map/write_out/pallas_call | solution.py:829

commit v3 on v2

--- a/solution.py
+++ b/solution.py
@@ -89,18 +89,32 @@
         post[1:5, PLACE[p], :, span] = scale * (even - odd) - 0.25 * state[p, :, :, span]
 
 
-def collide_heat(state, post, velocity, span):
+def collide_heat(state, post, velocity, span, x_done=None):
     keep = 1.0 - 1.0 / 0.7
     warmth = state[0, :, :, span]
     for q in range(1, 7):
         warmth = warmth + state[q, :, :, span]
-    post[1:5, 0, :, span] = keep * state[0, :, :, span] + (0.25 / 0.7) * warmth
     part = (0.125 / 0.7) * warmth
     for axis in range(3):
         tilt = part * (4.0 * velocity[axis, :, :, span])
         for q in (1 + 2 * axis, 2 + 2 * axis):
             sign = tilt if q == 1 + 2 * axis else -tilt
             post[1:5, q, :, span] = keep * state[q, :, :, span] + (part + sign)
+        if axis == 0 and x_done is not None:
+            x_done()
+    post[1:5, 0, :, span] = keep * state[0, :, :, span] + (0.25 / 0.7) * warmth
+
+
+def pick_rows(pick, value):
+    parts, rest = [], value
+    for _ in range(3):
+        parts.append(rest.astype(jnp.bfloat16))
+        rest = rest - parts[-1].astype(F32)
+    found = jnp.dot(
+        pick.astype(jnp.bfloat16), jnp.concatenate(parts, axis=1), preferred_element_type=F32
+    )
+    width = value.shape[1]
+    return found[:, 0:width] + (found[:, width : 2 * width] + found[:, 2 * width :])
 
 
 def lifted(value, cz, bounce):
@@ -202,10 +216,13 @@
     cell_ref,
     slot_key,
     early,
+    near_early,
     got_early,
     late,
+    near_late,
     got_late,
     third,
+    near_third,
     got_third,
     mid,
     got_mid,
@@ -237,13 +254,19 @@
     i, j = lax.axis_index("gx"), lax.axis_index("gy")
     right, left = lax.rem(i + 1, nx), lax.rem(i + nx - 1, nx)
     upper, lower = lax.rem(j + 1, ny), lax.rem(j + ny - 1, ny)
+    along = ny // 4
+    y = lax.rem(j // 2, along)
+    corner = j // (2 * along) * 2 + lax.rem(j, 2)
+
+    def seat(corner_there, y_there):
+        return corner_there // 2 * (2 * along) + 2 * y_there + lax.rem(corner_there, 2)
+
     barrier = pltpu.get_barrier_semaphore()
-    for device in ((right, j), (left, j)):
+    greeted = [(i, seat(lax.rem(corner + d, 4), y)) for d in (2, 3, 1)]
+    greeted += [(i, seat(corner, lax.rem(y + d, along))) for d in (4, 3, 5, 2, 6, 1, 7)]
+    greeted += [(right, j), (left, j), (i, upper), (i, lower)]
+    for device in greeted:
         pl.semaphore_signal(barrier, inc=1, device_id=device, device_id_type=MESH)
-
-    @pl.loop(1, ny)
-    def _(o):
-        pl.semaphore_signal(barrier, inc=1, device_id=(i, lax.rem(j + o, ny)), device_id_type=MESH)
 
     sent = []
 
@@ -295,26 +318,56 @@
             to_left(solid_k.at[2 * r, :, lanes], solid_high_x.at[r, :, lanes]),
         ]
 
-    def to_all(source, target, pair, personal):
-        @pl.loop(0, ny - 1)
-        def _(s):
+    def round_first(source, near, pair, personal):
+        for d in (2, 3, 1):
+            there = lax.rem(corner + d, 4)
             pltpu.make_async_remote_copy(
-                src_ref=source.at[s] if personal else source.at[0],
-                dst_ref=target.at[ny - 2 - s],
+                src_ref=source.at[there] if personal else source.at[0],
+                dst_ref=near.at[corner],
                 send_sem=g_send.at[pair],
                 recv_sem=g_recv.at[pair],
-                device_id=(i, lax.rem(j + 2 * ny - 1 - s, ny)),
+                device_id=(i, seat(there, y)),
                 device_id_type=MESH,
             ).start()
-
-        target[ny - 1] = source[ny - 1 if personal else 0]
-
-    def from_all(target, pair):
-        span = pl.ds(0, ny - 1)
+        near[corner] = source[corner] if personal else source[0]
+
+    def round_second(near, target, pair):
+        got_bytes(target, 3, pair)
+        for d in (4, 3, 5, 2, 6, 1, 7):
+            for half in range(2):
+                pltpu.make_async_remote_copy(
+                    src_ref=near.at[pl.ds(2 * half, 2)],
+                    dst_ref=target.at[pl.ds(2 * along * half + 2 * y, 2)],
+                    send_sem=g_send.at[pair + 1],
+                    recv_sem=g_recv.at[pair + 1],
+                    device_id=(i, seat(corner, lax.rem(y + d, along))),
+                    device_id_type=MESH,
+                ).start()
+        for half in range(2):
+            for c in range(2):
+                target[2 * along * half + 2 * y + c] = near[2 * half + c]
+
+    def to_all(source, target, pair):
+        @pl.loop(0, ny - 1)
+        def _(o):
+            there = lax.rem(j + 1 + lax.rem(o + ny // 2 - 1, ny - 1), ny)
+            pltpu.make_async_remote_copy(
+                src_ref=source.at[there],
+                dst_ref=target.at[j],
+                send_sem=g_send.at[pair],
+                recv_sem=g_recv.at[pair],
+                device_id=(i, there),
+                device_id_type=MESH,
+            ).start()
+
+        target[j] = source[j]
+
+    def got_bytes(target, blocks, pair):
+        span = pl.ds(0, blocks)
         pltpu.make_async_copy(target.at[span], target.at[span], g_recv.at[pair]).wait()
 
-    def all_sent(target, pair):
-        span = pl.ds(0, ny - 1)
+    def sent_bytes(target, blocks, pair):
+        span = pl.ds(0, blocks)
         pltpu.make_async_copy(target.at[span], target.at[span], g_send.at[pair]).wait()
 
     here, beyond, whole = pl.ds(0, 128), pl.ds(128, 128), pl.ds(0, 256)
@@ -326,18 +379,41 @@
         solid_k[6 + x, :, here] = 0.2 + 0.8 * m_in[pl.ds(x, 8, stride=2), :].astype(F32)
     solid_0 = [solid_k[x, :, here] for x in range(2)]
     k_here = [solid_k[6 + x, :, here] for x in range(2)]
-    pl.semaphore_wait(barrier, ny - 1 + 2)
+    pl.semaphore_wait(barrier, len(greeted))
     solid_x_halo = send_solid(0, here) + send_solid(3, here)
+
+    lane_8, sub_8 = lane_of((8, 128)), sub_of((8, 128))
+    arrivals[0].wait()
+    for q in range(7):
+        for x in range(4):
+            heat[q, x, :, here] = g_in[q, pl.ds(x, 8, stride=4), :]
+    arrivals[1].wait()
+    for q in range(19):
+        for x in range(4):
+            flow[q, x, :, here] = f_in[q, pl.ds(x, 8, stride=4), :]
+    units = [(flow, q, x) for q in range(19) for x in range(4)] + [(heat, q, x) for q in range(7) for x in range(4)]
+    for tile in range(5):
+        packed = jnp.zeros((8, 128), F32)
+        for n, (ref, q, x) in enumerate(units[21 * tile : 21 * tile + 21]):
+            inside = (lane_8 >= 6 * n) & (lane_8 < 6 * n + 6)
+            packed = jnp.where(inside, turn(ref[q, x, :, here], 6 * n + 3, 1), packed)
+        columns[tile] = packed
+    column_halo = [
+        copy(columns.at[pl.ds(0, 5)], columns_low.at[pl.ds(0, 5)], (i, upper)),
+        copy(columns.at[pl.ds(0, 5)], columns_high.at[pl.ds(0, 5)], (i, lower)),
+    ]
+    both = [solid_k.at[pl.ds(0, 2), :, here], solid_k.at[pl.ds(6, 2), :, here]]
+    solid_y_halo = [
+        made
+        for n, part in enumerate(both)
+        for made in (copy(part, solid_low_y.at[n], (i, upper)), copy(part, solid_high_y.at[n], (i, lower)))
+    ]
 
     square = (128, 128)
     lane, sub = lane_of(square), sub_of(square)
-    lane_8, sub_8 = lane_of((8, 128)), sub_of((8, 128))
     lane_32, sub_32 = lane_of((32, 128)), sub_of((32, 128))
     row_lane = lane_of((1, 128))
     diagonal = lane == sub
-
-    def column(row):
-        return jnp.sum(jnp.where(diagonal, jnp.broadcast_to(row, square), 0.0), axis=1, keepdims=True)
 
     def as_row(col):
         return jnp.sum(jnp.where(diagonal, jnp.broadcast_to(col, square), 0.0), axis=0, keepdims=True)
@@ -348,17 +424,27 @@
     face_index = face_in[...]
     wall = wall_in[...]
     live = lane_of((1, 128)) < jnp.broadcast_to(tally_in[...], (1, 128))
-    block = (j - owner - 1) & (ny - 1)
+    owner_y = (owner >> 1) & (along - 1)
+    owner_corner = ((owner >> 1) // along) * 2 + (owner & 1)
     cell_row = jnp.where(live, owner * 256 + face_index, -1).astype(F32)
-    cell_col = column(cell_row)
-    live_col = column(jnp.where(live, 1.0, 0.0))
-    block_row = block.astype(F32)
-    block_col = column(block_row)
-    face_col = column(face_index.astype(F32))
-    wall_y_col = column((wall & 127).astype(F32))
-    wall_x_col = column((wall >> 7).astype(F32))
+    small = [owner, owner_y, face_index >> 7, face_index & 127, wall >> 7, wall & 127]
+    rows_8 = jnp.zeros((8, 128), F32)
+    for n, row in enumerate([value.astype(F32) for value in small] + [jnp.where(live, 1.0, 0.0)]):
+        rows_8 = jnp.where(sub_8 == n, row, rows_8)
+    turned = lax.dot_general(
+        jnp.where(diagonal, 1.0, 0.0).astype(jnp.bfloat16),
+        rows_8.astype(jnp.bfloat16),
+        (((1,), (1,)), ((), ())),
+        preferred_element_type=F32,
+    )
+    owner_col, owner_y_col, face_x_col, face_y_col, wall_x_col, wall_y_col, live_col = (
+        jnp.sum(jnp.where(lane_of((128, 8)) == n, turned, 0.0), axis=1, keepdims=True) for n in range(7)
+    )
+    owner_row = owner.astype(F32)
+    face_col = 128.0 * face_x_col + face_y_col
+    cell_col = jnp.where(live_col > 0.5, 256.0 * owner_col + face_col, -1.0)
     rank_col = jnp.sum(
-        jnp.where((jnp.broadcast_to(block_row, square) == block_col) & (lane < sub), 1.0, 0.0),
+        jnp.where((jnp.broadcast_to(owner_row, square) == owner_col) & (lane < sub), 1.0, 0.0),
         axis=1,
         keepdims=True,
     )
@@ -366,8 +452,12 @@
     wall_hit = jnp.where(lane_f == wall_y_col, live_col, 0.0)
     for x in range(4):
         wall_mask[x] = jnp.where(wall_x_col == float(x), wall_hit, 0.0)
-    slot_key[...] = jnp.where((lane & 7).astype(F32) == rank_col, jnp.broadcast_to(live_col, square), 0.0)
-    to_owner = jnp.where(jnp.broadcast_to(block_row, (32, 128)) == sub_32.astype(F32), 1.0, 0.0)
+    slot_key[...] = jnp.where(
+        ((lane >> 4).astype(F32) == owner_y_col) & ((lane & 7).astype(F32) == rank_col),
+        jnp.broadcast_to(live_col, square),
+        0.0,
+    )
+    to_corner = jnp.where(jnp.broadcast_to(owner_corner, (8, 128)) == sub_8, 1.0, 0.0)
 
     def at_wall(rows):
         total = wall_mask[0] * rows[0]
@@ -378,64 +468,38 @@
     def on_wall(col):
         return [jnp.sum(wall_mask[x] * col, axis=0, keepdims=True) for x in range(4)]
 
-    def slots(first, second):
-        fields = jnp.where(lane < 8, first, jnp.where(lane < 16, second, 0.0))
-        return jnp.dot(
-            to_owner, fields * slot_key[...], precision=lax.Precision.HIGHEST, preferred_element_type=F32
-        )
+    def slots(buffer, n, first, second):
+        fields = jnp.where((lane & 8) == 0, first, second)
+        value = pick_rows(to_corner, fields * slot_key[...])
+        for there in range(4):
+            buffer[there, n : n + 1, :] = value[there : there + 1]
 
     def fill(buffer, n, value):
-        buffer[:, n, :] = jnp.broadcast_to(value, (32, 128))
-
-    arrivals[0].wait()
-    for q in range(7):
-        for x in range(4):
-            heat[q, x, :, here] = g_in[q, pl.ds(x, 8, stride=4), :]
-
-    def wall_sums():
-        total = heat[0, :, 0:1, here]
-        for q in range(1, 7):
-            total = total + heat[q, :, 0:1, here]
-        return [total[x] for x in range(4)]
-
-    t1_col = at_wall(wall_sums())
+        buffer[:, n, :] = jnp.broadcast_to(value, (buffer.shape[0], 128))
+
+    warmth = heat[0, :, 0:1, here]
+    for q in range(1, 7):
+        warmth = warmth + heat[q, :, 0:1, here]
+    t1_col = at_wall([warmth[x] for x in range(4)])
     fill(early, 0, cell_row)
     fill(early, 1, as_row(t1_col))
-    early[:, 2, :] = slots(t1_col, face_col + 1.0)
+    slots(early, 2, t1_col, face_col + 1.0)
     k_top = [k_here[x][7:8] for x in range(2)]
     k_inner = jnp.where(row_lane == 1, turn(k_top[1], 1, 1), turn(k_top[1], 127, 1))
     fill(early, 3, jnp.where((row_lane == 0) | (row_lane == 127), k_top[0], k_inner))
     for x in range(2):
         fill(early, 4 + x, solid_0[x][7:8])
-    to_all(early, got_early, 0, True)
-
-    arrivals[1].wait()
-    for q in range(19):
-        for x in range(4):
-            flow[q, x, :, here] = f_in[q, pl.ds(x, 8, stride=4), :]
+    round_first(early, near_early, 0, True)
+
     named = on_wall(cell_col + 1.0)
     named_8 = jnp.zeros((8, 128), F32)
     for x in range(4):
         named_8 = jnp.where((sub_8 & 3) == x, named[x], named_8)
-    units = [(flow, q, x) for q in range(19) for x in range(4)] + [(heat, q, x) for q in range(7) for x in range(4)]
-    for tile in range(5):
-        packed = jnp.zeros((8, 128), F32)
-        for n in range(21):
-            place = 21 * tile + n
-            value = named_8
-            if place < len(units):
-                ref, q, x = units[place]
-                value = ref[q, x, :, here]
-            packed = jnp.where((lane_8 >= 6 * n) & (lane_8 < 6 * n + 6), turn(value, 6 * n + 3, 1), packed)
-        columns[tile] = packed
-    column_halo = [copy(columns, columns_low, (i, upper)), copy(columns, columns_high, (i, lower))]
-    both = [solid_k.at[pl.ds(0, 2), :, here], solid_k.at[pl.ds(6, 2), :, here]]
-    solid_y_halo = [
-        made
-        for n, part in enumerate(both)
-        for made in (copy(part, solid_low_y.at[n], (i, upper)), copy(part, solid_high_y.at[n], (i, lower)))
+    columns[5] = named_8
+    column_halo += [
+        copy(columns.at[5], columns_low.at[5], (i, upper)),
+        copy(columns.at[5], columns_high.at[5], (i, lower)),
     ]
-
     collide_flow(flow, post_f.at[0], speeds.at[0], here)
     collide_heat(heat, post_g.at[0], speeds.at[0], here)
     up = down = jnp.zeros((1, 128), F32)
@@ -470,10 +534,28 @@
     inner_1 = conduct(solid_0, 0, k_here, here, (0.0, 0.0))
     for x in range(2):
         late[0, x : x + 1, :] = inner_1[x][7:8]
-    to_all(late, got_late, 1, False)
+    round_first(late, near_late, 2, False)
 
     for x in range(4):
         covered_ref[x, :, here] = jnp.broadcast_to(jnp.sum(wall_mask[x], axis=0, keepdims=True), (8, 128))
+    round_second(near_early, got_early, 0)
+    settle(solid_y_halo)
+    for x in range(2):
+        for n, at in ((0, 0), (1, 6)):
+            solid_k[at + x, :, beyond] = jnp.where(lane_8 < 64, solid_high_y[n, x], solid_low_y[n, x])
+    solid_x_halo = send_solid(0, beyond) + send_solid(3, beyond)
+    settle(column_halo)
+    for tile in range(5):
+        low, high = columns_low[tile], columns_high[tile]
+        for n, (ref, q, x) in enumerate(units[21 * tile : 21 * tile + 21]):
+            ref[q, x, :, beyond] = jnp.where(lane_8 < 64, turn(high, 125 - 6 * n, 1), turn(low, 125 - 6 * n, 1))
+    named_beyond = jnp.where(lane_8 < 64, columns_high[5], columns_low[5])
+    collide_flow(flow, post_f.at[0], speeds.at[0], beyond)
+    collide_heat(heat, post_g.at[0], speeds.at[0], beyond)
+    heat_halo = send_heat(0)
+    flow_halo = send_flow(0)
+    round_second(near_late, got_late, 2)
+
     settle(quick_halo)
     rest_rows = []
     for x in range(4):
@@ -486,31 +568,10 @@
         total = total + jnp.where(covered_ref[x, 0:1, here] > 0.5, -wall_post, wall_post)
         rest_rows.append(total + post_g[0, x + 1, 6, 1:2, here])
     a2_col = at_wall(rest_rows)
-    third[:, 0, :] = slots(a2_col, 0.0)
+    slots(third, 0, a2_col, 0.0)
     fill(third, 1, as_row(a2_col))
-    to_all(third, got_third, 2, True)
-
-    settle(solid_y_halo)
-    for x in range(2):
-        for n, at in ((0, 0), (1, 6)):
-            solid_k[at + x, :, beyond] = jnp.where(lane_8 < 64, solid_high_y[n, x], solid_low_y[n, x])
-    solid_x_halo = send_solid(0, beyond) + send_solid(3, beyond)
-    settle(column_halo)
-    named_beyond = None
-    for tile in range(5):
-        low, high = columns_low[tile], columns_high[tile]
-        for n in range(21):
-            place = 21 * tile + n
-            value = jnp.where(lane_8 < 64, turn(high, 125 - 6 * n, 1), turn(low, 125 - 6 * n, 1))
-            if place < len(units):
-                ref, q, x = units[place]
-                ref[q, x, :, beyond] = value
-            else:
-                named_beyond = value
-    collide_flow(flow, post_f.at[0], speeds.at[0], beyond)
-    collide_heat(heat, post_g.at[0], speeds.at[0], beyond)
-    heat_halo = send_heat(0)
-    flow_halo = send_flow(0)
+    round_first(third, near_third, 4, True)
+
     for x in range(4):
         covered_ref[x, :, beyond] = jnp.where(jnp.broadcast_to(named_beyond[x : x + 1], (8, 128)) > 0.5, 1.0, 0.0)
     halo_lanes = (126, 127, 0, 1)
@@ -524,11 +585,16 @@
         for n in (0, 2)
     ]
     rows_col = jnp.concatenate([cell_col] + halo_cells, axis=0)
-    cell_ref[...] = jnp.broadcast_to(rows_col, (144, 128))
-    rows_cell = cell_ref[...].astype(jnp.int32)
+    cell_ref[0:144] = jnp.broadcast_to(rows_col, (144, 128))
+    rows_cell = cell_ref[0:144].astype(jnp.int32)
+    above = (sub_8 & 3) >= 2
+    halo_column = jnp.where(above, (sub_8 & 3) - 2, 126 + (sub_8 & 3))
+    cell_ref[144:152] = (
+        (j + jnp.where(above, 1, -1)) * 256 + 128 * (sub_8 >> 2) + halo_column
+    ).astype(F32)
     lane_144 = lane_of((144, 128))
     face_hit = jnp.where(lane_144 == (rows_cell & 127), 1.0, 0.0)
-    rows_place = ((j - (rows_cell >> 8) - 1) & 31) + 32 * ((rows_cell >> 7) & 1)
+    rows_place = ((rows_cell >> 8) & 31) + 32 * ((rows_cell >> 7) & 1)
     pick = jnp.where(lane_144 == rows_place, 1.0, 0.0)[:, 0:64]
 
     def put_heat(q, value):
@@ -536,20 +602,13 @@
 
     def put_flow(q, value):
         flow[q] = value
-
-    settle(heat_halo)
-    stream(post_g.at[0], HEAT_PLACES, covered_ref[...], put_heat)
-    settle(flow_halo)
-    stream(post_f.at[0], FLOW_PLACES, None, put_flow)
-    collide_flow(flow, post_f.at[1], speeds.at[1], whole)
-    flow_halo = send_flow(1)
 
     settle(solid_x_halo)
     k = [solid_k[6 + x] for x in range(2)]
     field_0 = [solid_k[x] for x in range(2)]
     p1 = conduct(field_0, 0, k, whole, gates_y)
 
-    from_all(got_early, 0)
+    got_bytes(got_early, ny - 4, 1)
 
     def slot_columns(value, field):
         return [
@@ -559,7 +618,11 @@
             for c in range(CAP)
         ]
 
-    faces = slot_columns(got_early[:, 2, :], 1)
+    def mine(ref, n):
+        return pltpu.roll(ref[:, n, :], lax.rem(128 - 16 * y, 128), 1)
+
+    first_slots = mine(got_early, 2)
+    faces = slot_columns(first_slots, 1)
 
     def own_sums(fields):
         result = []
@@ -573,18 +636,13 @@
             result.append([jnp.sum(total, axis=0, keepdims=True) for total in totals])
         return result
 
-    def halo_sums(fields):
-        cells = got_early[:, 0, :]
+    def halo_sums(cols):
         result = []
         for x in range(2):
-            rows = [jnp.zeros((1, 128), F32) for _ in fields]
-            for at in halo_lanes:
-                there = (j + (1 if at < 64 else -1)) * 256 + 128 * x + at
-                hit = cells == jnp.full((32, 128), there, jnp.int32).astype(F32)
-                for n, field in enumerate(fields):
-                    total = jnp.sum(jnp.where(hit, 1.0 if field is None else field, 0.0), axis=0, keepdims=True)
-                    total = jnp.sum(total, axis=1, keepdims=True)
-                    rows[n] = jnp.where(row_lane == at, total, rows[n])
+            rows = [jnp.zeros((1, 128), F32) for _ in cols]
+            for n, col in enumerate(cols):
+                for m, at in enumerate(halo_lanes):
+                    rows[n] = jnp.where(row_lane == at, col[144 + 4 * x + m : 145 + 4 * x + m], rows[n])
             result.append(rows)
         return result
 
@@ -597,15 +655,6 @@
 
     def on_top(value, row):
         return value + jnp.where(top_256, jnp.broadcast_to(row, (8, 256)), 0.0)
-
-    sums = joined(
-        own_sums([slot_columns(got_early[:, 2, :], 0), None]), halo_sums([got_early[:, 1, :], None])
-    )
-    many = [sums[x][1] for x in range(2)]
-    solid_1 = [on_top(p1[x], DT * (sums[x][0] - many[x] * field_0[x][7:8])) for x in range(2)]
-    for x in range(2):
-        solid_k[2 + x] = solid_1[x]
-    solid_halo = send_solid(1, whole)
 
     def same_cell(ref, n, count, many_rows):
         cells = cell_ref[0:many_rows]
@@ -620,20 +669,36 @@
         zero = jnp.zeros((many_rows, 128), F32)
         return lax.fori_loop(0, ny, body, (zero, zero) if count else (zero,))
 
-    total_1, number = same_cell(got_early, 1, True, 144)
+    total_1, number = same_cell(got_early, 1, True, 152)
     number_col = jnp.sum(number, axis=1, keepdims=True)
+    total_1_col = jnp.sum(total_1, axis=1, keepdims=True)
+    sums = joined(own_sums([slot_columns(first_slots, 0), None]), halo_sums([total_1_col, number_col]))
+    many = [sums[x][1] for x in range(2)]
+    solid_1 = [on_top(p1[x], DT * (sums[x][0] - many[x] * field_0[x][7:8])) for x in range(2)]
+    for x in range(2):
+        solid_k[2 + x] = solid_1[x]
+    solid_halo = send_solid(1, whole)
+
     edge_k = got_early[:, 3, :]
     crossing = []
     for x in range(2):
         inside = got_early[:, 4 + x, :]
         inside_k = edge_k if x == 0 else jnp.where(lane_32 == 0, turn(edge_k, 127, 1), turn(edge_k, 1, 1))
-        outside, outside_k = (turn(turn(part, 1, 0), 127, 1) for part in (inside, inside_k))
+        outside, outside_k = (turn(turn(part, 31, 0), 127, 1) for part in (inside, inside_k))
         c, cb = conduct_of(inside, inside_k), conduct_of(outside, outside_k)
         rise = 2.0 * c * cb / (c + cb) * (outside - inside)
-        rise = jnp.where((lane_32 == 127) & (sub_32 != j), rise, 0.0)
-        crossing.append(DT * (rise - turn(turn(rise, 31, 0), 1, 1)))
-
-    from_all(got_late, 1)
+        rise = jnp.where((lane_32 == 127) & (sub_32 != ny - 1), rise, 0.0)
+        crossing.append(DT * (rise - turn(turn(rise, 1, 0), 1, 1)))
+
+    settle(heat_halo)
+    stream(post_g.at[0], HEAT_PLACES, covered_ref[...], put_heat)
+    settle(flow_halo)
+    stream(post_f.at[0], FLOW_PLACES, None, put_flow)
+    collide_flow(flow, post_f.at[1], speeds.at[1], whole)
+    flow_halo = send_flow(1)
+
+    round_second(near_third, got_third, 4)
+    got_bytes(got_late, ny - 4, 3)
     surfaces = jnp.concatenate(
         [
             jnp.concatenate([got_late[:, x, :] + crossing[x] for x in range(2)], axis=0),
@@ -641,12 +706,11 @@
         ],
         axis=1,
     )
-    picked = jnp.dot(pick, surfaces, precision=lax.Precision.HIGHEST, preferred_element_type=F32)
+    picked = pick_rows(pick, surfaces)
     w1_col = jnp.sum(
-        face_hit * (picked[:, 0:128] - DT * number_col * picked[:, 128:256]) + DT * total_1,
-        axis=1,
-        keepdims=True,
-    )
+        face_hit * (picked[:, 0:128] - DT * number_col[0:144] * picked[:, 128:256]), axis=1, keepdims=True
+    )
+    w1_col = w1_col + DT * total_1_col[0:144]
 
     def warm_wall(col):
         rows = on_wall(col[0:128])
@@ -659,27 +723,41 @@
             heat[5, x, 0:1, beyond] = heat[5, x, 0:1, beyond] + 0.25 * outer
 
     warm_wall(w1_col)
-    collide_heat(heat, post_g.at[1], speeds.at[1], whole)
-    heat_halo = send_heat(1)
-
-    from_all(got_third, 2)
-    rest = joined(own_sums([slot_columns(got_third[:, 0, :], 0)]), halo_sums([got_third[:, 1, :]]))
+    heat_halo = []
+    collide_heat(heat, post_g.at[1], speeds.at[1], whole, lambda: heat_halo.extend(send_heat(1)))
+
     settle(solid_halo)
-    solid_2 = conduct(solid_1, 1, k, whole, gates_y)
-    solid_2 = [
-        on_top(solid_2[x], DT * (rest[x][0] - 0.75 * many[x] * solid_1[x][7:8])) for x in range(2)
-    ]
+    p2 = conduct(solid_1, 1, k, whole, gates_y)
+    p2 = [on_top(p2[x], (-0.75 * DT) * many[x] * solid_1[x][7:8]) for x in range(2)]
+    for x in range(2):
+        fill(mid, 2 + x, p2[x][7:8, 0:128])
+
+    settle(heat_halo)
+    post = post_g.at[1]
+    warmth = post[1:5, 0, 0:1] + post[0:4, 1, 0:1] + post[2:6, 2, 0:1]
+    warmth = warmth + turn(post[1:5, 3, 0:1], 1, 2) + turn(post[1:5, 4, 0:1], -1, 2)
+    bounce = post[1:5, 6, 0:1]
+    warmth = warmth + jnp.where(covered_ref[:, 0:1] > 0.5, -bounce, bounce) + post[1:5, 6, 1:2]
+    a3_col = at_wall([warmth[x, :, 0:128] for x in range(4)])
+    fill(mid, 0, as_row(a3_col))
+    to_owner = jnp.where(jnp.broadcast_to(owner_row, (32, 128)) == sub_32.astype(F32), 1.0, 0.0)
+    mid[:, 1, :] = pick_rows(to_owner, jnp.where(lane_f == rank_col, a3_col * live_col, 0.0))
+    to_all(mid, got_mid, 6)
+    stream(post_g.at[1], HEAT_PLACES, covered_ref[...], put_heat)
+
+    got_bytes(got_third, ny - 4, 5)
+    (total_2,) = same_cell(got_third, 1, False, 152)
+    total_2_col = jnp.sum(total_2, axis=1, keepdims=True)
+    rest = joined(own_sums([slot_columns(mine(got_third, 0), 0)]), halo_sums([total_2_col]))
+    solid_2 = [on_top(p2[x], DT * rest[x][0]) for x in range(2)]
     for x in range(2):
         solid_k[4 + x] = solid_2[x]
-        fill(mid, 2 + x, solid_2[x][7:8, 0:128])
     solid_halo = send_solid(2, whole)
 
-    settle(heat_halo)
-    stream(post_g.at[1], HEAT_PLACES, covered_ref[...], put_heat)
-    a3_col = at_wall(wall_sums())
-    fill(mid, 0, as_row(a3_col))
-    mid[:, 1, :] = slots(a3_col, 0.0)
-    to_all(mid, got_mid, 3, True)
+    settle(flow_halo)
+    stream(post_f.at[1], FLOW_PLACES, None, put_flow)
+    collide_flow(flow, post_f.at[2], speeds.at[2], whole)
+    flow_halo = send_flow(2)
 
     settle(solid_halo)
     p3 = conduct(solid_2, 2, k, whole, gates_y)
@@ -691,20 +769,15 @@
         at_cell = jnp.where(first, p3[0][7:8], jnp.where(second, p3[1][7:8], 0.0))
         answer = jnp.where(lane_32 == c, jnp.sum(at_cell, axis=1, keepdims=True), answer)
     answer_out[:, 0, :] = answer
-    to_all(answer_out, got_answer, 4, True)
-
-    settle(flow_halo)
-    stream(post_f.at[1], FLOW_PLACES, None, put_flow)
-    collide_flow(flow, post_f.at[2], speeds.at[2], whole)
-    flow_halo = send_flow(2)
-
-    from_all(got_mid, 3)
+    to_all(answer_out, got_answer, 7)
+
+    got_bytes(got_mid, ny - 1, 6)
     surfaces = jnp.concatenate([got_mid[:, 2 + x, :] for x in range(2)], axis=0)
-    picked = jnp.dot(pick, surfaces, precision=lax.Precision.HIGHEST, preferred_element_type=F32)
-    w2_col = jnp.sum(face_hit * picked, axis=1, keepdims=True)
+    picked = pick_rows(pick, surfaces)
+    w2_col = jnp.sum(face_hit * picked, axis=1, keepdims=True) + DT * total_2_col[0:144]
     warm_wall(w2_col)
-    collide_heat(heat, post_g.at[2], speeds.at[2], whole)
-    heat_halo = send_heat(2)
+    heat_halo = []
+    collide_heat(heat, post_g.at[2], speeds.at[2], whole, lambda: heat_halo.extend(send_heat(2)))
 
     (total_3,) = same_cell(got_mid, 0, False, 128)
     last = own_sums([slot_columns(got_mid[:, 1, :], 0)])
@@ -719,9 +792,9 @@
 
     stream(post_f.at[2], FLOW_PLACES, None, write_flow)
 
-    from_all(got_answer, 4)
-    pick_owner = jnp.where(lane_of((128, 32)).astype(F32) == block_col, 1.0, 0.0)
-    found = jnp.dot(pick_owner, got_answer[:, 0, :], precision=lax.Precision.HIGHEST, preferred_element_type=F32)
+    got_bytes(got_answer, ny - 1, 7)
+    pick_owner = jnp.where(lane_of((128, 32)).astype(F32) == owner_col, 1.0, 0.0)
+    found = pick_rows(pick_owner, got_answer[:, 0, :])
     w3_col = jnp.sum(jnp.where(lane_f == rank_col, found, 0.0) + DT * total_3, axis=1, keepdims=True)
     w3_rows = on_wall(w3_col)
 
@@ -736,8 +809,11 @@
 
     stream(post_g.at[2], HEAT_PLACES, covered_ref[...], write_heat)
 
-    for n, target in enumerate((got_early, got_late, got_third, got_mid, got_answer)):
-        all_sent(target, n)
+    for n, target in enumerate((got_early, got_late, got_third)):
+        sent_bytes(target, 3, 2 * n)
+        sent_bytes(target, ny - 4, 2 * n + 1)
+    sent_bytes(got_mid, ny - 1, 6)
+    sent_bytes(got_answer, ny - 1, 7)
     for made, goes in sent:
         if goes is None:
             made.wait_send()
@@ -787,20 +863,23 @@
             vmem((4,) + wide),
             vmem((2, 2) + tile),
             vmem((2, 2) + tile),
-            vmem((5,) + tile),
-            vmem((5,) + tile),
-            vmem((5,) + tile),
+            vmem((6,) + tile),
+            vmem((6,) + tile),
+            vmem((6,) + tile),
             vmem((4, 1, 128)),
             vmem((4, 1, 128)),
             vmem((4, 128, 128)),
             vmem((4,) + wide),
-            vmem((144, 128)),
+            vmem((152, 128)),
             vmem((128, 128)),
-            vmem((32, 6, 128)),
+            vmem((4, 6, 128)),
+            vmem((4, 6, 128)),
             vmem((32, 6, 128)),
             vmem((1, 2, 128)),
+            vmem((4, 2, 128)),
             vmem((32, 2, 128)),
-            vmem((32, 2, 128)),
+            vmem((4, 2, 128)),
+            vmem((4, 2, 128)),
             vmem((32, 2, 128)),
             vmem((32, 4, 128)),
             vmem((32, 4, 128)),
@@ -809,8 +888,8 @@
             pltpu.SemaphoreType.DMA((8,)),
             pltpu.SemaphoreType.DMA((copies,)),
             pltpu.SemaphoreType.DMA((copies,)),
-            pltpu.SemaphoreType.DMA((5,)),
-            pltpu.SemaphoreType.DMA((5,)),
+            pltpu.SemaphoreType.DMA((8,)),
+            pltpu.SemaphoreType.DMA((8,)),
         ],
         compiler_params=pltpu.CompilerParams(
             collective_id=0, has_side_effects=True, vmem_limit_bytes=ROOM

time: 53 us -> 47.6 us (0.90)
  Pallas kernels: 51.6 us -> 46.2 us
    pallas_call x1, Pallas kernels: 50.8 us -> 45.4 us  [on_device(): pl.pallas_call(functools.partial(kernel, nx, ny), out_shape=tuple((pltpu....]
where the time goes in v3:
time: 47.6 us; the launch traced here: 47.5 us
  Pallas kernels  46.2 us (97%)
  between operations  1.29 us (3%)
    pallas_call x1, Pallas kernels, on_device(): pl.pallas_call(functools.partial(kernel, nx, ny), out_shape=tuple((pltpu....  45.4 us

profile of v3, /device:TPU:1, one launch (start us, length us, event | category | flops | bytes accessed | tf_op | source)
XLA Modules:
  0.0 47.5 jit_solution(7452989421363465367)
XLA Ops:
  1.3 45.4 %coupled_steps.1 = (f32[19,32,128]{2,1,0:T(8,128)S(1)}, f32[7,32,128]{2,1,0:T(8,128)S(1)}, f32[16,128]{1,0:T(8,128)S(1)}) custom-call(f32[19,32,128]{2,1,0:T(8,128)} %bitcast.8, f32[7,32,128]{2,1,0:T(8,128)} %bitcast.9, f32[16,128]{1,0:T(8,128)} %bitcast.10, s32[16,128]{1,0:T(8,128)} %bitcast.11, s32[1,128]{1,0:T(1,128)} %bitcast.12, ...), custom_call_target="tpu_custom_call" | custom-call | tf_op jit(solution)/shard_map/coupled_steps/pallas_call | solution.py:842
  46.7 0.8 %write_out.1 = (f32[19,32,128]{2,1,0:T(8,128)}, f32[7,32,128]{2,1,0:T(8,128)}, f32[16,128]{1,0:T(8,128)}) custom-call(f32[19,32,128]{2,1,0:T(8,128)S(1)} %get-tuple-element.9.refs_0_, f32[7,32,128]{2,1,0:T(8,128)S(1)} %get-tuple-element.10.refs_1_, f32[16,128]{1,0:T(8,128)S(1)} %get-tuple-element.11.refs_2_), custom_call_target="tpu_custom_call" | custom-call | tf_op jit(solution)/shard_map/write_out/pallas_call | solution.py:908

commit v4 on v3

--- a/solution.py
+++ b/solution.py
@@ -372,16 +372,6 @@
 
     here, beyond, whole = pl.ds(0, 128), pl.ds(128, 128), pl.ds(0, 256)
 
-    for n in (2, 3):
-        arrivals[n].wait()
-    for x in range(2):
-        solid_k[x, :, here] = s_in[pl.ds(x, 8, stride=2), :]
-        solid_k[6 + x, :, here] = 0.2 + 0.8 * m_in[pl.ds(x, 8, stride=2), :].astype(F32)
-    solid_0 = [solid_k[x, :, here] for x in range(2)]
-    k_here = [solid_k[6 + x, :, here] for x in range(2)]
-    pl.semaphore_wait(barrier, len(greeted))
-    solid_x_halo = send_solid(0, here) + send_solid(3, here)
-
     lane_8, sub_8 = lane_of((8, 128)), sub_of((8, 128))
     arrivals[0].wait()
     for q in range(7):
@@ -398,16 +388,13 @@
             inside = (lane_8 >= 6 * n) & (lane_8 < 6 * n + 6)
             packed = jnp.where(inside, turn(ref[q, x, :, here], 6 * n + 3, 1), packed)
         columns[tile] = packed
-    column_halo = [
-        copy(columns.at[pl.ds(0, 5)], columns_low.at[pl.ds(0, 5)], (i, upper)),
-        copy(columns.at[pl.ds(0, 5)], columns_high.at[pl.ds(0, 5)], (i, lower)),
-    ]
-    both = [solid_k.at[pl.ds(0, 2), :, here], solid_k.at[pl.ds(6, 2), :, here]]
-    solid_y_halo = [
-        made
-        for n, part in enumerate(both)
-        for made in (copy(part, solid_low_y.at[n], (i, upper)), copy(part, solid_high_y.at[n], (i, lower)))
-    ]
+    for n in (2, 3):
+        arrivals[n].wait()
+    for x in range(2):
+        solid_k[x, :, here] = s_in[pl.ds(x, 8, stride=2), :]
+        solid_k[6 + x, :, here] = 0.2 + 0.8 * m_in[pl.ds(x, 8, stride=2), :].astype(F32)
+    solid_0 = [solid_k[x, :, here] for x in range(2)]
+    k_here = [solid_k[6 + x, :, here] for x in range(2)]
 
     square = (128, 128)
     lane, sub = lane_of(square), sub_of(square)
@@ -489,17 +476,12 @@
     fill(early, 3, jnp.where((row_lane == 0) | (row_lane == 127), k_top[0], k_inner))
     for x in range(2):
         fill(early, 4 + x, solid_0[x][7:8])
-    round_first(early, near_early, 0, True)
 
     named = on_wall(cell_col + 1.0)
     named_8 = jnp.zeros((8, 128), F32)
     for x in range(4):
         named_8 = jnp.where((sub_8 & 3) == x, named[x], named_8)
     columns[5] = named_8
-    column_halo += [
-        copy(columns.at[5], columns_low.at[5], (i, upper)),
-        copy(columns.at[5], columns_high.at[5], (i, lower)),
-    ]
     collide_flow(flow, post_f.at[0], speeds.at[0], here)
     collide_heat(heat, post_g.at[0], speeds.at[0], here)
     up = down = jnp.zeros((1, 128), F32)
@@ -508,11 +490,24 @@
         down = jnp.where(row_lane == x, turn(post_g[0, x + 1, 4, 0:1, here], x, 1), down)
     quick[0], quick[1] = up, down
     quick[2], quick[3] = post_g[0, 4, 1, 0:1, here], post_g[0, 1, 2, 0:1, here]
+    for x in range(4):
+        covered_ref[x, :, here] = jnp.broadcast_to(jnp.sum(wall_mask[x], axis=0, keepdims=True), (8, 128))
+
+    pl.semaphore_wait(barrier, len(greeted))
+    solid_x_halo = send_solid(0, here) + send_solid(3, here)
+    round_first(early, near_early, 0, True)
+    column_halo = [copy(columns, columns_low, (i, upper)), copy(columns, columns_high, (i, lower))]
     quick_halo = [
         copy(quick.at[0], got_quick.at[0], (i, upper)),
         copy(quick.at[1], got_quick.at[1], (i, lower)),
         copy(quick.at[2], got_quick.at[2], (right, j)),
         copy(quick.at[3], got_quick.at[3], (left, j)),
+    ]
+    both = [solid_k.at[pl.ds(0, 2), :, here], solid_k.at[pl.ds(6, 2), :, here]]
+    solid_y_halo = [
+        made
+        for n, part in enumerate(both)
+        for made in (copy(part, solid_low_y.at[n], (i, upper)), copy(part, solid_high_y.at[n], (i, lower)))
     ]
 
     gates_x = (jnp.where(i == 0, 0.0, 1.0), jnp.where(i == nx - 1, 0.0, 1.0))
@@ -536,8 +531,6 @@
         late[0, x : x + 1, :] = inner_1[x][7:8]
     round_first(late, near_late, 2, False)
 
-    for x in range(4):
-        covered_ref[x, :, here] = jnp.broadcast_to(jnp.sum(wall_mask[x], axis=0, keepdims=True), (8, 128))
     round_second(near_early, got_early, 0)
     settle(solid_y_halo)
     for x in range(2):
@@ -603,6 +596,13 @@
     def put_flow(q, value):
         flow[q] = value
 
+    settle(heat_halo)
+    stream(post_g.at[0], HEAT_PLACES, covered_ref[...], put_heat)
+    settle(flow_halo)
+    stream(post_f.at[0], FLOW_PLACES, None, put_flow)
+    collide_flow(flow, post_f.at[1], speeds.at[1], whole)
+    flow_halo = send_flow(1)
+
     settle(solid_x_halo)
     k = [solid_k[6 + x] for x in range(2)]
     field_0 = [solid_k[x] for x in range(2)]
@@ -657,17 +657,20 @@
         return value + jnp.where(top_256, jnp.broadcast_to(row, (8, 256)), 0.0)
 
     def same_cell(ref, n, count, many_rows):
-        cells = cell_ref[0:many_rows]
-
-        def body(b, carry):
-            hit = cells == got_early[b, 0:1, :]
-            total = carry[0] + jnp.where(hit, ref[b, n : n + 1, :], 0.0)
-            if count:
-                return total, carry[1] + jnp.where(hit, 1.0, 0.0)
-            return (total,)
-
-        zero = jnp.zeros((many_rows, 128), F32)
-        return lax.fori_loop(0, ny, body, (zero, zero) if count else (zero,))
+        halves = []
+        for first, last in ((0, 80), (80, many_rows)):
+            cells = cell_ref[first:last]
+
+            def body(b, carry, cells=cells):
+                hit = cells == got_early[b, 0:1, :]
+                total = carry[0] + jnp.where(hit, ref[b, n : n + 1, :], 0.0)
+                if count:
+                    return total, carry[1] + jnp.where(hit, 1.0, 0.0)
+                return (total,)
+
+            zero = jnp.zeros((last - first, 128), F32)
+            halves.append(lax.fori_loop(0, ny, body, (zero, zero) if count else (zero,), unroll=2))
+        return [jnp.concatenate(parts, axis=0) for parts in zip(*halves)]
 
     total_1, number = same_cell(got_early, 1, True, 152)
     number_col = jnp.sum(number, axis=1, keepdims=True)
@@ -689,13 +692,6 @@
         rise = 2.0 * c * cb / (c + cb) * (outside - inside)
         rise = jnp.where((lane_32 == 127) & (sub_32 != ny - 1), rise, 0.0)
         crossing.append(DT * (rise - turn(turn(rise, 1, 0), 1, 1)))
-
-    settle(heat_halo)
-    stream(post_g.at[0], HEAT_PLACES, covered_ref[...], put_heat)
-    settle(flow_halo)
-    stream(post_f.at[0], FLOW_PLACES, None, put_flow)
-    collide_flow(flow, post_f.at[1], speeds.at[1], whole)
-    flow_halo = send_flow(1)
 
     round_second(near_third, got_third, 4)
     got_bytes(got_late, ny - 4, 3)

time: 47.6 us -> 48.2 us (1.013)
  Pallas kernels: 46.2 us -> 46.8 us
    pallas_call x1, Pallas kernels: 45.4 us -> 46 us  [on_device(): pl.pallas_call(functools.partial(kernel, nx, ny), out_shape=tuple((pltpu....]
where the time goes in v4:
time: 48.2 us; the launch traced here: 48.1 us
  Pallas kernels  46.8 us (97%)
  between operations  1.29 us (3%)
    pallas_call x1, Pallas kernels, on_device(): pl.pallas_call(functools.partial(kernel, nx, ny), out_shape=tuple((pltpu....  46 us

profile of v4, /device:TPU:1, one launch (start us, length us, event | category | flops | bytes accessed | tf_op | source)
XLA Modules:
  0.0 48.1 jit_solution(5641655008852323001)
XLA Ops:
  1.3 46.0 %coupled_steps.1 = (f32[19,32,128]{2,1,0:T(8,128)S(1)}, f32[7,32,128]{2,1,0:T(8,128)S(1)}, f32[16,128]{1,0:T(8,128)S(1)}) custom-call(f32[19,32,128]{2,1,0:T(8,128)} %bitcast.8, f32[7,32,128]{2,1,0:T(8,128)} %bitcast.9, f32[16,128]{1,0:T(8,128)} %bitcast.10, s32[16,128]{1,0:T(8,128)} %bitcast.11, s32[1,128]{1,0:T(1,128)} %bitcast.12, ...), custom_call_target="tpu_custom_call" | custom-call | tf_op jit(solution)/shard_map/coupled_steps/pallas_call | solution.py:838
  47.3 0.8 %write_out.1 = (f32[19,32,128]{2,1,0:T(8,128)}, f32[7,32,128]{2,1,0:T(8,128)}, f32[16,128]{1,0:T(8,128)}) custom-call(f32[19,32,128]{2,1,0:T(8,128)S(1)} %get-tuple-element.9.refs_0_, f32[7,32,128]{2,1,0:T(8,128)S(1)} %get-tuple-element.10.refs_1_, f32[16,128]{1,0:T(8,128)S(1)} %get-tuple-element.11.refs_2_), custom_call_target="tpu_custom_call" | custom-call | tf_op jit(solution)/shard_map/write_out/pallas_call | solution.py:904

commit v5 on v4

--- a/solution.py
+++ b/solution.py
@@ -224,6 +224,8 @@
     third,
     near_third,
     got_third,
+    surface,
+    got_surface,
     mid,
     got_mid,
     answer_out,
@@ -532,6 +534,22 @@
     round_first(late, near_late, 2, False)
 
     round_second(near_early, got_early, 0)
+    settle(quick_halo)
+    rest_rows = []
+    for x in range(4):
+        post = lambda q, at=x: post_g[0, at + 1, q, 0:1, here]
+        total = post(0) + (post_g[0, x, 1, 0:1, here] if x else got_quick[2])
+        total = total + (post_g[0, x + 2, 2, 0:1, here] if x < 3 else got_quick[3])
+        total = total + jnp.where(row_lane == 0, turn(got_quick[0], 128 - x, 1), turn(post(3), 1, 1))
+        total = total + jnp.where(row_lane == 127, turn(got_quick[1], 127 - x, 1), turn(post(4), 127, 1))
+        wall_post = post(6)
+        total = total + jnp.where(covered_ref[x, 0:1, here] > 0.5, -wall_post, wall_post)
+        rest_rows.append(total + post_g[0, x + 1, 6, 1:2, here])
+    a2_col = at_wall(rest_rows)
+    slots(third, 0, a2_col, 0.0)
+    fill(third, 1, as_row(a2_col))
+    round_first(third, near_third, 4, True)
+
     settle(solid_y_halo)
     for x in range(2):
         for n, at in ((0, 0), (1, 6)):
@@ -548,22 +566,6 @@
     heat_halo = send_heat(0)
     flow_halo = send_flow(0)
     round_second(near_late, got_late, 2)
-
-    settle(quick_halo)
-    rest_rows = []
-    for x in range(4):
-        post = lambda q, at=x: post_g[0, at + 1, q, 0:1, here]
-        total = post(0) + (post_g[0, x, 1, 0:1, here] if x else got_quick[2])
-        total = total + (post_g[0, x + 2, 2, 0:1, here] if x < 3 else got_quick[3])
-        total = total + jnp.where(row_lane == 0, turn(got_quick[0], 128 - x, 1), turn(post(3), 1, 1))
-        total = total + jnp.where(row_lane == 127, turn(got_quick[1], 127 - x, 1), turn(post(4), 127, 1))
-        wall_post = post(6)
-        total = total + jnp.where(covered_ref[x, 0:1, here] > 0.5, -wall_post, wall_post)
-        rest_rows.append(total + post_g[0, x + 1, 6, 1:2, here])
-    a2_col = at_wall(rest_rows)
-    slots(third, 0, a2_col, 0.0)
-    fill(third, 1, as_row(a2_col))
-    round_first(third, near_third, 4, True)
 
     for x in range(4):
         covered_ref[x, :, beyond] = jnp.where(jnp.broadcast_to(named_beyond[x : x + 1], (8, 128)) > 0.5, 1.0, 0.0)
@@ -693,20 +695,21 @@
         rise = jnp.where((lane_32 == 127) & (sub_32 != ny - 1), rise, 0.0)
         crossing.append(DT * (rise - turn(turn(rise, 1, 0), 1, 1)))
 
-    round_second(near_third, got_third, 4)
-    got_bytes(got_late, ny - 4, 3)
-    surfaces = jnp.concatenate(
-        [
-            jnp.concatenate([got_late[:, x, :] + crossing[x] for x in range(2)], axis=0),
-            jnp.concatenate([got_early[:, 4 + x, :] for x in range(2)], axis=0),
-        ],
+    known = jnp.concatenate(
+        [jnp.concatenate(crossing, axis=0), jnp.concatenate([got_early[:, 4 + x, :] for x in range(2)], axis=0)],
         axis=1,
     )
-    picked = pick_rows(pick, surfaces)
-    w1_col = jnp.sum(
-        face_hit * (picked[:, 0:128] - DT * number_col[0:144] * picked[:, 128:256]), axis=1, keepdims=True
-    )
-    w1_col = w1_col + DT * total_1_col[0:144]
+    known = pick_rows(pick, known)
+    known = face_hit * (known[:, 0:128] - DT * number_col[0:144] * known[:, 128:256])
+    known_col = jnp.sum(known, axis=1, keepdims=True) + DT * total_1_col[0:144]
+    round_second(near_third, got_third, 4)
+
+    def surface_at_rows(ref):
+        surface = jnp.concatenate([ref[:, x, :] for x in range(2)], axis=0)
+        return jnp.sum(face_hit * pick_rows(pick, surface), axis=1, keepdims=True)
+
+    got_bytes(got_late, ny - 4, 3)
+    w1_col = known_col + surface_at_rows(got_late)
 
     def warm_wall(col):
         rows = on_wall(col[0:128])
@@ -726,7 +729,8 @@
     p2 = conduct(solid_1, 1, k, whole, gates_y)
     p2 = [on_top(p2[x], (-0.75 * DT) * many[x] * solid_1[x][7:8]) for x in range(2)]
     for x in range(2):
-        fill(mid, 2 + x, p2[x][7:8, 0:128])
+        fill(surface, x, p2[x][7:8, 0:128])
+    to_all(surface, got_surface, 8)
 
     settle(heat_halo)
     post = post_g.at[1]
@@ -767,14 +771,13 @@
     answer_out[:, 0, :] = answer
     to_all(answer_out, got_answer, 7)
 
-    got_bytes(got_mid, ny - 1, 6)
-    surfaces = jnp.concatenate([got_mid[:, 2 + x, :] for x in range(2)], axis=0)
-    picked = pick_rows(pick, surfaces)
-    w2_col = jnp.sum(face_hit * picked, axis=1, keepdims=True) + DT * total_2_col[0:144]
+    got_bytes(got_surface, ny - 1, 8)
+    w2_col = surface_at_rows(got_surface) + DT * total_2_col[0:144]
     warm_wall(w2_col)
     heat_halo = []
     collide_heat(heat, post_g.at[2], speeds.at[2], whole, lambda: heat_halo.extend(send_heat(2)))
 
+    got_bytes(got_mid, ny - 1, 6)
     (total_3,) = same_cell(got_mid, 0, False, 128)
     last = own_sums([slot_columns(got_mid[:, 1, :], 0)])
     for x in range(2):
@@ -810,6 +813,7 @@
         sent_bytes(target, ny - 4, 2 * n + 1)
     sent_bytes(got_mid, ny - 1, 6)
     sent_bytes(got_answer, ny - 1, 7)
+    sent_bytes(got_surface, ny - 1, 8)
     for made, goes in sent:
         if goes is None:
             made.wait_send()
@@ -877,15 +881,17 @@
             vmem((4, 2, 128)),
             vmem((4, 2, 128)),
             vmem((32, 2, 128)),
-            vmem((32, 4, 128)),
-            vmem((32, 4, 128)),
+            vmem((32, 2, 128)),
+            vmem((32, 2, 128)),
+            vmem((32, 2, 128)),
+            vmem((32, 2, 128)),
             vmem((32, 1, 128)),
             vmem((32, 1, 128)),
             pltpu.SemaphoreType.DMA((8,)),
             pltpu.SemaphoreType.DMA((copies,)),
             pltpu.SemaphoreType.DMA((copies,)),
-            pltpu.SemaphoreType.DMA((8,)),
-            pltpu.SemaphoreType.DMA((8,)),
+            pltpu.SemaphoreType.DMA((9,)),
+            pltpu.SemaphoreType.DMA((9,)),
         ],
         compiler_params=pltpu.CompilerParams(
             collective_id=0, has_side_effects=True, vmem_limit_bytes=ROOM

time: 48.2 us -> 47 us (0.975)
  Pallas kernels: 46.8 us -> 45.5 us
    pallas_call x1, Pallas kernels: 46 us -> 44.7 us  [on_device(): pl.pallas_call(functools.partial(kernel, nx, ny), out_shape=tuple((pltpu....]
where the time goes in v5:
time: 47 us; the launch traced here: 46.8 us
  Pallas kernels  45.5 us (97%)
  between operations  1.29 us (3%)
    pallas_call x1, Pallas kernels, on_device(): pl.pallas_call(functools.partial(kernel, nx, ny), out_shape=tuple((pltpu....  44.7 us

profile of v5, /device:TPU:1, one launch (start us, length us, event | category | flops | bytes accessed | tf_op | source)
XLA Modules:
  0.0 46.8 jit_solution(5685985538640329264)
XLA Ops:
  1.3 44.7 %coupled_steps.1 = (f32[19,32,128]{2,1,0:T(8,128)S(1)}, f32[7,32,128]{2,1,0:T(8,128)S(1)}, f32[16,128]{1,0:T(8,128)S(1)}) custom-call(f32[19,32,128]{2,1,0:T(8,128)} %bitcast.8, f32[7,32,128]{2,1,0:T(8,128)} %bitcast.9, f32[16,128]{1,0:T(8,128)} %bitcast.10, s32[16,128]{1,0:T(8,128)} %bitcast.11, s32[1,128]{1,0:T(1,128)} %bitcast.12, ...), custom_call_target="tpu_custom_call" | custom-call | tf_op jit(solution)/shard_map/coupled_steps/pallas_call | solution.py:842
  46.0 0.8 %write_out.1 = (f32[19,32,128]{2,1,0:T(8,128)}, f32[7,32,128]{2,1,0:T(8,128)}, f32[16,128]{1,0:T(8,128)}) custom-call(f32[19,32,128]{2,1,0:T(8,128)S(1)} %get-tuple-element.9.refs_0_, f32[7,32,128]{2,1,0:T(8,128)S(1)} %get-tuple-element.10.refs_1_, f32[16,128]{1,0:T(8,128)S(1)} %get-tuple-element.11.refs_2_), custom_call_target="tpu_custom_call" | custom-call | tf_op jit(solution)/shard_map/write_out/pallas_call | solution.py:910

commit v6 on v5

--- a/solution.py
+++ b/solution.py
@@ -236,6 +236,23 @@
     g_send,
     g_recv,
 ):
+    i, j = lax.axis_index("gx"), lax.axis_index("gy")
+    right, left = lax.rem(i + 1, nx), lax.rem(i + nx - 1, nx)
+    upper, lower = lax.rem(j + 1, ny), lax.rem(j + ny - 1, ny)
+    along = ny // 4
+    y = lax.rem(j // 2, along)
+    corner = j // (2 * along) * 2 + lax.rem(j, 2)
+
+    def seat(corner_there, y_there):
+        return corner_there // 2 * (2 * along) + 2 * y_there + lax.rem(corner_there, 2)
+
+    barrier = pltpu.get_barrier_semaphore()
+    greeted = [(i, seat(lax.rem(corner + d, 4), y)) for d in (2, 3, 1)]
+    greeted += [(i, seat(corner, lax.rem(y + d, along))) for d in (4, 3, 5, 2, 6, 1, 7)]
+    greeted += [(right, j), (left, j), (i, upper), (i, lower)]
+    for device in greeted:
+        pl.semaphore_signal(barrier, inc=1, device_id=device, device_id_type=MESH)
+
     arrivals = []
     for n, (source, target) in enumerate(
         (
@@ -253,23 +270,6 @@
         made.start()
         arrivals.append(made)
 
-    i, j = lax.axis_index("gx"), lax.axis_index("gy")
-    right, left = lax.rem(i + 1, nx), lax.rem(i + nx - 1, nx)
-    upper, lower = lax.rem(j + 1, ny), lax.rem(j + ny - 1, ny)
-    along = ny // 4
-    y = lax.rem(j // 2, along)
-    corner = j // (2 * along) * 2 + lax.rem(j, 2)
-
-    def seat(corner_there, y_there):
-        return corner_there // 2 * (2 * along) + 2 * y_there + lax.rem(corner_there, 2)
-
-    barrier = pltpu.get_barrier_semaphore()
-    greeted = [(i, seat(lax.rem(corner + d, 4), y)) for d in (2, 3, 1)]
-    greeted += [(i, seat(corner, lax.rem(y + d, along))) for d in (4, 3, 5, 2, 6, 1, 7)]
-    greeted += [(right, j), (left, j), (i, upper), (i, lower)]
-    for device in greeted:
-        pl.semaphore_signal(barrier, inc=1, device_id=device, device_id_type=MESH)
-
     sent = []
 
     def copy(source, target, device, goes=None, comes=None):
@@ -325,29 +325,36 @@
             there = lax.rem(corner + d, 4)
             pltpu.make_async_remote_copy(
                 src_ref=source.at[there] if personal else source.at[0],
-                dst_ref=near.at[corner],
+                dst_ref=near.at[corner // 2, lax.rem(corner, 2)],
                 send_sem=g_send.at[pair],
                 recv_sem=g_recv.at[pair],
                 device_id=(i, seat(there, y)),
                 device_id_type=MESH,
             ).start()
-        near[corner] = source[corner] if personal else source[0]
+        near[corner // 2, lax.rem(corner, 2)] = source[corner] if personal else source[0]
 
     def round_second(near, target, pair):
-        got_bytes(target, 3, pair)
+        few = target.at[0, pl.ds(0, 3)]
+        pltpu.make_async_copy(few, few, g_recv.at[pair]).wait()
         for d in (4, 3, 5, 2, 6, 1, 7):
-            for half in range(2):
-                pltpu.make_async_remote_copy(
-                    src_ref=near.at[pl.ds(2 * half, 2)],
-                    dst_ref=target.at[pl.ds(2 * along * half + 2 * y, 2)],
-                    send_sem=g_send.at[pair + 1],
-                    recv_sem=g_recv.at[pair + 1],
-                    device_id=(i, seat(corner, lax.rem(y + d, along))),
-                    device_id_type=MESH,
-                ).start()
+            pltpu.make_async_remote_copy(
+                src_ref=near,
+                dst_ref=target.at[:, pl.ds(2 * y, 2)],
+                send_sem=g_send.at[pair + 1],
+                recv_sem=g_recv.at[pair + 1],
+                device_id=(i, seat(corner, lax.rem(y + d, along))),
+                device_id_type=MESH,
+            ).start()
         for half in range(2):
             for c in range(2):
-                target[2 * along * half + 2 * y + c] = near[2 * half + c]
+                target[half, 2 * y + c] = near[half, c]
+
+    def second_wait(target, sems):
+        most = target.at[:, pl.ds(0, ny // 2 - 2)]
+        pltpu.make_async_copy(most, most, sems).wait()
+
+    def rows_of(ref, n):
+        return jnp.concatenate([ref[half, :, n, :] for half in range(2)], axis=0)
 
     def to_all(source, target, pair):
         @pl.loop(0, ny - 1)
@@ -610,7 +617,7 @@
     field_0 = [solid_k[x] for x in range(2)]
     p1 = conduct(field_0, 0, k, whole, gates_y)
 
-    got_bytes(got_early, ny - 4, 1)
+    second_wait(got_early, g_recv.at[1])
 
     def slot_columns(value, field):
         return [
@@ -621,7 +628,7 @@
         ]
 
     def mine(ref, n):
-        return pltpu.roll(ref[:, n, :], lax.rem(128 - 16 * y, 128), 1)
+        return pltpu.roll(rows_of(ref, n), lax.rem(128 - 16 * y, 128), 1)
 
     first_slots = mine(got_early, 2)
     faces = slot_columns(first_slots, 1)
@@ -658,14 +665,14 @@
     def on_top(value, row):
         return value + jnp.where(top_256, jnp.broadcast_to(row, (8, 256)), 0.0)
 
-    def same_cell(ref, n, count, many_rows):
+    def same_cell(value_of, count, many_rows):
         halves = []
         for first, last in ((0, 80), (80, many_rows)):
             cells = cell_ref[first:last]
 
             def body(b, carry, cells=cells):
-                hit = cells == got_early[b, 0:1, :]
-                total = carry[0] + jnp.where(hit, ref[b, n : n + 1, :], 0.0)
+                hit = cells == got_early[b // 16, lax.rem(b, 16), 0:1, :]
+                total = carry[0] + jnp.where(hit, value_of(b), 0.0)
                 if count:
                     return total, carry[1] + jnp.where(hit, 1.0, 0.0)
                 return (total,)
@@ -674,7 +681,7 @@
             halves.append(lax.fori_loop(0, ny, body, (zero, zero) if count else (zero,), unroll=2))
         return [jnp.concatenate(parts, axis=0) for parts in zip(*halves)]
 
-    total_1, number = same_cell(got_early, 1, True, 152)
+    total_1, number = same_cell(lambda b: got_early[b // 16, lax.rem(b, 16), 1:2, :], True, 152)
     number_col = jnp.sum(number, axis=1, keepdims=True)
     total_1_col = jnp.sum(total_1, axis=1, keepdims=True)
     sums = joined(own_sums([slot_columns(first_slots, 0), None]), halo_sums([total_1_col, number_col]))
@@ -684,10 +691,10 @@
         solid_k[2 + x] = solid_1[x]
     solid_halo = send_solid(1, whole)
 
-    edge_k = got_early[:, 3, :]
+    edge_k = rows_of(got_early, 3)
     crossing = []
     for x in range(2):
-        inside = got_early[:, 4 + x, :]
+        inside = rows_of(got_early, 4 + x)
         inside_k = edge_k if x == 0 else jnp.where(lane_32 == 0, turn(edge_k, 127, 1), turn(edge_k, 1, 1))
         outside, outside_k = (turn(turn(part, 31, 0), 127, 1) for part in (inside, inside_k))
         c, cb = conduct_of(inside, inside_k), conduct_of(outside, outside_k)
@@ -696,7 +703,7 @@
         crossing.append(DT * (rise - turn(turn(rise, 1, 0), 1, 1)))
 
     known = jnp.concatenate(
-        [jnp.concatenate(crossing, axis=0), jnp.concatenate([got_early[:, 4 + x, :] for x in range(2)], axis=0)],
+        [jnp.concatenate(crossing, axis=0), jnp.concatenate([rows_of(got_early, 4 + x) for x in range(2)], axis=0)],
         axis=1,
     )
     known = pick_rows(pick, known)
@@ -704,12 +711,11 @@
     known_col = jnp.sum(known, axis=1, keepdims=True) + DT * total_1_col[0:144]
     round_second(near_third, got_third, 4)
 
-    def surface_at_rows(ref):
-        surface = jnp.concatenate([ref[:, x, :] for x in range(2)], axis=0)
-        return jnp.sum(face_hit * pick_rows(pick, surface), axis=1, keepdims=True)
-
-    got_bytes(got_late, ny - 4, 3)
-    w1_col = known_col + surface_at_rows(got_late)
+    def surface_at_rows(rows):
+        return jnp.sum(face_hit * pick_rows(pick, jnp.concatenate(rows, axis=0)), axis=1, keepdims=True)
+
+    second_wait(got_late, g_recv.at[3])
+    w1_col = known_col + surface_at_rows([rows_of(got_late, x) for x in range(2)])
 
     def warm_wall(col):
         rows = on_wall(col[0:128])
@@ -740,13 +746,13 @@
     warmth = warmth + jnp.where(covered_ref[:, 0:1] > 0.5, -bounce, bounce) + post[1:5, 6, 1:2]
     a3_col = at_wall([warmth[x, :, 0:128] for x in range(4)])
     fill(mid, 0, as_row(a3_col))
+    to_all(mid, got_mid, 6)
     to_owner = jnp.where(jnp.broadcast_to(owner_row, (32, 128)) == sub_32.astype(F32), 1.0, 0.0)
-    mid[:, 1, :] = pick_rows(to_owner, jnp.where(lane_f == rank_col, a3_col * live_col, 0.0))
-    to_all(mid, got_mid, 6)
+    answer_out[:, 1, :] = pick_rows(to_owner, jnp.where(lane_f == rank_col, a3_col * live_col, 0.0))
     stream(post_g.at[1], HEAT_PLACES, covered_ref[...], put_heat)
 
-    got_bytes(got_third, ny - 4, 5)
-    (total_2,) = same_cell(got_third, 1, False, 152)
+    second_wait(got_third, g_recv.at[5])
+    (total_2,) = same_cell(lambda b: got_third[b // 16, lax.rem(b, 16), 1:2, :], False, 152)
     total_2_col = jnp.sum(total_2, axis=1, keepdims=True)
     rest = joined(own_sums([slot_columns(mine(got_third, 0), 0)]), halo_sums([total_2_col]))
     solid_2 = [on_top(p2[x], DT * rest[x][0]) for x in range(2)]
@@ -772,17 +778,11 @@
     to_all(answer_out, got_answer, 7)
 
     got_bytes(got_surface, ny - 1, 8)
-    w2_col = surface_at_rows(got_surface) + DT * total_2_col[0:144]
+    w2_col = surface_at_rows([got_surface[:, x, :] for x in range(2)]) + DT * total_2_col[0:144]
     warm_wall(w2_col)
     heat_halo = []
     collide_heat(heat, post_g.at[2], speeds.at[2], whole, lambda: heat_halo.extend(send_heat(2)))
 
-    got_bytes(got_mid, ny - 1, 6)
-    (total_3,) = same_cell(got_mid, 0, False, 128)
-    last = own_sums([slot_columns(got_mid[:, 1, :], 0)])
-    for x in range(2):
-        s_out[pl.ds(x, 8, stride=2), :] = p3[x] + jnp.where(sub_8 == 7, DT * last[x][0], 0.0)
-
     settle(flow_halo)
 
     def write_flow(q, value):
@@ -791,11 +791,17 @@
 
     stream(post_f.at[2], FLOW_PLACES, None, write_flow)
 
+    got_bytes(got_mid, ny - 1, 6)
+    (total_3,) = same_cell(lambda b: got_mid[b], False, 128)
     got_bytes(got_answer, ny - 1, 7)
     pick_owner = jnp.where(lane_of((128, 32)).astype(F32) == owner_col, 1.0, 0.0)
     found = pick_rows(pick_owner, got_answer[:, 0, :])
     w3_col = jnp.sum(jnp.where(lane_f == rank_col, found, 0.0) + DT * total_3, axis=1, keepdims=True)
     w3_rows = on_wall(w3_col)
+    last = own_sums([slot_columns(got_answer[:, 1, :], 0)])
+    for x in range(2):
+        s_out[pl.ds(x, 8, stride=2), :] = p3[x] + jnp.where(sub_8 == 7, DT * last[x][0], 0.0)
+
 
     settle(heat_halo)
 
@@ -809,8 +815,9 @@
     stream(post_g.at[2], HEAT_PLACES, covered_ref[...], write_heat)
 
     for n, target in enumerate((got_early, got_late, got_third)):
-        sent_bytes(target, 3, 2 * n)
-        sent_bytes(target, ny - 4, 2 * n + 1)
+        few = target.at[0, pl.ds(0, 3)]
+        pltpu.make_async_copy(few, few, g_send.at[2 * n]).wait()
+        second_wait(target, g_send.at[2 * n + 1])
     sent_bytes(got_mid, ny - 1, 6)
     sent_bytes(got_answer, ny - 1, 7)
     sent_bytes(got_surface, ny - 1, 8)
@@ -873,20 +880,20 @@
             vmem((152, 128)),
             vmem((128, 128)),
             vmem((4, 6, 128)),
-            vmem((4, 6, 128)),
-            vmem((32, 6, 128)),
+            vmem((2, 2, 6, 128)),
+            vmem((2, 16, 6, 128)),
             vmem((1, 2, 128)),
+            vmem((2, 2, 2, 128)),
+            vmem((2, 16, 2, 128)),
             vmem((4, 2, 128)),
-            vmem((32, 2, 128)),
-            vmem((4, 2, 128)),
-            vmem((4, 2, 128)),
-            vmem((32, 2, 128)),
-            vmem((32, 2, 128)),
-            vmem((32, 2, 128)),
+            vmem((2, 2, 2, 128)),
+            vmem((2, 16, 2, 128)),
             vmem((32, 2, 128)),
             vmem((32, 2, 128)),
             vmem((32, 1, 128)),
             vmem((32, 1, 128)),
+            vmem((32, 2, 128)),
+            vmem((32, 2, 128)),
             pltpu.SemaphoreType.DMA((8,)),
             pltpu.SemaphoreType.DMA((copies,)),
             pltpu.SemaphoreType.DMA((copies,)),

time: 47 us -> 47.7 us (1.015)
  Pallas kernels: 45.5 us -> 46.3 us
    pallas_call x1, Pallas kernels: 44.7 us -> 45.5 us  [on_device(): pl.pallas_call(functools.partial(kernel, nx, ny), out_shape=tuple((pltpu....]
where the time goes in v6:
time: 47.7 us; the launch traced here: 47.5 us
  Pallas kernels  46.3 us (97%)
  between operations  1.29 us (3%)
    pallas_call x1, Pallas kernels, on_device(): pl.pallas_call(functools.partial(kernel, nx, ny), out_shape=tuple((pltpu....  45.5 us

profile of v6, /device:TPU:1, one launch (start us, length us, event | category | flops | bytes accessed | tf_op | source)
XLA Modules:
  0.0 47.5 jit_solution(10361475009378765364)
XLA Ops:
  1.3 45.5 %coupled_steps.1 = (f32[19,32,128]{2,1,0:T(8,128)S(1)}, f32[7,32,128]{2,1,0:T(8,128)S(1)}, f32[16,128]{1,0:T(8,128)S(1)}) custom-call(f32[19,32,128]{2,1,0:T(8,128)} %bitcast.8, f32[7,32,128]{2,1,0:T(8,128)} %bitcast.9, f32[16,128]{1,0:T(8,128)} %bitcast.10, s32[16,128]{1,0:T(8,128)} %bitcast.11, s32[1,128]{1,0:T(1,128)} %bitcast.12, ...), custom_call_target="tpu_custom_call" | custom-call | tf_op jit(solution)/shard_map/coupled_steps/pallas_call | solution.py:849
  46.8 0.8 %write_out.1 = (f32[19,32,128]{2,1,0:T(8,128)}, f32[7,32,128]{2,1,0:T(8,128)}, f32[16,128]{1,0:T(8,128)}) custom-call(f32[19,32,128]{2,1,0:T(8,128)S(1)} %get-tuple-element.9.refs_0_, f32[7,32,128]{2,1,0:T(8,128)S(1)} %get-tuple-element.10.refs_1_, f32[16,128]{1,0:T(8,128)S(1)} %get-tuple-element.11.refs_2_), custom_call_target="tpu_custom_call" | custom-call | tf_op jit(solution)/shard_map/write_out/pallas_call | solution.py:917

commit v7 on v6

--- a/solution.py
+++ b/solution.py
@@ -214,7 +214,6 @@
     wall_mask,
     covered_ref,
     cell_ref,
-    slot_key,
     early,
     near_early,
     got_early,
@@ -320,18 +319,18 @@
             to_left(solid_k.at[2 * r, :, lanes], solid_high_x.at[r, :, lanes]),
         ]
 
-    def round_first(source, near, pair, personal):
+    def round_first(source, near, pair):
         for d in (2, 3, 1):
             there = lax.rem(corner + d, 4)
             pltpu.make_async_remote_copy(
-                src_ref=source.at[there] if personal else source.at[0],
+                src_ref=source.at[0],
                 dst_ref=near.at[corner // 2, lax.rem(corner, 2)],
                 send_sem=g_send.at[pair],
                 recv_sem=g_recv.at[pair],
                 device_id=(i, seat(there, y)),
                 device_id_type=MESH,
             ).start()
-        near[corner // 2, lax.rem(corner, 2)] = source[corner] if personal else source[0]
+        near[corner // 2, lax.rem(corner, 2)] = source[0]
 
     def round_second(near, target, pair):
         few = target.at[0, pl.ds(0, 3)]
@@ -386,17 +385,6 @@
     for q in range(7):
         for x in range(4):
             heat[q, x, :, here] = g_in[q, pl.ds(x, 8, stride=4), :]
-    arrivals[1].wait()
-    for q in range(19):
-        for x in range(4):
-            flow[q, x, :, here] = f_in[q, pl.ds(x, 8, stride=4), :]
-    units = [(flow, q, x) for q in range(19) for x in range(4)] + [(heat, q, x) for q in range(7) for x in range(4)]
-    for tile in range(5):
-        packed = jnp.zeros((8, 128), F32)
-        for n, (ref, q, x) in enumerate(units[21 * tile : 21 * tile + 21]):
-            inside = (lane_8 >= 6 * n) & (lane_8 < 6 * n + 6)
-            packed = jnp.where(inside, turn(ref[q, x, :, here], 6 * n + 3, 1), packed)
-        columns[tile] = packed
     for n in (2, 3):
         arrivals[n].wait()
     for x in range(2):
@@ -420,10 +408,8 @@
     face_index = face_in[...]
     wall = wall_in[...]
     live = lane_of((1, 128)) < jnp.broadcast_to(tally_in[...], (1, 128))
-    owner_y = (owner >> 1) & (along - 1)
-    owner_corner = ((owner >> 1) // along) * 2 + (owner & 1)
     cell_row = jnp.where(live, owner * 256 + face_index, -1).astype(F32)
-    small = [owner, owner_y, face_index >> 7, face_index & 127, wall >> 7, wall & 127]
+    small = [owner, face_index >> 7, face_index & 127, wall >> 7, wall & 127]
     rows_8 = jnp.zeros((8, 128), F32)
     for n, row in enumerate([value.astype(F32) for value in small] + [jnp.where(live, 1.0, 0.0)]):
         rows_8 = jnp.where(sub_8 == n, row, rows_8)
@@ -433,8 +419,8 @@
         (((1,), (1,)), ((), ())),
         preferred_element_type=F32,
     )
-    owner_col, owner_y_col, face_x_col, face_y_col, wall_x_col, wall_y_col, live_col = (
-        jnp.sum(jnp.where(lane_of((128, 8)) == n, turned, 0.0), axis=1, keepdims=True) for n in range(7)
+    owner_col, face_x_col, face_y_col, wall_x_col, wall_y_col, live_col = (
+        jnp.sum(jnp.where(lane_of((128, 8)) == n, turned, 0.0), axis=1, keepdims=True) for n in range(6)
     )
     owner_row = owner.astype(F32)
     face_col = 128.0 * face_x_col + face_y_col
@@ -448,13 +434,6 @@
     wall_hit = jnp.where(lane_f == wall_y_col, live_col, 0.0)
     for x in range(4):
         wall_mask[x] = jnp.where(wall_x_col == float(x), wall_hit, 0.0)
-    slot_key[...] = jnp.where(
-        ((lane >> 4).astype(F32) == owner_y_col) & ((lane & 7).astype(F32) == rank_col),
-        jnp.broadcast_to(live_col, square),
-        0.0,
-    )
-    to_corner = jnp.where(jnp.broadcast_to(owner_corner, (8, 128)) == sub_8, 1.0, 0.0)
-
     def at_wall(rows):
         total = wall_mask[0] * rows[0]
         for x in range(1, 4):
@@ -463,12 +442,6 @@
 
     def on_wall(col):
         return [jnp.sum(wall_mask[x] * col, axis=0, keepdims=True) for x in range(4)]
-
-    def slots(buffer, n, first, second):
-        fields = jnp.where((lane & 8) == 0, first, second)
-        value = pick_rows(to_corner, fields * slot_key[...])
-        for there in range(4):
-            buffer[there, n : n + 1, :] = value[there : there + 1]
 
     def fill(buffer, n, value):
         buffer[:, n, :] = jnp.broadcast_to(value, (buffer.shape[0], 128))
@@ -479,18 +452,40 @@
     t1_col = at_wall([warmth[x] for x in range(4)])
     fill(early, 0, cell_row)
     fill(early, 1, as_row(t1_col))
-    slots(early, 2, t1_col, face_col + 1.0)
     k_top = [k_here[x][7:8] for x in range(2)]
     k_inner = jnp.where(row_lane == 1, turn(k_top[1], 1, 1), turn(k_top[1], 127, 1))
-    fill(early, 3, jnp.where((row_lane == 0) | (row_lane == 127), k_top[0], k_inner))
+    fill(early, 2, jnp.where((row_lane == 0) | (row_lane == 127), k_top[0], k_inner))
     for x in range(2):
-        fill(early, 4 + x, solid_0[x][7:8])
+        fill(early, 3 + x, solid_0[x][7:8])
 
     named = on_wall(cell_col + 1.0)
     named_8 = jnp.zeros((8, 128), F32)
     for x in range(4):
         named_8 = jnp.where((sub_8 & 3) == x, named[x], named_8)
     columns[5] = named_8
+    pl.semaphore_wait(barrier, len(greeted))
+    solid_x_halo = send_solid(0, here) + send_solid(3, here)
+    round_first(early, near_early, 0)
+
+    arrivals[1].wait()
+    for q in range(19):
+        for x in range(4):
+            flow[q, x, :, here] = f_in[q, pl.ds(x, 8, stride=4), :]
+    units = [(flow, q, x) for q in range(19) for x in range(4)] + [(heat, q, x) for q in range(7) for x in range(4)]
+    for tile in range(5):
+        packed = jnp.zeros((8, 128), F32)
+        for n, (ref, q, x) in enumerate(units[21 * tile : 21 * tile + 21]):
+            inside = (lane_8 >= 6 * n) & (lane_8 < 6 * n + 6)
+            packed = jnp.where(inside, turn(ref[q, x, :, here], 6 * n + 3, 1), packed)
+        columns[tile] = packed
+    column_halo = [copy(columns, columns_low, (i, upper)), copy(columns, columns_high, (i, lower))]
+    both = [solid_k.at[pl.ds(0, 2), :, here], solid_k.at[pl.ds(6, 2), :, here]]
+    solid_y_halo = [
+        made
+        for n, part in enumerate(both)
+        for made in (copy(part, solid_low_y.at[n], (i, upper)), copy(part, solid_high_y.at[n], (i, lower)))
+    ]
+
     collide_flow(flow, post_f.at[0], speeds.at[0], here)
     collide_heat(heat, post_g.at[0], speeds.at[0], here)
     up = down = jnp.zeros((1, 128), F32)
@@ -502,21 +497,11 @@
     for x in range(4):
         covered_ref[x, :, here] = jnp.broadcast_to(jnp.sum(wall_mask[x], axis=0, keepdims=True), (8, 128))
 
-    pl.semaphore_wait(barrier, len(greeted))
-    solid_x_halo = send_solid(0, here) + send_solid(3, here)
-    round_first(early, near_early, 0, True)
-    column_halo = [copy(columns, columns_low, (i, upper)), copy(columns, columns_high, (i, lower))]
     quick_halo = [
         copy(quick.at[0], got_quick.at[0], (i, upper)),
         copy(quick.at[1], got_quick.at[1], (i, lower)),
         copy(quick.at[2], got_quick.at[2], (right, j)),
         copy(quick.at[3], got_quick.at[3], (left, j)),
-    ]
-    both = [solid_k.at[pl.ds(0, 2), :, here], solid_k.at[pl.ds(6, 2), :, here]]
-    solid_y_halo = [
-        made
-        for n, part in enumerate(both)
-        for made in (copy(part, solid_low_y.at[n], (i, upper)), copy(part, solid_high_y.at[n], (i, lower)))
     ]
 
     gates_x = (jnp.where(i == 0, 0.0, 1.0), jnp.where(i == nx - 1, 0.0, 1.0))
@@ -538,7 +523,7 @@
     inner_1 = conduct(solid_0, 0, k_here, here, (0.0, 0.0))
     for x in range(2):
         late[0, x : x + 1, :] = inner_1[x][7:8]
-    round_first(late, near_late, 2, False)
+    round_first(late, near_late, 2)
 
     round_second(near_early, got_early, 0)
     settle(quick_halo)
@@ -553,9 +538,8 @@
         total = total + jnp.where(covered_ref[x, 0:1, here] > 0.5, -wall_post, wall_post)
         rest_rows.append(total + post_g[0, x + 1, 6, 1:2, here])
     a2_col = at_wall(rest_rows)
-    slots(third, 0, a2_col, 0.0)
-    fill(third, 1, as_row(a2_col))
-    round_first(third, near_third, 4, True)
+    fill(third, 0, as_row(a2_col))
+    round_first(third, near_third, 4)
 
     settle(solid_y_halo)
     for x in range(2):
@@ -619,19 +603,24 @@
 
     second_wait(got_early, g_recv.at[1])
 
-    def slot_columns(value, field):
+    cells = rows_of(got_early, 0).astype(jnp.int32)
+    named_here = (cells >> 8) == j
+    earlier = jnp.dot(
+        jnp.where(named_here, 1.0, 0.0).astype(jnp.bfloat16),
+        jnp.where(sub < lane, 1.0, 0.0).astype(jnp.bfloat16),
+        preferred_element_type=F32,
+    )
+    slot = jnp.where(named_here, earlier, -1.0)
+
+    def slot_columns(value):
         return [
             jnp.broadcast_to(
-                jnp.sum(jnp.where(lane_32 == 8 * field + c, value, 0.0), axis=1, keepdims=True), (32, 128)
+                jnp.sum(jnp.where(slot == float(c), value, 0.0), axis=1, keepdims=True), (32, 128)
             )
             for c in range(CAP)
         ]
 
-    def mine(ref, n):
-        return pltpu.roll(rows_of(ref, n), lax.rem(128 - 16 * y, 128), 1)
-
-    first_slots = mine(got_early, 2)
-    faces = slot_columns(first_slots, 1)
+    faces = slot_columns(((cells & 255) + 1).astype(F32))
 
     def own_sums(fields):
         result = []
@@ -684,17 +673,17 @@
     total_1, number = same_cell(lambda b: got_early[b // 16, lax.rem(b, 16), 1:2, :], True, 152)
     number_col = jnp.sum(number, axis=1, keepdims=True)
     total_1_col = jnp.sum(total_1, axis=1, keepdims=True)
-    sums = joined(own_sums([slot_columns(first_slots, 0), None]), halo_sums([total_1_col, number_col]))
+    sums = joined(own_sums([slot_columns(rows_of(got_early, 1)), None]), halo_sums([total_1_col, number_col]))
     many = [sums[x][1] for x in range(2)]
     solid_1 = [on_top(p1[x], DT * (sums[x][0] - many[x] * field_0[x][7:8])) for x in range(2)]
     for x in range(2):
         solid_k[2 + x] = solid_1[x]
     solid_halo = send_solid(1, whole)
 
-    edge_k = rows_of(got_early, 3)
+    edge_k = rows_of(got_early, 2)
     crossing = []
     for x in range(2):
-        inside = rows_of(got_early, 4 + x)
+        inside = rows_of(got_early, 3 + x)
         inside_k = edge_k if x == 0 else jnp.where(lane_32 == 0, turn(edge_k, 127, 1), turn(edge_k, 1, 1))
         outside, outside_k = (turn(turn(part, 31, 0), 127, 1) for part in (inside, inside_k))
         c, cb = conduct_of(inside, inside_k), conduct_of(outside, outside_k)
@@ -703,7 +692,7 @@
         crossing.append(DT * (rise - turn(turn(rise, 1, 0), 1, 1)))
 
     known = jnp.concatenate(
-        [jnp.concatenate(crossing, axis=0), jnp.concatenate([rows_of(got_early, 4 + x) for x in range(2)], axis=0)],
+        [jnp.concatenate(crossing, axis=0), jnp.concatenate([rows_of(got_early, 3 + x) for x in range(2)], axis=0)],
         axis=1,
     )
     known = pick_rows(pick, known)
@@ -747,14 +736,12 @@
     a3_col = at_wall([warmth[x, :, 0:128] for x in range(4)])
     fill(mid, 0, as_row(a3_col))
     to_all(mid, got_mid, 6)
-    to_owner = jnp.where(jnp.broadcast_to(owner_row, (32, 128)) == sub_32.astype(F32), 1.0, 0.0)
-    answer_out[:, 1, :] = pick_rows(to_owner, jnp.where(lane_f == rank_col, a3_col * live_col, 0.0))
     stream(post_g.at[1], HEAT_PLACES, covered_ref[...], put_heat)
 
     second_wait(got_third, g_recv.at[5])
-    (total_2,) = same_cell(lambda b: got_third[b // 16, lax.rem(b, 16), 1:2, :], False, 152)
+    (total_2,) = same_cell(lambda b: got_third[b // 16, lax.rem(b, 16)], False, 152)
     total_2_col = jnp.sum(total_2, axis=1, keepdims=True)
-    rest = joined(own_sums([slot_columns(mine(got_third, 0), 0)]), halo_sums([total_2_col]))
+    rest = joined(own_sums([slot_columns(rows_of(got_third, 0))]), halo_sums([total_2_col]))
     solid_2 = [on_top(p2[x], DT * rest[x][0]) for x in range(2)]
     for x in range(2):
         solid_k[4 + x] = solid_2[x]
@@ -798,7 +785,7 @@
     found = pick_rows(pick_owner, got_answer[:, 0, :])
     w3_col = jnp.sum(jnp.where(lane_f == rank_col, found, 0.0) + DT * total_3, axis=1, keepdims=True)
     w3_rows = on_wall(w3_col)
-    last = own_sums([slot_columns(got_answer[:, 1, :], 0)])
+    last = own_sums([slot_columns(got_mid[:, 0, :])])
     for x in range(2):
         s_out[pl.ds(x, 8, stride=2), :] = p3[x] + jnp.where(sub_8 == 7, DT * last[x][0], 0.0)
 
@@ -878,22 +865,21 @@
             vmem((4, 128, 128)),
             vmem((4,) + wide),
             vmem((152, 128)),
-            vmem((128, 128)),
-            vmem((4, 6, 128)),
-            vmem((2, 2, 6, 128)),
-            vmem((2, 16, 6, 128)),
+            vmem((1, 5, 128)),
+            vmem((2, 2, 5, 128)),
+            vmem((2, 16, 5, 128)),
             vmem((1, 2, 128)),
             vmem((2, 2, 2, 128)),
             vmem((2, 16, 2, 128)),
-            vmem((4, 2, 128)),
-            vmem((2, 2, 2, 128)),
-            vmem((2, 16, 2, 128)),
+            vmem((1, 1, 128)),
+            vmem((2, 2, 1, 128)),
+            vmem((2, 16, 1, 128)),
             vmem((32, 2, 128)),
             vmem((32, 2, 128)),
             vmem((32, 1, 128)),
             vmem((32, 1, 128)),
-            vmem((32, 2, 128)),
-            vmem((32, 2, 128)),
+            vmem((32, 1, 128)),
+            vmem((32, 1, 128)),
             pltpu.SemaphoreType.DMA((8,)),
             pltpu.SemaphoreType.DMA((copies,)),
             pltpu.SemaphoreType.DMA((copies,)),

time: 47.7 us -> 47.6 us (level)
  no operation moved by 1% of the time
where the time goes in v7:
time: 47.6 us; the launch traced here: 47.4 us
  Pallas kernels  46.2 us (97%)
  between operations  1.29 us (3%)
    pallas_call x1, Pallas kernels, on_device(): pl.pallas_call(functools.partial(kernel, nx, ny), out_shape=tuple((pltpu....  45.4 us

profile of v7, /device:TPU:1, one launch (start us, length us, event | category | flops | bytes accessed | tf_op | source)
XLA Modules:
  0.0 47.4 jit_solution(983569220266668838)
XLA Ops:
  1.3 45.4 %coupled_steps.1 = (f32[19,32,128]{2,1,0:T(8,128)S(1)}, f32[7,32,128]{2,1,0:T(8,128)S(1)}, f32[16,128]{1,0:T(8,128)S(1)}) custom-call(f32[19,32,128]{2,1,0:T(8,128)} %bitcast.8, f32[7,32,128]{2,1,0:T(8,128)} %bitcast.9, f32[16,128]{1,0:T(8,128)} %bitcast.10, s32[16,128]{1,0:T(8,128)} %bitcast.11, s32[1,128]{1,0:T(1,128)} %bitcast.12, ...), custom_call_target="tpu_custom_call" | custom-call | tf_op jit(solution)/shard_map/coupled_steps/pallas_call | solution.py:836
  46.7 0.8 %write_out.1 = (f32[19,32,128]{2,1,0:T(8,128)}, f32[7,32,128]{2,1,0:T(8,128)}, f32[16,128]{1,0:T(8,128)}) custom-call(f32[19,32,128]{2,1,0:T(8,128)S(1)} %get-tuple-element.9.refs_0_, f32[7,32,128]{2,1,0:T(8,128)S(1)} %get-tuple-element.10.refs_1_, f32[16,128]{1,0:T(8,128)S(1)} %get-tuple-element.11.refs_2_), custom_call_target="tpu_custom_call" | custom-call | tf_op jit(solution)/shard_map/write_out/pallas_call | solution.py:903

commit v8 on v7

--- a/solution.py
+++ b/solution.py
@@ -640,7 +640,7 @@
             rows = [jnp.zeros((1, 128), F32) for _ in cols]
             for n, col in enumerate(cols):
                 for m, at in enumerate(halo_lanes):
-                    rows[n] = jnp.where(row_lane == at, col[144 + 4 * x + m : 145 + 4 * x + m], rows[n])
+                    rows[n] = jnp.where(row_lane == at, col[4 * x + m : 4 * x + m + 1], rows[n])
             result.append(rows)
         return result
 
@@ -654,9 +654,9 @@
     def on_top(value, row):
         return value + jnp.where(top_256, jnp.broadcast_to(row, (8, 256)), 0.0)
 
-    def same_cell(value_of, count, many_rows):
+    def same_cell(value_of, count, spans):
         halves = []
-        for first, last in ((0, 80), (80, many_rows)):
+        for first, last in spans:
             cells = cell_ref[first:last]
 
             def body(b, carry, cells=cells):
@@ -670,10 +670,10 @@
             halves.append(lax.fori_loop(0, ny, body, (zero, zero) if count else (zero,), unroll=2))
         return [jnp.concatenate(parts, axis=0) for parts in zip(*halves)]
 
-    total_1, number = same_cell(lambda b: got_early[b // 16, lax.rem(b, 16), 1:2, :], True, 152)
+    total_1, number = same_cell(lambda b: got_early[b // 16, lax.rem(b, 16), 1:2, :], True, ((0, 80), (80, 152)))
     number_col = jnp.sum(number, axis=1, keepdims=True)
     total_1_col = jnp.sum(total_1, axis=1, keepdims=True)
-    sums = joined(own_sums([slot_columns(rows_of(got_early, 1)), None]), halo_sums([total_1_col, number_col]))
+    sums = joined(own_sums([slot_columns(rows_of(got_early, 1)), None]), halo_sums([total_1_col[144:152], number_col[144:152]]))
     many = [sums[x][1] for x in range(2)]
     solid_1 = [on_top(p1[x], DT * (sums[x][0] - many[x] * field_0[x][7:8])) for x in range(2)]
     for x in range(2):
@@ -739,13 +739,15 @@
     stream(post_g.at[1], HEAT_PLACES, covered_ref[...], put_heat)
 
     second_wait(got_third, g_recv.at[5])
-    (total_2,) = same_cell(lambda b: got_third[b // 16, lax.rem(b, 16)], False, 152)
-    total_2_col = jnp.sum(total_2, axis=1, keepdims=True)
-    rest = joined(own_sums([slot_columns(rows_of(got_third, 0))]), halo_sums([total_2_col]))
+    rest_of = lambda b: got_third[b // 16, lax.rem(b, 16)]
+    (beyond_2,) = same_cell(rest_of, False, ((144, 152),))
+    rest = joined(own_sums([slot_columns(rows_of(got_third, 0))]), halo_sums([jnp.sum(beyond_2, axis=1, keepdims=True)]))
     solid_2 = [on_top(p2[x], DT * rest[x][0]) for x in range(2)]
     for x in range(2):
         solid_k[4 + x] = solid_2[x]
     solid_halo = send_solid(2, whole)
+    (total_2,) = same_cell(rest_of, False, ((0, 80), (80, 144)))
+    total_2_col = jnp.sum(total_2, axis=1, keepdims=True)
 
     settle(flow_halo)
     stream(post_f.at[1], FLOW_PLACES, None, put_flow)
@@ -765,7 +767,7 @@
     to_all(answer_out, got_answer, 7)
 
     got_bytes(got_surface, ny - 1, 8)
-    w2_col = surface_at_rows([got_surface[:, x, :] for x in range(2)]) + DT * total_2_col[0:144]
+    w2_col = surface_at_rows([got_surface[:, x, :] for x in range(2)]) + DT * total_2_col
     warm_wall(w2_col)
     heat_halo = []
     collide_heat(heat, post_g.at[2], speeds.at[2], whole, lambda: heat_halo.extend(send_heat(2)))
@@ -779,7 +781,7 @@
     stream(post_f.at[2], FLOW_PLACES, None, write_flow)
 
     got_bytes(got_mid, ny - 1, 6)
-    (total_3,) = same_cell(lambda b: got_mid[b], False, 128)
+    (total_3,) = same_cell(lambda b: got_mid[b], False, ((0, 64), (64, 128)))
     got_bytes(got_answer, ny - 1, 7)
     pick_owner = jnp.where(lane_of((128, 32)).astype(F32) == owner_col, 1.0, 0.0)
     found = pick_rows(pick_owner, got_answer[:, 0, :])

time: 47.6 us -> 47.2 us (level)
  Pallas kernels: 46.2 us -> 45.7 us
where the time goes in v8:
time: 47.2 us; the launch traced here: 47 us
  Pallas kernels  45.7 us (97%)
  between operations  1.29 us (3%)
    pallas_call x1, Pallas kernels, on_device(): pl.pallas_call(functools.partial(kernel, nx, ny), out_shape=tuple((pltpu....  44.9 us

profile of v8, /device:TPU:1, one launch (start us, length us, event | category | flops | bytes accessed | tf_op | source)
XLA Modules:
  0.0 47.0 jit_solution(1542503822499564605)
XLA Ops:
  1.3 44.9 %coupled_steps.1 = (f32[19,32,128]{2,1,0:T(8,128)S(1)}, f32[7,32,128]{2,1,0:T(8,128)S(1)}, f32[16,128]{1,0:T(8,128)S(1)}) custom-call(f32[19,32,128]{2,1,0:T(8,128)} %bitcast.8, f32[7,32,128]{2,1,0:T(8,128)} %bitcast.9, f32[16,128]{1,0:T(8,128)} %bitcast.10, s32[16,128]{1,0:T(8,128)} %bitcast.11, s32[1,128]{1,0:T(1,128)} %bitcast.12, ...), custom_call_target="tpu_custom_call" | custom-call | tf_op jit(solution)/shard_map/coupled_steps/pallas_call | solution.py:838
  46.2 0.8 %write_out.1 = (f32[19,32,128]{2,1,0:T(8,128)}, f32[7,32,128]{2,1,0:T(8,128)}, f32[16,128]{1,0:T(8,128)}) custom-call(f32[19,32,128]{2,1,0:T(8,128)S(1)} %get-tuple-element.9.refs_0_, f32[7,32,128]{2,1,0:T(8,128)S(1)} %get-tuple-element.10.refs_1_, f32[16,128]{1,0:T(8,128)S(1)} %get-tuple-element.11.refs_2_), custom_call_target="tpu_custom_call" | custom-call | tf_op jit(solution)/shard_map/write_out/pallas_call | solution.py:905
